TPU v7x, 128 devices: a whole 4x4x4 slice. The times are simulated.
128 devices in a mesh: gx: 8 (over z, x_hi), gy: 8 (over y, x_lo), sa: 2 (over core).
Axes of the slice: x: 4 (x_hi: 2, x_lo: 2; x = x_hi * 2 + x_lo), y: 4, z: 4, core: 2. Of those that a mesh axis runs over, the one named last changes fastest.
Arguments:
- mass_concentration: float32 [8, 2048, 2048], P('sa', 'gx', 'gy'), may hold values from 0.5 to 2
- thermal_reading: float32 [8, 2048, 2048], P('sa', 'gx', 'gy'), may hold values from 0.5 to 4
- eastward_transport_ratio: float32 [8, 2048, 2048], P('sa', 'gx', 'gy'), may hold values from 0.1 to 0.9
- northward_transport_ratio: float32 [8, 2048, 2048], P('sa', 'gx', 'gy'), may hold values from 0.1 to 0.9
- partition_processor: int32 [8, 8], P('gx'), may hold values from 0 to 1, as said below
Outputs:
- advected: float32 [2, 8, 2048, 2048], P(None, 'sa', 'gx', 'gy')
- gradients: float32 [96, 2, 3, 8, 32, 2048], P(('gx', 'sa'), None, None, None, None, 'gy')
- wedge: float32 [96, 8, 32, 2048], P(('gx', 'sa'), None, None, 'gy')
Inputs may be any that keep to these rules, and one draw needn't show every extreme that they name: `partition_processor`: in every row of 8 entries at most 6 are 0 and at most 6 are 1.
All inputs are finite; a program needn't handle non-finite values.
Results may differ from a plain program's by a relative error of at most 0.0003.
Values sent between devices are 32-bit elements; how exact they have to be, the bound alone decides.
No kernel may reach another device: no remote copies, remote signals or barrier semaphores. Data moves between devices by JAX's collectives and lax.ppermute only.
A program may use at most 128 MiB of HBM per device.

v0:
```python
import jax
import jax.numpy as jnp
from jax import lax
from jax.experimental import pallas as pl
from jax.experimental.pallas import tpu as pltpu
from jax.sharding import PartitionSpec as P

CAP = 6
NP = 8
RIM = 8
LANES = 128
F32 = jnp.float32
MIB = 1024 * 1024


def ring(count, step):
    return [(i, (i + step) % count) for i in range(count)]


def coefficients(c):
    d = 1.0 - c
    m = c * d
    k_right = m * d
    k_left = m * c
    return k_right, k_left, c - k_right + k_left


def face_value(qm1, q0, q1, q2):
    return (7.0 / 12.0) * (q0 + q1) - (1.0 / 12.0) * (qm1 + q2)


def sweep_rows(load_q, load_c, store, a_scr, f_scr, base, count, chunk, fields=2):
    done = 0
    while done < count:
        n = min(chunk, count - done)
        r = base + done
        k_right, k_left, k_mid = coefficients(load_c(r, n))
        for f in range(fields):
            q0 = load_q(f, r, n)
            a = face_value(load_q(f, r - 1, n), q0, load_q(f, r + 1, n), load_q(f, r + 2, n))
            a_scr[f, pl.ds(8 + done, n), :] = a
            flux = k_right * a - k_left * a_scr[f, pl.ds(7 + done, n), :] + k_mid * q0
            f_scr[f, pl.ds(8 + done, n), :] = flux
            store(f, r, n, q0 - (flux - f_scr[f, pl.ds(7 + done, n), :]))
        done += n


def lane_iota(rows):
    return lax.broadcasted_iota(jnp.int32, (rows, LANES), 1)


def half(h, start=0):
    return slice(start + h * LANES, start + (h + 1) * LANES)


def call(
    kernel, out_shape, operands, name, spaces=None, scratch=(), aliases=None, cost=None, mib=20
):
    vmem = pl.BlockSpec(memory_space=pltpu.VMEM)
    return pl.pallas_call(
        kernel,
        in_specs=[pl.BlockSpec(memory_space=x) for x in spaces] if spaces else [vmem] * len(operands),
        out_specs=jax.tree.map(lambda _: vmem, out_shape),
        out_shape=out_shape,
        scratch_shapes=list(scratch),
        input_output_aliases=aliases or {},
        compiler_params=pltpu.CompilerParams(vmem_limit_bytes=mib * MIB),
        cost_estimate=cost,
        name=name,
    )(*operands)


def out(*shape):
    return jax.ShapeDtypeStruct(shape, F32)


SWEEP_COST = pl.CostEstimate(flops=20_000_000, bytes_accessed=6_000_000, transcendentals=0)


def edge_rows_kernel(d, t, cx, cy, lo, hi, sems):
    rows = d.shape[1]
    copies = []
    for f, ref in enumerate((d, t, cx, cy)):
        copies.append(pltpu.make_async_copy(ref.at[:, 0:RIM, :], lo.at[f], sems.at[f]))
        copies.append(
            pltpu.make_async_copy(ref.at[:, rows - RIM : rows, :], hi.at[f], sems.at[4 + f])
        )
    for c in copies:
        c.start()
    for c in copies:
        c.wait()


def edge_rows(fields):
    planes, _, cols = fields[0].shape
    shape = out(4, planes, RIM, cols)
    return call(
        edge_rows_kernel,
        (shape, shape),
        fields,
        "edge_rows",
        spaces=[pl.ANY] * 4,
        scratch=[pltpu.SemaphoreType.DMA((8,))],
        mib=60,
    )


def x_inner_kernel(d, t, cx, cy, xs, cy_t, win, a_scr, f_scr):
    planes, rows, _ = d.shape

    def body(p, _):
        for h in range(2):
            for f, ref in enumerate((d, t, cx)):
                win[f, 0:rows, :] = ref[p, :, half(h)]

            def store(f, r, n, value):
                xs[p, f, h, pl.ds(RIM + r, n), :] = value

            sweep_rows(
                lambda f, r, n: win[f, pl.ds(r, n), :],
                lambda r, n: win[2, pl.ds(r, n), :],
                store,
                a_scr,
                f_scr,
                6,
                rows - 8,
                32,
            )
            for x in range(2):
                cy_t[p, x, half(h, RIM), :] = cy[p, half(x), half(h)].T
        return 0

    lax.fori_loop(0, planes, body, 0, unroll=False)


def x_inner(d, t, cx, cy):
    planes, rows, cols = d.shape
    ext = rows + 2 * RIM
    return call(
        x_inner_kernel,
        (out(planes, 2, 2, ext, LANES), out(planes, 2, ext, LANES)),
        (d, t, cx, cy),
        "x_inner",
        scratch=[pltpu.VMEM((3, ext, LANES), F32)] + [pltpu.VMEM((2, ext, LANES), F32)] * 2,
        cost=SWEEP_COST,
    )


def edge_sweep(own, rim, high, win, a_scr, f_scr, res):
    lead, rim_at = (0, 16) if high else (8, 0)
    for f in range(3):
        win[f, lead : lead + 16, :] = own(f)
        win[f, rim_at : rim_at + 8, :] = rim(f)

    def store(f, r, n, value):
        res[f, pl.ds(r, n), :] = value

    sweep_rows(
        lambda f, r, n: win[f, pl.ds(r, n), :],
        lambda r, n: win[2, pl.ds(r, n), :],
        store,
        a_scr,
        f_scr,
        6 if high else 4,
        16,
        16,
    )


EDGE_SCRATCH = [
    pltpu.VMEM((3, 32, LANES), F32),
    pltpu.VMEM((2, 32, LANES), F32),
    pltpu.VMEM((2, 32, LANES), F32),
    pltpu.VMEM((2, 32, LANES), F32),
]


def x_edge_kernel(
    d, t, cx, left, right, xs_in, cy_t, xs, x_t, h_t, to_l, to_r, rim_rows, win, a_scr, f_scr, res
):
    planes, rows, _ = d.shape
    ext = rows + 2 * RIM

    for p in range(planes):
        for h in range(2):
            for high in range(2):
                rim = right if high else left
                at = slice(rows - 16, rows) if high else slice(0, 16)
                edge_sweep(
                    lambda f: (d, t, cx)[f][p, at, half(h)],
                    lambda f: rim[f, p, :, half(h)],
                    high,
                    win,
                    a_scr,
                    f_scr,
                    res,
                )
                for f in range(2):
                    k = (f * 4 + p) * 4 + 2 * high
                    if high:
                        xs[p, f, h, rows : rows + RIM, :] = res[f, 8:16, :]
                        rim_rows[h, k : k + 2, :] = res[f, 16:18, :]
                        rim_rows[h, 32 + k : 34 + k, :] = rim[3, p, 0:2, half(h)]
                    else:
                        xs[p, f, h, RIM : 2 * RIM, :] = res[f, 8:16, :]
                        rim_rows[h, k : k + 2, :] = res[f, 6:8, :]
                        rim_rows[h, 32 + k : 34 + k, :] = rim[3, p, 6:8, half(h)]
    for h in range(2):
        h_t[half(h, RIM), :] = rim_rows[h].T
    for p in range(planes):
        for f in range(2):
            for x in range(2):
                for h in range(2):
                    x_t[p, f, x, half(h, RIM), :] = xs[p, f, h, half(x, RIM), :].T
    for buf, at in ((to_l, slice(RIM, 2 * RIM)), (to_r, slice(rows, rows + RIM))):
        for p in range(planes):
            for x in range(2):
                for f in range(2):
                    buf[(p * 2 + f) * 2 + x] = x_t[p, f, x, at, :]
                buf[16 + p * 2 + x] = cy_t[p, x, at, :]
        buf[24] = h_t[at, :]


def x_edge(d, t, cx, left, right, xs, cy_t):
    ext = xs.shape[3]
    return call(
        x_edge_kernel,
        (out(*xs.shape), out(*xs.shape), out(ext, LANES), out(25, RIM, LANES), out(25, RIM, LANES)),
        (d, t, cx, left, right, xs, cy_t),
        "x_edge",
        scratch=[pltpu.VMEM((2, LANES, LANES), F32)] + EDGE_SCRATCH,
        aliases={5: 0},
    )[1:]


def rim_courant(x):
    return pltpu.roll(x, LANES - 32, 1)


def y_inner_kernel(x_t, cy_t, h_t, s_t, sh_t, a_scr, f_scr):
    planes = x_t.shape[0]
    rows = x_t.shape[3] - 2 * RIM

    def run(load_q, load_c, store):
        sweep_rows(load_q, load_c, store, a_scr, f_scr, RIM + 6, rows - 8, 32)

    def body(p, _):
        for x in range(2):

            def store(f, r, n, value):
                s_t[p, f, x, pl.ds(r, n), :] = value

            run(
                lambda f, r, n: x_t[p, f, x, pl.ds(r, n), :],
                lambda r, n: cy_t[p, x, pl.ds(r, n), :],
                store,
            )
        return 0

    lax.fori_loop(0, planes, body, 0, unroll=False)

    def store_rim(f, r, n, value):
        sh_t[pl.ds(r, n), :] = value

    sweep_rows(
        lambda f, r, n: h_t[pl.ds(r, n), :],
        lambda r, n: rim_courant(h_t[pl.ds(r, n), :]),
        store_rim,
        a_scr,
        f_scr,
        RIM + 6,
        rows - 8,
        32,
        fields=1,
    )


def y_inner(x_t, cy_t, h_t):
    ext = x_t.shape[3]
    return call(
        y_inner_kernel,
        (out(*x_t.shape), out(*h_t.shape)),
        (x_t, cy_t, h_t),
        "y_inner",
        scratch=[pltpu.VMEM((2, ext, LANES), F32)] * 2,
        cost=SWEEP_COST,
    )


def y_edge_kernel(
    x_t, cy_t, h_t, from_l, from_r, st_in, sh_in, s_t, sh_t, s, adv, rim_rows, win, a_scr, f_scr, res
):
    planes = x_t.shape[0]
    ext = x_t.shape[3]
    rows = ext - 2 * RIM

    for high in range(2):
        rim = from_r if high else from_l
        at = slice(ext - 24, ext - 8) if high else slice(8, 24)
        to = slice(ext - 16, ext) if high else slice(0, 16)
        got = slice(8, 24) if high else slice(0, 16)
        for p in range(planes):
            for x in range(2):
                edge_sweep(
                    lambda f: cy_t[p, x, at, :] if f == 2 else x_t[p, f, x, at, :],
                    lambda f: rim[16 + p * 2 + x] if f == 2 else rim[(p * 2 + f) * 2 + x],
                    high,
                    win,
                    a_scr,
                    f_scr,
                    res,
                )
                for f in range(2):
                    s_t[p, f, x, to, :] = res[f, got, :]
                    k = (f * 4 + p) * 8
                    if high:
                        rim_rows[x, k : k + 2, :] = res[f, 16:18, :]
                    else:
                        k = (k + LANES - 2) % LANES
                        rim_rows[x, k : k + 2, :] = res[f, 6:8, :]
        edge_sweep(
            lambda f: rim_courant(h_t[at, :]) if f == 2 else h_t[at, :],
            lambda f: rim_courant(rim[24]) if f == 2 else rim[24],
            high,
            win,
            a_scr,
            f_scr,
            res,
        )
        sh_t[to, :] = res[0, got, :]
    for x in range(2):
        s[16, half(x, RIM), :] = rim_rows[x].T
    for h in range(2):
        beyond = sh_t[half(h, RIM), :].T
        for p in range(planes):
            for f in range(2):
                k = (f * 4 + p) * 4
                i = (p * 2 + f) * 2 + h
                s[i, RIM - 2 : RIM, :] = beyond[k : k + 2, :]
                s[i, RIM + rows : RIM + rows + 2, :] = beyond[k + 2 : k + 4, :]
                for x in range(2):
                    block = s_t[p, f, x, half(h, RIM), :].T
                    s[i, half(x, RIM), :] = block
                    adv[f, p, half(x), half(h)] = block


def y_edge(x_t, cy_t, h_t, from_l, from_r, s_t, sh_t):
    planes, _, _, ext, _ = x_t.shape
    rows = ext - 2 * RIM
    res = call(
        y_edge_kernel,
        (
            out(*s_t.shape),
            out(*sh_t.shape),
            out(17, ext, LANES),
            out(2, planes, rows, 2 * LANES),
        ),
        (x_t, cy_t, h_t, from_l, from_r, s_t, sh_t),
        "y_edge",
        scratch=[pltpu.VMEM((2, LANES, LANES), F32)] + EDGE_SCRATCH,
        aliases={5: 0, 6: 1},
    )
    return res[0], res[2], res[3]


def slope(w1, w2):
    return (2.0 / 3.0) * w1 - (1.0 / 12.0) * w2


def rows_slope(ref, r, n):
    return slope(
        ref[pl.ds(r + 1, n), :] - ref[pl.ds(r - 1, n), :],
        ref[pl.ds(r + 2, n), :] - ref[pl.ds(r - 2, n), :],
    )


def own_slopes_kernel(s, s_t, gx, gy):
    planes, _, _, ext, _ = s_t.shape
    rows = ext - 2 * RIM

    def body(p, _):
        for f in range(2):
            for h in range(2):
                ref = s.at[(p * 2 + f) * 2 + h]
                for r in range(0, rows, 64):
                    gx[p, f, h, r : r + 64, :] = rows_slope(ref, RIM + r, 64)
                for x in range(2):
                    ref_t = s_t.at[p, f, x]
                    gy[p, f, h, half(x), :] = rows_slope(ref_t, RIM + h * LANES, LANES).T
        return 0

    lax.fori_loop(0, planes, body, 0, unroll=False)


def own_slopes(s, s_t):
    planes, _, _, ext, _ = s_t.shape
    shape = out(planes, 2, 2, ext - 2 * RIM, LANES)
    return call(own_slopes_kernel, (shape, shape), (s, s_t), "own_slopes", cost=SWEEP_COST)


def gradient_kernel(owner, core, own, other, own_x, own_y, grad, wedge):
    slot = pl.program_id(0)
    s = core[0]
    rank = jnp.int32(0)
    piece = jnp.int32(0)
    for j in range(NP):
        mine = owner[0, j] == s
        piece = jnp.where(jnp.logical_and(mine, rank == slot), j, piece)
        rank = rank + mine.astype(jnp.int32)
    used = slot < rank
    width = grad.shape[4]

    @pl.when(jnp.logical_not(used))
    def _():
        grad[...] = jnp.zeros_like(grad)
        wedge[...] = jnp.zeros_like(wedge)

    @pl.when(used)
    def _():
        n = 8
        lane = lane_iota(n)
        first = pl.multiple_of(piece * width, 8)

        def body(i, _):
            at = pl.multiple_of(first + i * n, n)
            r = pl.multiple_of(RIM + at, n)
            to = pl.ds(pl.multiple_of(i * n, n), n)
            rim = other[16, pl.ds(r, n), :]
            for h in range(2):

                def plane(z, f, row, hh=h):
                    ref = own if z < 4 else other
                    return ref[((z % 4) * 2 + f) * 2 + hh, pl.ds(row, n), :]

                q = [[plane(z, f, r) for f in range(2)] for z in range(8)]
                for z in range(8):
                    zo = lax.rem(z + 4 * s, 8)
                    g = []
                    for f in range(2):
                        if z < 4:
                            x_slope = own_x[z, f, h, pl.ds(at, n), :]
                            y_slope = own_y[z, f, h, pl.ds(at, n), :]
                        else:
                            here = q[z][f]
                            there = plane(z, f, r, 1 - h)
                            beyond = pltpu.roll(rim, (LANES - (f * 4 + z % 4) * 8) % LANES, 1)
                            after = beyond if h else there
                            before = there if h else beyond

                            def step(k):
                                up = pltpu.roll(jnp.where(lane < k, after, here), LANES - k, 1)
                                down = pltpu.roll(
                                    jnp.where(lane >= LANES - k, before, here), k, 1
                                )
                                return up - down

                            x_slope = slope(
                                plane(z, f, r + 1) - plane(z, f, r - 1),
                                plane(z, f, r + 2) - plane(z, f, r - 2),
                            )
                            y_slope = slope(step(1), step(2))
                        z_slope = slope(
                            q[(z + 1) % 8][f] - q[(z + 7) % 8][f],
                            q[(z + 2) % 8][f] - q[(z + 6) % 8][f],
                        )
                        g.append((x_slope, y_slope, z_slope))
                        for k in range(3):
                            grad[0, f, k, zo, to, half(h)] = g[-1][k]
                    rx, ry, rz = g[0]
                    tx, ty, tz = g[1]
                    a = ry * tz - rz * ty
                    b = rz * tx - rx * tz
                    c = rx * ty - ry * tx
                    wedge[0, zo, to, half(h)] = a * a + b * b + c * c
            return 0

        lax.fori_loop(0, width // n, body, 0, unroll=False)


def gradients_of(owner, core, own, other, own_x, own_y):
    rows = own.shape[1] - 2 * RIM
    width = rows // NP
    cols = 2 * LANES
    vmem = pl.BlockSpec(memory_space=pltpu.VMEM)
    return pl.pallas_call(
        gradient_kernel,
        grid_spec=pltpu.PrefetchScalarGridSpec(
            num_scalar_prefetch=2,
            grid=(CAP,),
            in_specs=[vmem] * 4,
            out_specs=(
                pl.BlockSpec((1, 2, 3, 8, width, cols), lambda k, o, c: (k, 0, 0, 0, 0, 0)),
                pl.BlockSpec((1, 8, width, cols), lambda k, o, c: (k, 0, 0, 0)),
            ),
        ),
        out_shape=(
            jax.ShapeDtypeStruct((CAP, 2, 3, 8, width, cols), F32),
            jax.ShapeDtypeStruct((CAP, 8, width, cols), F32),
        ),
        compiler_params=pltpu.CompilerParams(vmem_limit_bytes=20 * MIB),
        name="gradient",
    )(owner, core, own, other, own_x, own_y)


def per_device(density, heat, cx, cy, owner):
    nx, ny = lax.axis_size("gx"), lax.axis_size("gy")
    lo, hi = edge_rows((density, heat, cx, cy))
    left = lax.ppermute(hi, "gx", ring(nx, 1))
    right = lax.ppermute(lo, "gx", ring(nx, -1))
    xs, cy_t = x_inner(density, heat, cx, cy)
    x_t, h_t, to_l, to_r = x_edge(density, heat, cx, left, right, xs, cy_t)
    from_l = lax.ppermute(to_r, "gy", ring(ny, 1))
    from_r = lax.ppermute(to_l, "gy", ring(ny, -1))
    s_t, sh_t = y_inner(x_t, cy_t, h_t)
    s_t, swept, advected = y_edge(x_t, cy_t, h_t, from_l, from_r, s_t, sh_t)
    other = lax.ppermute(swept, "sa", ring(2, 1))
    own_x, own_y = own_slopes(swept, s_t)
    core = lax.axis_index("sa").astype(jnp.int32).reshape(1)
    gradients, wedge = gradients_of(owner, core, swept, other, own_x, own_y)
    return advected, gradients, wedge


def solution(mesh):
    block = P("sa", "gx", "gy")
    return jax.shard_map(
        per_device,
        mesh=mesh,
        in_specs=(block, block, block, block, P("gx", None)),
        out_specs=(
            P(None, "sa", "gx", "gy"),
            P(("gx", "sa"), None, None, None, None, "gy"),
            P(("gx", "sa"), None, None, "gy"),
        ),
        check_vma=False,
    )
```

profile of v0, /device:TPU:1, one launch (start us, length us, event | category | flops | bytes accessed | tf_op | source)
XLA Modules:
  0.0 40.6 jit_solution(17087678285790464463)
XLA Ops:
  0.6 0.0 copy-start.2
  0.6 0.0 copy-start.1
  0.7 0.0 copy-start
  0.7 1.8 %edge_rows.1 = (f32[4,4,8,256]{3,2,1,0:T(8,128)}, f32[4,4,8,256]{3,2,1,0:T(8,128)}) custom-call(f32[4,256,256]{2,1,0:T(8,128)} %d.5, f32[4,256,256]{2,1,0:T(8,128)} %t.5, f32[4,256,256]{2,1,0:T(8,128)} %cx.5, f32[4,256,256]{2,1,0:T(8,128)} %cy.3), custom_call_target="tpu_custom_call" | custom-call | tf_op jit(solution)/shard_map/edge_rows/pallas_call | solution.py:60
  2.5 3.6 %collective-permute-start = (f32[4,4,8,256]{3,2,1,0:T(8,128)}, f32[4,4,8,256]{3,2,1,0:T(8,128)S(1)}, u32[]{:S(2)}, u32[]{:S(2)}) collective-permute-start(f32[4,4,8,256]{3,2,1,0:T(8,128)} %get-tuple-element.20), channel_id=1, source_target_pairs={{0,16},{16,32},{32,48},{48,64},{64,80},{80,96},{96,112},{112,0},{1... | collective-permute-start | bytes 393224 | tf_op jit(solution)/shard_map/ppermute | solution.py:508
  6.1 3.6 %collective-permute-start.1 = (f32[4,4,8,256]{3,2,1,0:T(8,128)}, f32[4,4,8,256]{3,2,1,0:T(8,128)S(1)}, u32[]{:S(2)}, u32[]{:S(2)}) collective-permute-start(f32[4,4,8,256]{3,2,1,0:T(8,128)} %get-tuple-element.21), channel_id=1, source_target_pairs={{0,112},{16,0},{32,16},{48,32},{64,48},{80,64},{96,80},{112,96},{1... | collective-permute-start | bytes 393224 | tf_op jit(solution)/shard_map/ppermute | solution.py:509
  9.7 0.0 copy-done.2
  9.7 0.0 copy-done.1
  9.7 0.0 copy-done
  9.7 0.0 copy-start.5
  9.7 1.2 %copy-done.5 = f32[4,256,256]{2,1,0:T(8,128)S(1)} copy-done((f32[4,256,256]{2,1,0:T(8,128)S(1)}, f32[4,256,256]{2,1,0:T(8,128)}, u32[]{:S(2)}) %copy-start.5) | copy-done | bytes 1048600
  10.9 1.7 %x_inner.1 = (f32[4,2,2,272,128]{4,3,2,1,0:T(8,128)S(1)}, f32[4,2,272,128]{3,2,1,0:T(8,128)S(1)}) custom-call(f32[4,256,256]{2,1,0:T(8,128)S(1)} %copy-done, f32[4,256,256]{2,1,0:T(8,128)S(1)} %copy-done.1, f32[4,256,256]{2,1,0:T(8,128)S(1)} %copy-done.2, f32[4,256,256]{2,1,0:T(8,128)S(1)} %copy-done.5), custom_call_target="tpu_custom_call" | custom-call | flops 20000000 | bytes 6000000 | tf_op jit(solution)/shard_map/x_inner/pallas_call | solution.py:60
  12.6 0.5 %collective-permute-done.left = f32[4,4,8,256]{3,2,1,0:T(8,128)S(1)} collective-permute-done((f32[4,4,8,256]{3,2,1,0:T(8,128)}, f32[4,4,8,256]{3,2,1,0:T(8,128)S(1)}, u32[]{:S(2)}, u32[]{:S(2)}) %collective-permute-start) | collective-permute-done | bytes 131104 | tf_op jit(solution)/shard_map/ppermute | solution.py:508
  13.0 0.6 %collective-permute-done.1.right = f32[4,4,8,256]{3,2,1,0:T(8,128)S(1)} collective-permute-done((f32[4,4,8,256]{3,2,1,0:T(8,128)}, f32[4,4,8,256]{3,2,1,0:T(8,128)S(1)}, u32[]{:S(2)}, u32[]{:S(2)}) %collective-permute-start.1) | collective-permute-done | bytes 131104 | tf_op jit(solution)/shard_map/ppermute | solution.py:509
  13.6 0.9 %x_edge.1 = (f32[4,2,2,272,128]{4,3,2,1,0:T(8,128)S(1)}, f32[4,2,2,272,128]{4,3,2,1,0:T(8,128)S(1)}, f32[272,128]{1,0:T(8,128)S(1)}, f32[25,8,128]{2,1,0:T(8,128)S(1)}, f32[25,8,128]{2,1,0:T(8,128)S(1)}) custom-call(f32[4,256,256]{2,1,0:T(8,128)S(1)} %copy-done, f32[4,256,256]{2,1,0:T(8,128)S(1)} %copy-done.1, ...), custom_call_target="tpu_custom_call", output_to_operand_aliasing={{0}: (5, {})} | custom-call | tf_op jit(solution)/shard_map/x_edge/pallas_call | solution.py:60
  14.5 1.3 %collective-permute-start.2 = (f32[25,8,128]{2,1,0:T(8,128)S(1)}, f32[25,8,128]{2,1,0:T(8,128)S(1)}, u32[]{:S(2)}, u32[]{:S(2)}) collective-permute-start(f32[25,8,128]{2,1,0:T(8,128)S(1)} %get-tuple-element.26), channel_id=1, source_target_pairs={{0,2},{2,4},{4,6},{6,8},{8,10},{10,12},{12,14},{14,0},{1,3},{3,5},... | collective-permute-start | bytes 307208 | tf_op jit(solution)/shard_map/ppermute | solution.py:512
  15.8 2.5 %collective-permute-start.3 = (f32[25,8,128]{2,1,0:T(8,128)S(1)}, f32[25,8,128]{2,1,0:T(8,128)S(1)}, u32[]{:S(2)}, u32[]{:S(2)}) collective-permute-start(f32[25,8,128]{2,1,0:T(8,128)S(1)} %get-tuple-element.27), channel_id=1, source_target_pairs={{0,14},{2,0},{4,2},{6,4},{8,6},{10,8},{12,10},{14,12},{1,15},{3,1}... | collective-permute-start | bytes 307208 | tf_op jit(solution)/shard_map/ppermute | solution.py:513
  18.3 1.6 %y_inner.1 = (f32[4,2,2,272,128]{4,3,2,1,0:T(8,128)S(1)}, f32[272,128]{1,0:T(8,128)S(1)}) custom-call(f32[4,2,2,272,128]{4,3,2,1,0:T(8,128)S(1)} %get-tuple-element.24.x_t, f32[4,2,272,128]{3,2,1,0:T(8,128)S(1)} %get-tuple-element.23.cy_t, f32[272,128]{1,0:T(8,128)S(1)} %get-tuple-element.25.h_t), custom_call_target="tpu_custom_call" | custom-call | flops 20000000 | bytes 6000000 | tf_op jit(solution)/shard_map/y_inner/pallas_call | solution.py:60
  19.9 0.4 collective-permute-done.2.from_l
  20.3 0.2 collective-permute-done.3.from_r
  20.5 2.3 %y_edge.1 = (f32[4,2,2,272,128]{4,3,2,1,0:T(8,128)S(1)}, f32[272,128]{1,0:T(8,128)S(1)}, f32[17,272,128]{2,1,0:T(8,128)S(1)}, f32[2,4,256,256]{3,2,1,0:T(8,128)}) custom-call(f32[4,2,2,272,128]{4,3,2,1,0:T(8,128)S(1)} %get-tuple-element.24.x_t, f32[4,2,272,128]{3,2,1,0:T(8,128)S(1)} %get-tuple-element.23.cy_t, ...), custom_call_target="tpu_custom_call", output_to_operand_aliasing={{0}: (5, {}), {1}: (6, {})} | custom-call | tf_op jit(solution)/shard_map/y_edge/pallas_call | solution.py:60
  22.8 0.0 copy-start.3
  22.8 1.4 %copy-done.3 = f32[4,2,2,272,128]{4,3,2,1,0:T(8,128)} copy-done((f32[4,2,2,272,128]{4,3,2,1,0:T(8,128)}, f32[4,2,2,272,128]{4,3,2,1,0:T(8,128)S(1)}, u32[]{:S(2)}) %copy-start.3) | copy-done | bytes 2228248
  24.1 3.0 %collective-permute-start.4 = (f32[17,272,128]{2,1,0:T(8,128)S(1)}, f32[17,272,128]{2,1,0:T(8,128)}, u32[]{:S(2)}, u32[]{:S(2)}) collective-permute-start(f32[17,272,128]{2,1,0:T(8,128)S(1)} %get-tuple-element.31.s.own), channel_id=1, source_target_pairs={{0,1},{1,0},{2,3},{3,2},{4,5},{5,4},{6,7},{7,6},{8,9},{9,8},{10,11... | collective-permute-start | bytes 7102472 | tf_op jit(solution)/shard_map/ppermute | solution.py:516
  27.2 0.0 copy-start.4
  27.2 1.6 %copy-done.4 = f32[4,2,2,272,128]{4,3,2,1,0:T(8,128)S(1)} copy-done((f32[4,2,2,272,128]{4,3,2,1,0:T(8,128)S(1)}, f32[4,2,2,272,128]{4,3,2,1,0:T(8,128)}, u32[]{:S(2)}) %copy-start.4) | copy-done | bytes 2228248
  28.8 0.0 copy-start.6
  28.8 0.9 %own_slopes.1 = (f32[4,2,2,256,128]{4,3,2,1,0:T(8,128)S(1)}, f32[4,2,2,256,128]{4,3,2,1,0:T(8,128)S(1)}) custom-call(f32[17,272,128]{2,1,0:T(8,128)S(1)} %get-tuple-element.31.s.own, f32[4,2,2,272,128]{4,3,2,1,0:T(8,128)S(1)} %copy-done.4), custom_call_target="tpu_custom_call" | custom-call | flops 20000000 | bytes 6000000 | tf_op jit(solution)/shard_map/own_slopes/pallas_call | solution.py:60
  29.8 1.7 %collective-permute-done.4.other = f32[17,272,128]{2,1,0:T(8,128)} collective-permute-done((f32[17,272,128]{2,1,0:T(8,128)S(1)}, f32[17,272,128]{2,1,0:T(8,128)}, u32[]{:S(2)}, u32[]{:S(2)}) %collective-permute-start.4) | collective-permute-done | bytes 2367520 | tf_op jit(solution)/shard_map/ppermute | solution.py:516
  31.5 0.0 copy-done.6
  31.5 9.1 %gradient.1 = (f32[6,2,3,8,32,256]{5,4,3,2,1,0:T(8,128)}, f32[6,8,32,256]{3,2,1,0:T(8,128)}) custom-call(s32[1,8]{1,0:T(1,128)S(1)} %copy-done.6, s32[1]{0:T(128)} %bitcast.core, f32[17,272,128]{2,1,0:T(8,128)S(1)} %get-tuple-element.31.s.own, f32[17,272,128]{2,1,0:T(8,128)} %collective-permute-done.4.other, ...), custom_call_target="tpu_custom_call" | custom-call | tf_op jit(solution)/shard_map/gradient/pallas_call | solution.py:485
Async XLA Ops:
  0.6 9.0 %copy-start.2 = (f32[4,256,256]{2,1,0:T(8,128)S(1)}, f32[4,256,256]{2,1,0:T(8,128)}, u32[]{:S(2)}) copy-start(f32[4,256,256]{2,1,0:T(8,128)} %cx.5) | copy-start | bytes 3145732
  0.6 9.0 %copy-start.1 = (f32[4,256,256]{2,1,0:T(8,128)S(1)}, f32[4,256,256]{2,1,0:T(8,128)}, u32[]{:S(2)}) copy-start(f32[4,256,256]{2,1,0:T(8,128)} %t.5) | copy-start | bytes 3145732
  0.7 9.0 %copy-start = (f32[4,256,256]{2,1,0:T(8,128)S(1)}, f32[4,256,256]{2,1,0:T(8,128)}, u32[]{:S(2)}) copy-start(f32[4,256,256]{2,1,0:T(8,128)} %d.5) | copy-start | bytes 3145732
  2.5 10.5 %collective-permute-start = (f32[4,4,8,256]{3,2,1,0:T(8,128)}, f32[4,4,8,256]{3,2,1,0:T(8,128)S(1)}, u32[]{:S(2)}, u32[]{:S(2)}) collective-permute-start(f32[4,4,8,256]{3,2,1,0:T(8,128)} %get-tuple-element.20), channel_id=1, source_target_pairs={{0,16},{16,32},{32,48},{48,64},{64,80},{80,96},{96,112},{112,0},{1... | collective-permute-start | bytes 393224 | tf_op jit(solution)/shard_map/ppermute | solution.py:508
  6.1 7.5 %collective-permute-start.1 = (f32[4,4,8,256]{3,2,1,0:T(8,128)}, f32[4,4,8,256]{3,2,1,0:T(8,128)S(1)}, u32[]{:S(2)}, u32[]{:S(2)}) collective-permute-start(f32[4,4,8,256]{3,2,1,0:T(8,128)} %get-tuple-element.21), channel_id=1, source_target_pairs={{0,112},{16,0},{32,16},{48,32},{64,48},{80,64},{96,80},{112,96},{1... | collective-permute-start | bytes 393224 | tf_op jit(solution)/shard_map/ppermute | solution.py:509
  9.7 1.2 %copy-start.5 = (f32[4,256,256]{2,1,0:T(8,128)S(1)}, f32[4,256,256]{2,1,0:T(8,128)}, u32[]{:S(2)}) copy-start(f32[4,256,256]{2,1,0:T(8,128)} %cy.3) | copy-start | bytes 3145732
  14.5 5.8 %collective-permute-start.2 = (f32[25,8,128]{2,1,0:T(8,128)S(1)}, f32[25,8,128]{2,1,0:T(8,128)S(1)}, u32[]{:S(2)}, u32[]{:S(2)}) collective-permute-start(f32[25,8,128]{2,1,0:T(8,128)S(1)} %get-tuple-element.26), channel_id=1, source_target_pairs={{0,2},{2,4},{4,6},{6,8},{8,10},{10,12},{12,14},{14,0},{1,3},{3,5},... | collective-permute-start | bytes 307208 | tf_op jit(solution)/shard_map/ppermute | solution.py:512
  15.8 4.7 %collective-permute-start.3 = (f32[25,8,128]{2,1,0:T(8,128)S(1)}, f32[25,8,128]{2,1,0:T(8,128)S(1)}, u32[]{:S(2)}, u32[]{:S(2)}) collective-permute-start(f32[25,8,128]{2,1,0:T(8,128)S(1)} %get-tuple-element.27), channel_id=1, source_target_pairs={{0,14},{2,0},{4,2},{6,4},{8,6},{10,8},{12,10},{14,12},{1,15},{3,1}... | collective-permute-start | bytes 307208 | tf_op jit(solution)/shard_map/ppermute | solution.py:513
  22.8 1.4 %copy-start.3 = (f32[4,2,2,272,128]{4,3,2,1,0:T(8,128)}, f32[4,2,2,272,128]{4,3,2,1,0:T(8,128)S(1)}, u32[]{:S(2)}) copy-start(f32[4,2,2,272,128]{4,3,2,1,0:T(8,128)S(1)} %get-tuple-element.32.s_t) | copy-start | bytes 6684676
  24.1 7.3 %collective-permute-start.4 = (f32[17,272,128]{2,1,0:T(8,128)S(1)}, f32[17,272,128]{2,1,0:T(8,128)}, u32[]{:S(2)}, u32[]{:S(2)}) collective-permute-start(f32[17,272,128]{2,1,0:T(8,128)S(1)} %get-tuple-element.31.s.own), channel_id=1, source_target_pairs={{0,1},{1,0},{2,3},{3,2},{4,5},{5,4},{6,7},{7,6},{8,9},{9,8},{10,11... | collective-permute-start | bytes 7102472 | tf_op jit(solution)/shard_map/ppermute | solution.py:516
  27.2 1.6 %copy-start.4 = (f32[4,2,2,272,128]{4,3,2,1,0:T(8,128)S(1)}, f32[4,2,2,272,128]{4,3,2,1,0:T(8,128)}, u32[]{:S(2)}) copy-start(f32[4,2,2,272,128]{4,3,2,1,0:T(8,128)} %copy-done.3) | copy-start | bytes 6684676
  28.8 2.7 %copy-start.6 = (s32[1,8]{1,0:T(1,128)S(1)}, s32[1,8]{1,0:T(1,128)}, u32[]{:S(2)}) copy-start(s32[1,8]{1,0:T(1,128)} %owner.1) | copy-start | bytes 100
where the time goes:
time: 40.8 us; the launch traced here: 40.6 us
  Pallas kernels  18.3 us (45%)
  starting transfers between devices  14.1 us (35%)
  local copies, waits for them, and re-layouts  4.23 us (10%)
  waiting for transfers between devices  3.37 us (8%)
  between operations  0.7 us (2%)
    pallas_call x1, Pallas kernels, gradients_of(): pl.pallas_call(gradient_kernel, grid_spec=pltpu.PrefetchScalarGridSpec(nu...  9.13 us
    pallas_call x6, Pallas kernels, call(): pl.pallas_call(kernel, in_specs=[pl.BlockSpec(memory_space=x) for x in sp...  9.13 us
    unnamed x14, local copies, waits for them, and re-layouts  4.23 us
    ppermute x1, starting transfers between devices, per_device(): left = lax.ppermute(hi, 'gx', ring(nx, 1))  3.64 us
    ppermute x1, starting transfers between devices, per_device(): right = lax.ppermute(lo, 'gx', ring(nx, -1))  3.55 us
    ppermute x1, starting transfers between devices, per_device(): other = lax.ppermute(swept, 'sa', ring(2, 1))  3.04 us
    ppermute x1, starting transfers between devices, per_device(): from_r = lax.ppermute(to_l, 'gy', ring(ny, -1))  2.53 us
    ppermute x1, waiting for transfers between devices, per_device(): other = lax.ppermute(swept, 'sa', ring(2, 1))  1.72 us
  transfers between devices with their start and end apart: 5, of which 5 were waited for; matrix products, arithmetic and copies ran while one was open for 0% of the time, Pallas kernels for 10%

commit v1 on v0

--- a/solution.py
+++ b/solution.py
@@ -77,31 +77,49 @@
 SWEEP_COST = pl.CostEstimate(flops=20_000_000, bytes_accessed=6_000_000, transcendentals=0)
 
 
-def edge_rows_kernel(d, t, cx, cy, lo, hi, sems):
-    rows = d.shape[1]
+LAST = (5, 5, 3, 2)
+FIRST = (4, 4, 2, 2)
+
+
+def padded(rows):
+    return -(-rows // 8) * 8
+
+
+def place(counts, p, f):
+    return p * sum(counts) + sum(counts[:f]), counts[f]
+
+
+def edge_rows_kernel(d, t, cx, cy, lo, hi, first, last, sems):
+    planes, rows, _ = d.shape
     copies = []
     for f, ref in enumerate((d, t, cx, cy)):
-        copies.append(pltpu.make_async_copy(ref.at[:, 0:RIM, :], lo.at[f], sems.at[f]))
+        copies.append(pltpu.make_async_copy(ref.at[:, 0:RIM, :], first.at[f], sems.at[f]))
         copies.append(
-            pltpu.make_async_copy(ref.at[:, rows - RIM : rows, :], hi.at[f], sems.at[4 + f])
+            pltpu.make_async_copy(ref.at[:, rows - RIM : rows, :], last.at[f], sems.at[4 + f])
         )
     for c in copies:
         c.start()
     for c in copies:
         c.wait()
+    for p in range(planes):
+        for f in range(4):
+            at, n = place(FIRST, p, f)
+            lo[at : at + n, :] = first[f, p, 0:n, :]
+            at, n = place(LAST, p, f)
+            hi[at : at + n, :] = last[f, p, RIM - n : RIM, :]
 
 
 def edge_rows(fields):
     planes, _, cols = fields[0].shape
-    shape = out(4, planes, RIM, cols)
+    tiles = pltpu.VMEM((4, planes, RIM, cols), F32)
     return call(
         edge_rows_kernel,
-        (shape, shape),
+        (out(padded(planes * sum(FIRST)), cols), out(padded(planes * sum(LAST)), cols)),
         fields,
         "edge_rows",
         spaces=[pl.ANY] * 4,
-        scratch=[pltpu.SemaphoreType.DMA((8,))],
-        mib=60,
+        scratch=[tiles, tiles, pltpu.SemaphoreType.DMA((8,))],
+        mib=56,
     )
 
 
@@ -150,7 +168,11 @@
     lead, rim_at = (0, 16) if high else (8, 0)
     for f in range(3):
         win[f, lead : lead + 16, :] = own(f)
-        win[f, rim_at : rim_at + 8, :] = rim(f)
+        beyond = rim(f)
+        if beyond is not None:
+            n = beyond.shape[0]
+            at = rim_at if high else 8 - n
+            win[f, at : at + n, :] = beyond
 
     def store(f, r, n, value):
         res[f, pl.ds(r, n), :] = value
@@ -184,11 +206,16 @@
     for p in range(planes):
         for h in range(2):
             for high in range(2):
-                rim = right if high else left
+                rim, counts = (right, FIRST) if high else (left, LAST)
                 at = slice(rows - 16, rows) if high else slice(0, 16)
+
+                def beyond(f):
+                    r, n = place(counts, p, f)
+                    return rim[r : r + n, half(h)]
+
                 edge_sweep(
                     lambda f: (d, t, cx)[f][p, at, half(h)],
-                    lambda f: rim[f, p, :, half(h)],
+                    beyond,
                     high,
                     win,
                     a_scr,
@@ -200,11 +227,11 @@
                     if high:
                         xs[p, f, h, rows : rows + RIM, :] = res[f, 8:16, :]
                         rim_rows[h, k : k + 2, :] = res[f, 16:18, :]
-                        rim_rows[h, 32 + k : 34 + k, :] = rim[3, p, 0:2, half(h)]
+                        rim_rows[h, 32 + k : 34 + k, :] = beyond(3)
                     else:
                         xs[p, f, h, RIM : 2 * RIM, :] = res[f, 8:16, :]
                         rim_rows[h, k : k + 2, :] = res[f, 6:8, :]
-                        rim_rows[h, 32 + k : 34 + k, :] = rim[3, p, 6:8, half(h)]
+                        rim_rows[h, 32 + k : 34 + k, :] = beyond(3)
     for h in range(2):
         h_t[half(h, RIM), :] = rim_rows[h].T
     for p in range(planes):
@@ -212,20 +239,34 @@
             for x in range(2):
                 for h in range(2):
                     x_t[p, f, x, half(h, RIM), :] = xs[p, f, h, half(x, RIM), :].T
-    for buf, at in ((to_l, slice(RIM, 2 * RIM)), (to_r, slice(rows, rows + RIM))):
+    for buf, counts in ((to_l, FIRST), (to_r, LAST)):
+
+        def put(i, f, ref):
+            at, n = y_place(counts, i, f)
+            top = RIM if counts is FIRST else RIM + rows - n
+            buf[at : at + n, :] = ref[top : top + n, :]
+
         for p in range(planes):
             for x in range(2):
                 for f in range(2):
-                    buf[(p * 2 + f) * 2 + x] = x_t[p, f, x, at, :]
-                buf[16 + p * 2 + x] = cy_t[p, x, at, :]
-        buf[24] = h_t[at, :]
+                    put((p * 2 + f) * 2 + x, 0, x_t.at[p, f, x])
+                put(p * 2 + x, 2, cy_t.at[p, x])
+        put(16, 0, h_t)
+
+
+def y_place(counts, i, f):
+    return (17 * counts[0] if f == 2 else 0) + i * counts[f], counts[f]
+
+
+def y_rim(counts):
+    return out(padded(17 * counts[0] + 8 * counts[2]), LANES)
 
 
 def x_edge(d, t, cx, left, right, xs, cy_t):
     ext = xs.shape[3]
     return call(
         x_edge_kernel,
-        (out(*xs.shape), out(*xs.shape), out(ext, LANES), out(25, RIM, LANES), out(25, RIM, LANES)),
+        (out(*xs.shape), out(*xs.shape), out(ext, LANES), y_rim(FIRST), y_rim(LAST)),
         (d, t, cx, left, right, xs, cy_t),
         "x_edge",
         scratch=[pltpu.VMEM((2, LANES, LANES), F32)] + EDGE_SCRATCH,
@@ -288,14 +329,19 @@
 
 
 def y_edge_kernel(
-    x_t, cy_t, h_t, from_l, from_r, st_in, sh_in, s_t, sh_t, s, adv, rim_rows, win, a_scr, f_scr, res
+    x_t, cy_t, h_t, from_l, from_r, st_in, sh_in, s_t, sh_t, s, rim_rows, win, a_scr, f_scr, res
 ):
     planes = x_t.shape[0]
     ext = x_t.shape[3]
     rows = ext - 2 * RIM
 
     for high in range(2):
-        rim = from_r if high else from_l
+        rim, counts = (from_r, FIRST) if high else (from_l, LAST)
+
+        def beyond(i, f):
+            r, n = y_place(counts, i, f)
+            return rim[r : r + n, :]
+
         at = slice(ext - 24, ext - 8) if high else slice(8, 24)
         to = slice(ext - 16, ext) if high else slice(0, 16)
         got = slice(8, 24) if high else slice(0, 16)
@@ -303,7 +349,7 @@
             for x in range(2):
                 edge_sweep(
                     lambda f: cy_t[p, x, at, :] if f == 2 else x_t[p, f, x, at, :],
-                    lambda f: rim[16 + p * 2 + x] if f == 2 else rim[(p * 2 + f) * 2 + x],
+                    lambda f: beyond(p * 2 + x if f == 2 else (p * 2 + f) * 2 + x, f),
                     high,
                     win,
                     a_scr,
@@ -314,13 +360,13 @@
                     s_t[p, f, x, to, :] = res[f, got, :]
                     k = (f * 4 + p) * 8
                     if high:
-                        rim_rows[x, k : k + 2, :] = res[f, 16:18, :]
+                        k = (k + LANES - 2) % LANES
+                        rim_rows[x, k : k + 2, :] = rows_slope(s_t.at[p, f, x], ext - 16, 8)[6:8]
                     else:
-                        k = (k + LANES - 2) % LANES
-                        rim_rows[x, k : k + 2, :] = res[f, 6:8, :]
+                        rim_rows[x, k : k + 2, :] = rows_slope(s_t.at[p, f, x], 8, 8)[0:2]
         edge_sweep(
             lambda f: rim_courant(h_t[at, :]) if f == 2 else h_t[at, :],
-            lambda f: rim_courant(rim[24]) if f == 2 else rim[24],
+            lambda f: rim_courant(beyond(16, 0)) if f == 2 else beyond(16, 0),
             high,
             win,
             a_scr,
@@ -339,28 +385,24 @@
                 s[i, RIM - 2 : RIM, :] = beyond[k : k + 2, :]
                 s[i, RIM + rows : RIM + rows + 2, :] = beyond[k + 2 : k + 4, :]
                 for x in range(2):
-                    block = s_t[p, f, x, half(h, RIM), :].T
-                    s[i, half(x, RIM), :] = block
-                    adv[f, p, half(x), half(h)] = block
+                    s[i, half(x, RIM), :] = s_t[p, f, x, half(h, RIM), :].T
 
 
 def y_edge(x_t, cy_t, h_t, from_l, from_r, s_t, sh_t):
-    planes, _, _, ext, _ = x_t.shape
-    rows = ext - 2 * RIM
+    ext = x_t.shape[3]
     res = call(
         y_edge_kernel,
         (
             out(*s_t.shape),
             out(*sh_t.shape),
             out(17, ext, LANES),
-            out(2, planes, rows, 2 * LANES),
         ),
         (x_t, cy_t, h_t, from_l, from_r, s_t, sh_t),
         "y_edge",
         scratch=[pltpu.VMEM((2, LANES, LANES), F32)] + EDGE_SCRATCH,
         aliases={5: 0, 6: 1},
     )
-    return res[0], res[2], res[3]
+    return res[2]
 
 
 def slope(w1, w2):
@@ -374,132 +416,275 @@
     )
 
 
-def own_slopes_kernel(s, s_t, gx, gy):
-    planes, _, _, ext, _ = s_t.shape
-    rows = ext - 2 * RIM
-
-    def body(p, _):
+def columns_slope(pair, turned, store):
+    for h in range(2):
+        turned[half(h, RIM), :] = pair(h).T
+    for h in range(2):
+        store(h, rows_slope(turned, RIM + h * LANES, LANES).T)
+
+
+def edge_columns(strips, k):
+    return pltpu.roll(strips, LANES - k * 8, 1)
+
+
+def with_edge(value, edge, h, lane):
+    return jnp.where(lane >= LANES - 2 if h else lane < 2, edge, value)
+
+
+def piece_of(owner, core, slot):
+    rank = jnp.int32(0)
+    piece = jnp.int32(0)
+    for j in range(NP):
+        mine = owner[0, j] == core
+        piece = jnp.where(jnp.logical_and(mine, rank == slot), j, piece)
+        rank = rank + mine.astype(jnp.int32)
+    return piece, slot < rank
+
+
+def own_slopes_kernel(owner, core, s, adv, grad, own, zeros, turned, adv_sem, sems):
+    planes, rows = adv.shape[1:3]
+    width = grad.shape[4]
+    me = core[0]
+    copies = []
+    for p in range(planes):
         for f in range(2):
+            for h in range(2):
+                i = (p * 2 + f) * 2 + h
+                copies.append(
+                    pltpu.make_async_copy(
+                        s.at[i, RIM : RIM + rows, :], adv.at[f, p, :, half(h)], adv_sem.at[i]
+                    )
+                )
+    for c in copies:
+        c.start()
+    zeros[...] = jnp.zeros_like(zeros)
+    mine = pl.ds(pl.multiple_of(planes * me, planes), planes)
+
+    def send(k, f):
+        for slot in range(CAP):
+            piece, used = piece_of(owner, me, slot)
+            to = grad.at[slot, f, k, mine]
+            sem = sems.at[slot, f, k]
+
+            @pl.when(used)
+            def _():
+                at = pl.ds(pl.multiple_of(piece * width, width), width)
+                pltpu.make_async_copy(own.at[k, f, :, at, :], to, sem).start()
+
+            @pl.when(jnp.logical_not(used))
+            def _():
+                pltpu.make_async_copy(zeros, to, sem).start()
+
+    for f in range(2):
+
+        def x_body(p, _):
             for h in range(2):
                 ref = s.at[(p * 2 + f) * 2 + h]
                 for r in range(0, rows, 64):
-                    gx[p, f, h, r : r + 64, :] = rows_slope(ref, RIM + r, 64)
-                for x in range(2):
-                    ref_t = s_t.at[p, f, x]
-                    gy[p, f, h, half(x), :] = rows_slope(ref_t, RIM + h * LANES, LANES).T
-        return 0
-
-    lax.fori_loop(0, planes, body, 0, unroll=False)
-
-
-def own_slopes(s, s_t):
-    planes, _, _, ext, _ = s_t.shape
-    shape = out(planes, 2, 2, ext - 2 * RIM, LANES)
-    return call(own_slopes_kernel, (shape, shape), (s, s_t), "own_slopes", cost=SWEEP_COST)
-
-
-def gradient_kernel(owner, core, own, other, own_x, own_y, grad, wedge):
-    slot = pl.program_id(0)
-    s = core[0]
-    rank = jnp.int32(0)
-    piece = jnp.int32(0)
-    for j in range(NP):
-        mine = owner[0, j] == s
-        piece = jnp.where(jnp.logical_and(mine, rank == slot), j, piece)
-        rank = rank + mine.astype(jnp.int32)
-    used = slot < rank
+                    own[0, f, p, r : r + 64, half(h)] = rows_slope(ref, RIM + r, 64)
+            return 0
+
+        lax.fori_loop(0, planes, x_body, 0, unroll=False)
+        send(0, f)
+    n = 8
+    lane = lane_iota(n)
+    for f in range(2):
+
+        def y_body(p, _):
+            for x in range(2):
+
+                def pair(h):
+                    return s[(p * 2 + f) * 2 + h, half(x, RIM), :]
+
+                def store(h, y):
+                    own[1, f, p, half(x), half(h)] = y
+
+                columns_slope(pair, turned.at[x], store)
+            strip = f * 4 + p
+            for r in range(0, rows, n):
+                edge = edge_columns(s[16, RIM + r : RIM + r + n, :], strip)
+                for h in range(2):
+                    at = own.at[1, f, p, r : r + n, half(h)]
+                    at[...] = with_edge(at[...], edge, h, lane)
+            return 0
+
+        lax.fori_loop(0, planes, y_body, 0, unroll=False)
+        send(1, f)
+    for c in copies:
+        c.wait()
+    for slot in range(CAP):
+        for f in range(2):
+            for k in range(2):
+                pltpu.make_async_copy(zeros, grad.at[slot, f, k, mine], sems.at[slot, f, k]).wait()
+
+
+SMEM = pl.BlockSpec(memory_space=pltpu.SMEM)
+VMEM = pl.BlockSpec(memory_space=pltpu.VMEM)
+ANY = pl.BlockSpec(memory_space=pl.ANY)
+
+
+def own_slopes(owner, core, s):
+    planes = (s.shape[0] - 1) // 4
+    rows = s.shape[1] - 2 * RIM
+    cols = 2 * LANES
+    width = rows // NP
+    return pl.pallas_call(
+        own_slopes_kernel,
+        in_specs=[SMEM, SMEM, VMEM],
+        out_specs=(ANY, ANY, VMEM),
+        out_shape=(
+            out(2, planes, rows, cols),
+            out(CAP, 2, 3, 2 * planes, width, cols),
+            out(2, 2, planes, rows, cols),
+        ),
+        scratch_shapes=[
+            pltpu.VMEM((planes, width, cols), F32),
+            pltpu.VMEM((2, rows + 2 * RIM, LANES), F32),
+            pltpu.SemaphoreType.DMA((16,)),
+            pltpu.SemaphoreType.DMA((CAP, 2, 2)),
+        ],
+        compiler_params=pltpu.CompilerParams(vmem_limit_bytes=20 * MIB),
+        cost_estimate=SWEEP_COST,
+        name="own_slopes",
+    )(owner, core, s)
+
+
+def gradient_kernel(
+    owner, core, own, other, own_xy, grad_in, grad, wedge, part, wpart, turned, zeros, sems, wsems
+):
+    planes = own_xy.shape[2]
     width = grad.shape[4]
-
-    @pl.when(jnp.logical_not(used))
-    def _():
-        grad[...] = jnp.zeros_like(grad)
-        wedge[...] = jnp.zeros_like(wedge)
-
-    @pl.when(used)
-    def _():
+    me = core[0]
+    mine = pl.ds(pl.multiple_of(planes * me, planes), planes)
+    theirs = pl.ds(pl.multiple_of(planes * (1 - me), planes), planes)
+    kinds = ((2, mine), (2, theirs), (0, theirs), (1, theirs))
+
+    def copies(slot, used=True):
+        res = []
+        for f in range(2):
+            for k, (dim, where) in enumerate(kinds):
+                src = part.at[slot, f, k] if used else zeros
+                res.append(
+                    pltpu.make_async_copy(src, grad.at[slot, f, dim, where], sems.at[slot, f, k])
+                )
+        for k, where in enumerate((mine, theirs)):
+            src = wpart.at[slot, k] if used else zeros
+            res.append(pltpu.make_async_copy(src, wedge.at[slot, where], wsems.at[slot, k]))
+        return res
+
+    def fill(slot, piece):
         n = 8
         lane = lane_iota(n)
         first = pl.multiple_of(piece * width, 8)
+
+        for f in range(2):
+
+            def pair(h):
+                at = pl.ds(first + RIM, width)
+                return jnp.concatenate(
+                    [other[(p * 2 + f) * 2 + h, at, :] for p in range(planes)], axis=0
+                )
+
+            def store(h, y):
+                for p in range(planes):
+                    part[slot, f, 3, p, :, half(h)] = y[p * width : (p + 1) * width, :]
+
+            columns_slope(pair, turned.at[f], store)
 
         def body(i, _):
             at = pl.multiple_of(first + i * n, n)
             r = pl.multiple_of(RIM + at, n)
             to = pl.ds(pl.multiple_of(i * n, n), n)
-            rim = other[16, pl.ds(r, n), :]
+            strips = other[16, pl.ds(r, n), :]
+            edges = [edge_columns(strips, k) for k in range(2 * planes)]
             for h in range(2):
-
-                def plane(z, f, row, hh=h):
-                    ref = own if z < 4 else other
-                    return ref[((z % 4) * 2 + f) * 2 + hh, pl.ds(row, n), :]
+                cols = half(h)
+
+                def plane(z, f, row):
+                    ref = own if z < planes else other
+                    return ref[((z % planes) * 2 + f) * 2 + h, pl.ds(row, n), :]
 
                 q = [[plane(z, f, r) for f in range(2)] for z in range(8)]
                 for z in range(8):
-                    zo = lax.rem(z + 4 * s, 8)
                     g = []
+                    p = z % planes
                     for f in range(2):
-                        if z < 4:
-                            x_slope = own_x[z, f, h, pl.ds(at, n), :]
-                            y_slope = own_y[z, f, h, pl.ds(at, n), :]
+                        z_slope = slope(
+                            q[(z + 1) % 8][f] - q[(z + 7) % 8][f],
+                            q[(z + 2) % 8][f] - q[(z + 6) % 8][f],
+                        )
+                        part[slot, f, z // planes, p, to, cols] = z_slope
+                        if z < planes:
+                            x_slope = own_xy[0, f, p, pl.ds(at, n), cols]
+                            y_slope = own_xy[1, f, p, pl.ds(at, n), cols]
                         else:
-                            here = q[z][f]
-                            there = plane(z, f, r, 1 - h)
-                            beyond = pltpu.roll(rim, (LANES - (f * 4 + z % 4) * 8) % LANES, 1)
-                            after = beyond if h else there
-                            before = there if h else beyond
-
-                            def step(k):
-                                up = pltpu.roll(jnp.where(lane < k, after, here), LANES - k, 1)
-                                down = pltpu.roll(
-                                    jnp.where(lane >= LANES - k, before, here), k, 1
-                                )
-                                return up - down
-
                             x_slope = slope(
                                 plane(z, f, r + 1) - plane(z, f, r - 1),
                                 plane(z, f, r + 2) - plane(z, f, r - 2),
                             )
-                            y_slope = slope(step(1), step(2))
-                        z_slope = slope(
-                            q[(z + 1) % 8][f] - q[(z + 7) % 8][f],
-                            q[(z + 2) % 8][f] - q[(z + 6) % 8][f],
-                        )
+                            part[slot, f, 2, p, to, cols] = x_slope
+                            y_slope = with_edge(
+                                part[slot, f, 3, p, to, cols], edges[f * 4 + p], h, lane
+                            )
+                            part[slot, f, 3, p, to, cols] = y_slope
                         g.append((x_slope, y_slope, z_slope))
-                        for k in range(3):
-                            grad[0, f, k, zo, to, half(h)] = g[-1][k]
                     rx, ry, rz = g[0]
                     tx, ty, tz = g[1]
                     a = ry * tz - rz * ty
                     b = rz * tx - rx * tz
                     c = rx * ty - ry * tx
-                    wedge[0, zo, to, half(h)] = a * a + b * b + c * c
+                    wpart[slot, z // planes, p, to, cols] = a * a + b * b + c * c
             return 0
 
         lax.fori_loop(0, width // n, body, 0, unroll=False)
 
-
-def gradients_of(owner, core, own, other, own_x, own_y):
-    rows = own.shape[1] - 2 * RIM
+    def slot_body(slot, _):
+        piece, used = piece_of(owner, me, slot)
+
+        @pl.when(used)
+        def _():
+            fill(slot, piece)
+            for c in copies(slot):
+                c.start()
+
+        @pl.when(jnp.logical_not(used))
+        def _():
+            for c in copies(slot, False):
+                c.start()
+
+        return 0
+
+    zeros[...] = jnp.zeros_like(zeros)
+    lax.fori_loop(0, CAP, slot_body, 0, unroll=False)
+
+    def wait_body(slot, _):
+        for c in copies(slot):
+            c.wait()
+        return 0
+
+    lax.fori_loop(0, CAP, wait_body, 0, unroll=False)
+
+
+def gradients_of(owner, core, own, other, own_xy, grad):
+    _, _, planes, rows, cols = own_xy.shape
     width = rows // NP
-    cols = 2 * LANES
-    vmem = pl.BlockSpec(memory_space=pltpu.VMEM)
     return pl.pallas_call(
         gradient_kernel,
-        grid_spec=pltpu.PrefetchScalarGridSpec(
-            num_scalar_prefetch=2,
-            grid=(CAP,),
-            in_specs=[vmem] * 4,
-            out_specs=(
-                pl.BlockSpec((1, 2, 3, 8, width, cols), lambda k, o, c: (k, 0, 0, 0, 0, 0)),
-                pl.BlockSpec((1, 8, width, cols), lambda k, o, c: (k, 0, 0, 0)),
-            ),
-        ),
-        out_shape=(
-            jax.ShapeDtypeStruct((CAP, 2, 3, 8, width, cols), F32),
-            jax.ShapeDtypeStruct((CAP, 8, width, cols), F32),
-        ),
-        compiler_params=pltpu.CompilerParams(vmem_limit_bytes=20 * MIB),
+        in_specs=[SMEM, SMEM, VMEM, VMEM, VMEM, ANY],
+        out_specs=(ANY, ANY),
+        out_shape=(out(*grad.shape), out(CAP, 2 * planes, width, cols)),
+        scratch_shapes=[
+            pltpu.VMEM((CAP, 2, 4, planes, width, cols), F32),
+            pltpu.VMEM((CAP, 2, planes, width, cols), F32),
+            pltpu.VMEM((2, rows + 2 * RIM, LANES), F32),
+            pltpu.VMEM((planes, width, cols), F32),
+            pltpu.SemaphoreType.DMA((CAP, 2, 4)),
+            pltpu.SemaphoreType.DMA((CAP, 2)),
+        ],
+        input_output_aliases={5: 0},
+        compiler_params=pltpu.CompilerParams(vmem_limit_bytes=24 * MIB),
         name="gradient",
-    )(owner, core, own, other, own_x, own_y)
+    )(owner, core, own, other, own_xy, grad)
 
 
 def per_device(density, heat, cx, cy, owner):
@@ -512,11 +697,11 @@
     from_l = lax.ppermute(to_r, "gy", ring(ny, 1))
     from_r = lax.ppermute(to_l, "gy", ring(ny, -1))
     s_t, sh_t = y_inner(x_t, cy_t, h_t)
-    s_t, swept, advected = y_edge(x_t, cy_t, h_t, from_l, from_r, s_t, sh_t)
+    swept = y_edge(x_t, cy_t, h_t, from_l, from_r, s_t, sh_t)
     other = lax.ppermute(swept, "sa", ring(2, 1))
-    own_x, own_y = own_slopes(swept, s_t)
     core = lax.axis_index("sa").astype(jnp.int32).reshape(1)
-    gradients, wedge = gradients_of(owner, core, swept, other, own_x, own_y)
+    advected, gradients, own_xy = own_slopes(owner, core, swept)
+    gradients, wedge = gradients_of(owner, core, swept, other, own_xy, gradients)
     return advected, gradients, wedge
 
 

time: 40.8 us -> 33.8 us (0.83)
  local copies, waits for them, and re-layouts: 4.23 us -> 0.02 us
  waiting for transfers between devices: 3.37 us -> 0.1 us
  Pallas kernels: 18.3 us -> 19.3 us
  starting transfers between devices: 14.1 us -> 13.6 us
    unnamed x14 -> x10, local copies, waits for them, and re-layouts: 4.23 us -> 0.02 us
    pallas_call x1 -> x2, Pallas kernels: 9.13 us -> 12.4 us  [the longest x1 7.31 us: gradients_of(): pl.pallas_call(gradient_kernel, in_specs=[SMEM, SMEM, VMEM, VMEM, VMEM, A...]
    pallas_call x6 -> x5, Pallas kernels: 9.13 us -> 6.9 us  [call(): pl.pallas_call(kernel, in_specs=[pl.BlockSpec(memory_space=x) for x in sp...]
    ppermute x1, waiting for transfers between devices: 1.72 us -> 0.01 us  [per_device(): other = lax.ppermute(swept, 'sa', ring(2, 1))]
    ppermute x1, starting transfers between devices: 1.28 us -> 0.38 us  [per_device(): from_l = lax.ppermute(to_r, 'gy', ring(ny, 1))]
    ppermute x1, starting transfers between devices: 2.53 us -> 3.26 us  [per_device(): from_r = lax.ppermute(to_l, 'gy', ring(ny, -1))]
    ppermute x1, waiting for transfers between devices: 0.59 us -> 0.01 us  [per_device(): right = lax.ppermute(lo, 'gx', ring(nx, -1))]
  transfers between devices with their start and end apart: 5 -> 5, of which waited for: 5 -> 1; matrix products, arithmetic and copies ran while one was open for 0% -> 0% of each run, Pallas kernels for 10% -> 25%
where the time goes in v1:
time: 33.8 us; the launch traced here: 33.7 us
  Pallas kernels  19.3 us (57%)
  starting transfers between devices  13.6 us (40%)
  between operations  0.75 us (2%)
    pallas_call x1, Pallas kernels, gradients_of(): pl.pallas_call(gradient_kernel, in_specs=[SMEM, SMEM, VMEM, VMEM, VMEM, A...  7.31 us
    pallas_call x5, Pallas kernels, call(): pl.pallas_call(kernel, in_specs=[pl.BlockSpec(memory_space=x) for x in sp...  6.9 us
    pallas_call x1, Pallas kernels, own_slopes(): pl.pallas_call(own_slopes_kernel, in_specs=[SMEM, SMEM, VMEM], out_specs=...  5.05 us
    ppermute x1, starting transfers between devices, per_device(): left = lax.ppermute(hi, 'gx', ring(nx, 1))  3.64 us
    ppermute x1, starting transfers between devices, per_device(): right = lax.ppermute(lo, 'gx', ring(nx, -1))  3.55 us
    ppermute x1, starting transfers between devices, per_device(): from_r = lax.ppermute(to_l, 'gy', ring(ny, -1))  3.26 us
    ppermute x1, starting transfers between devices, per_device(): other = lax.ppermute(swept, 'sa', ring(2, 1))  2.72 us
  transfers between devices with their start and end apart: 5, of which 1 were waited for; matrix products, arithmetic and copies ran while one was open for 0% of the time, Pallas kernels for 25%

profile of v1, /device:TPU:1, one launch (start us, length us, event | category | flops | bytes accessed | tf_op | source)
XLA Modules:
  0.0 33.7 jit_solution(12035405309763395132)
XLA Ops:
  0.6 0.0 copy-start.2
  0.6 0.0 copy-start.1
  0.7 0.0 copy-start
  0.7 0.0 copy-start.3
  0.7 1.8 %edge_rows.1 = (f32[48,256]{1,0:T(8,128)}, f32[64,256]{1,0:T(8,128)}) custom-call(f32[4,256,256]{2,1,0:T(8,128)} %d.5, f32[4,256,256]{2,1,0:T(8,128)} %t.5, f32[4,256,256]{2,1,0:T(8,128)} %cx.5, f32[4,256,256]{2,1,0:T(8,128)} %cy.3), custom_call_target="tpu_custom_call" | custom-call | tf_op jit(solution)/shard_map/edge_rows/pallas_call | solution.py:60
  2.4 3.6 %collective-permute-start = (f32[64,256]{1,0:T(8,128)}, f32[64,256]{1,0:T(8,128)S(1)}, u32[]{:S(2)}, u32[]{:S(2)}) collective-permute-start(f32[64,256]{1,0:T(8,128)} %get-tuple-element.19), channel_id=1, source_target_pairs={{0,16},{16,32},{32,48},{48,64},{64,80},{80,96},{96,112},{112,0},{1... | collective-permute-start | bytes 196616 | tf_op jit(solution)/shard_map/ppermute | solution.py:693
  6.1 3.6 %collective-permute-start.1 = (f32[48,256]{1,0:T(8,128)}, f32[48,256]{1,0:T(8,128)S(1)}, u32[]{:S(2)}, u32[]{:S(2)}) collective-permute-start(f32[48,256]{1,0:T(8,128)} %get-tuple-element.20), channel_id=1, source_target_pairs={{0,112},{16,0},{32,16},{48,32},{64,48},{80,64},{96,80},{112,96},{1... | collective-permute-start | bytes 147464 | tf_op jit(solution)/shard_map/ppermute | solution.py:694
  9.6 0.0 copy-done.2
  9.6 0.0 copy-done.1
  9.6 0.0 copy-done
  9.6 0.0 copy-done.3
  9.7 1.7 %x_inner.1 = (f32[4,2,2,272,128]{4,3,2,1,0:T(8,128)S(1)}, f32[4,2,272,128]{3,2,1,0:T(8,128)S(1)}) custom-call(f32[4,256,256]{2,1,0:T(8,128)S(1)} %copy-done, f32[4,256,256]{2,1,0:T(8,128)S(1)} %copy-done.1, f32[4,256,256]{2,1,0:T(8,128)S(1)} %copy-done.2, f32[4,256,256]{2,1,0:T(8,128)S(1)} %copy-done.3), custom_call_target="tpu_custom_call" | custom-call | flops 20000000 | bytes 6000000 | tf_op jit(solution)/shard_map/x_inner/pallas_call | solution.py:60
  11.3 0.0 collective-permute-done.1.right
  11.3 0.1 collective-permute-done.left
  11.4 0.9 %x_edge.1 = (f32[4,2,2,272,128]{4,3,2,1,0:T(8,128)S(1)}, f32[4,2,2,272,128]{4,3,2,1,0:T(8,128)S(1)}, f32[272,128]{1,0:T(8,128)S(1)}, f32[88,128]{1,0:T(8,128)S(1)}, f32[112,128]{1,0:T(8,128)S(1)}) custom-call(f32[4,256,256]{2,1,0:T(8,128)S(1)} %copy-done, f32[4,256,256]{2,1,0:T(8,128)S(1)} %copy-done.1, ...), custom_call_target="tpu_custom_call", output_to_operand_aliasing={{0}: (5, {})} | custom-call | tf_op jit(solution)/shard_map/x_edge/pallas_call | solution.py:60
  12.3 0.4 %collective-permute-start.2 = (f32[112,128]{1,0:T(8,128)S(1)}, f32[112,128]{1,0:T(8,128)S(1)}, u32[]{:S(2)}, u32[]{:S(2)}) collective-permute-start(f32[112,128]{1,0:T(8,128)S(1)} %get-tuple-element.25), channel_id=1, source_target_pairs={{0,2},{2,4},{4,6},{6,8},{8,10},{10,12},{12,14},{14,0},{1,3},{3,5},... | collective-permute-start | bytes 172040 | tf_op jit(solution)/shard_map/ppermute | solution.py:697
  12.7 3.3 %collective-permute-start.3 = (f32[88,128]{1,0:T(8,128)S(1)}, f32[88,128]{1,0:T(8,128)S(1)}, u32[]{:S(2)}, u32[]{:S(2)}) collective-permute-start(f32[88,128]{1,0:T(8,128)S(1)} %get-tuple-element.26), channel_id=1, source_target_pairs={{0,14},{2,0},{4,2},{6,4},{8,6},{10,8},{12,10},{14,12},{1,15},{3,1}... | collective-permute-start | bytes 135176 | tf_op jit(solution)/shard_map/ppermute | solution.py:698
  16.0 1.6 %y_inner.1 = (f32[4,2,2,272,128]{4,3,2,1,0:T(8,128)S(1)}, f32[272,128]{1,0:T(8,128)S(1)}) custom-call(f32[4,2,2,272,128]{4,3,2,1,0:T(8,128)S(1)} %get-tuple-element.23.x_t, f32[4,2,272,128]{3,2,1,0:T(8,128)S(1)} %get-tuple-element.22.cy_t, f32[272,128]{1,0:T(8,128)S(1)} %get-tuple-element.24.h_t), custom_call_target="tpu_custom_call" | custom-call | flops 20000000 | bytes 6000000 | tf_op jit(solution)/shard_map/y_inner/pallas_call | solution.py:60
  17.6 0.0 collective-permute-done.3.from_r
  17.6 0.0 collective-permute-done.2.from_l
  17.6 0.0 copy-start.4
  17.6 1.0 %y_edge.1 = (f32[4,2,2,272,128]{4,3,2,1,0:T(8,128)S(1)}, f32[272,128]{1,0:T(8,128)S(1)}, f32[17,272,128]{2,1,0:T(8,128)S(1)}) custom-call(f32[4,2,2,272,128]{4,3,2,1,0:T(8,128)S(1)} %get-tuple-element.23.x_t, f32[4,2,272,128]{3,2,1,0:T(8,128)S(1)} %get-tuple-element.22.cy_t, ...), custom_call_target="tpu_custom_call", output_to_operand_aliasing={{0}: (5, {}), {1}: (6, {})} | custom-call | tf_op jit(solution)/shard_map/y_edge/pallas_call | solution.py:60
  18.6 2.7 %collective-permute-start.4 = (f32[17,272,128]{2,1,0:T(8,128)S(1)}, f32[17,272,128]{2,1,0:T(8,128)}, u32[]{:S(2)}, u32[]{:S(2)}) collective-permute-start(f32[17,272,128]{2,1,0:T(8,128)S(1)} %get-tuple-element.29.s.own), channel_id=1, source_target_pairs={{0,1},{1,0},{2,3},{3,2},{4,5},{5,4},{6,7},{7,6},{8,9},{9,8},{10,11... | collective-permute-start | bytes 7102472 | tf_op jit(solution)/shard_map/ppermute | solution.py:701
  21.3 0.0 copy-done.4
  21.3 5.0 %own_slopes.1 = (f32[2,4,256,256]{3,2,1,0:T(8,128)}, f32[6,2,3,8,32,256]{5,4,3,2,1,0:T(8,128)}, f32[2,2,4,256,256]{4,3,2,1,0:T(8,128)S(1)}) custom-call(s32[1,8]{1,0:T(1,128)S(1)} %copy-done.4, s32[1]{0:T(128)} %bitcast.core, f32[17,272,128]{2,1,0:T(8,128)S(1)} %get-tuple-element.29.s.own), custom_call_target="tpu_custom_call" | custom-call | flops 20000000 | bytes 6000000 | tf_op jit(solution)/shard_map/own_slopes/pallas_call | solution.py:531
  26.4 0.0 collective-permute-done.4.other
  26.4 7.3 %gradient.1 = (f32[6,2,3,8,32,256]{5,4,3,2,1,0:T(8,128)}, f32[6,8,32,256]{3,2,1,0:T(8,128)}) custom-call(s32[1,8]{1,0:T(1,128)S(1)} %copy-done.4, s32[1]{0:T(128)} %bitcast.core, f32[17,272,128]{2,1,0:T(8,128)S(1)} %get-tuple-element.29.s.own, f32[17,272,128]{2,1,0:T(8,128)} %collective-permute-done.4.other, ...), custom_call_target="tpu_custom_call", output_to_operand_aliasing={{0}: (5, {})} | custom-call | tf_op jit(solution)/shard_map/gradient/pallas_call | solution.py:671
Async XLA Ops:
  0.6 9.0 %copy-start.2 = (f32[4,256,256]{2,1,0:T(8,128)S(1)}, f32[4,256,256]{2,1,0:T(8,128)}, u32[]{:S(2)}) copy-start(f32[4,256,256]{2,1,0:T(8,128)} %cx.5) | copy-start | bytes 3145732
  0.6 9.0 %copy-start.1 = (f32[4,256,256]{2,1,0:T(8,128)S(1)}, f32[4,256,256]{2,1,0:T(8,128)}, u32[]{:S(2)}) copy-start(f32[4,256,256]{2,1,0:T(8,128)} %t.5) | copy-start | bytes 3145732
  0.7 9.0 %copy-start = (f32[4,256,256]{2,1,0:T(8,128)S(1)}, f32[4,256,256]{2,1,0:T(8,128)}, u32[]{:S(2)}) copy-start(f32[4,256,256]{2,1,0:T(8,128)} %d.5) | copy-start | bytes 3145732
  0.7 9.0 %copy-start.3 = (f32[4,256,256]{2,1,0:T(8,128)S(1)}, f32[4,256,256]{2,1,0:T(8,128)}, u32[]{:S(2)}) copy-start(f32[4,256,256]{2,1,0:T(8,128)} %cy.3) | copy-start | bytes 3145732
  2.4 9.0 %collective-permute-start = (f32[64,256]{1,0:T(8,128)}, f32[64,256]{1,0:T(8,128)S(1)}, u32[]{:S(2)}, u32[]{:S(2)}) collective-permute-start(f32[64,256]{1,0:T(8,128)} %get-tuple-element.19), channel_id=1, source_target_pairs={{0,16},{16,32},{32,48},{48,64},{64,80},{80,96},{96,112},{112,0},{1... | collective-permute-start | bytes 196616 | tf_op jit(solution)/shard_map/ppermute | solution.py:693
  6.1 5.2 %collective-permute-start.1 = (f32[48,256]{1,0:T(8,128)}, f32[48,256]{1,0:T(8,128)S(1)}, u32[]{:S(2)}, u32[]{:S(2)}) collective-permute-start(f32[48,256]{1,0:T(8,128)} %get-tuple-element.20), channel_id=1, source_target_pairs={{0,112},{16,0},{32,16},{48,32},{64,48},{80,64},{96,80},{112,96},{1... | collective-permute-start | bytes 147464 | tf_op jit(solution)/shard_map/ppermute | solution.py:694
  12.3 5.2 %collective-permute-start.2 = (f32[112,128]{1,0:T(8,128)S(1)}, f32[112,128]{1,0:T(8,128)S(1)}, u32[]{:S(2)}, u32[]{:S(2)}) collective-permute-start(f32[112,128]{1,0:T(8,128)S(1)} %get-tuple-element.25), channel_id=1, source_target_pairs={{0,2},{2,4},{4,6},{6,8},{8,10},{10,12},{12,14},{14,0},{1,3},{3,5},... | collective-permute-start | bytes 172040 | tf_op jit(solution)/shard_map/ppermute | solution.py:697
  12.7 4.8 %collective-permute-start.3 = (f32[88,128]{1,0:T(8,128)S(1)}, f32[88,128]{1,0:T(8,128)S(1)}, u32[]{:S(2)}, u32[]{:S(2)}) collective-permute-start(f32[88,128]{1,0:T(8,128)S(1)} %get-tuple-element.26), channel_id=1, source_target_pairs={{0,14},{2,0},{4,2},{6,4},{8,6},{10,8},{12,10},{14,12},{1,15},{3,1}... | collective-permute-start | bytes 135176 | tf_op jit(solution)/shard_map/ppermute | solution.py:698
  17.6 3.7 %copy-start.4 = (s32[1,8]{1,0:T(1,128)S(1)}, s32[1,8]{1,0:T(1,128)}, u32[]{:S(2)}) copy-start(s32[1,8]{1,0:T(1,128)} %owner.3) | copy-start | bytes 100
  18.6 7.8 %collective-permute-start.4 = (f32[17,272,128]{2,1,0:T(8,128)S(1)}, f32[17,272,128]{2,1,0:T(8,128)}, u32[]{:S(2)}, u32[]{:S(2)}) collective-permute-start(f32[17,272,128]{2,1,0:T(8,128)S(1)} %get-tuple-element.29.s.own), channel_id=1, source_target_pairs={{0,1},{1,0},{2,3},{3,2},{4,5},{5,4},{6,7},{7,6},{8,9},{9,8},{10,11... | collective-permute-start | bytes 7102472 | tf_op jit(solution)/shard_map/ppermute | solution.py:701

commit v2 on v1

v2 whole, which is shorter than its diff:
```python
import jax
import jax.numpy as jnp
from jax import lax
from jax.experimental import pallas as pl
from jax.experimental.pallas import tpu as pltpu
from jax.sharding import PartitionSpec as P

CAP = 6
NP = 8
RIM = 8
LANES = 128
F32 = jnp.float32
MIB = 1024 * 1024


def ring(count, step):
    return [(i, (i + step) % count) for i in range(count)]


def coefficients(c):
    d = 1.0 - c
    m = c * d
    k_right = m * d
    k_left = m * c
    return k_right, k_left, c - k_right + k_left


def face_value(qm1, q0, q1, q2):
    return (7.0 / 12.0) * (q0 + q1) - (1.0 / 12.0) * (qm1 + q2)


def sweep_rows(load_q, load_c, store, a_scr, f_scr, base, count, chunk, fields=2):
    done = 0
    while done < count:
        n = min(chunk, count - done)
        r = base + done
        k_right, k_left, k_mid = coefficients(load_c(r, n))
        for f in range(fields):
            q0 = load_q(f, r, n)
            a = face_value(load_q(f, r - 1, n), q0, load_q(f, r + 1, n), load_q(f, r + 2, n))
            a_scr[f, pl.ds(8 + done, n), :] = a
            flux = k_right * a - k_left * a_scr[f, pl.ds(7 + done, n), :] + k_mid * q0
            f_scr[f, pl.ds(8 + done, n), :] = flux
            store(f, r, n, q0 - (flux - f_scr[f, pl.ds(7 + done, n), :]))
        done += n


def lane_iota(rows):
    return lax.broadcasted_iota(jnp.int32, (rows, LANES), 1)


def half(h, start=0):
    return slice(start + h * LANES, start + (h + 1) * LANES)


def call(
    kernel, out_shape, operands, name, spaces=None, scratch=(), aliases=None, cost=None, mib=20,
    out_spaces=None,
):
    vmem = pl.BlockSpec(memory_space=pltpu.VMEM)
    return pl.pallas_call(
        kernel,
        in_specs=[pl.BlockSpec(memory_space=x) for x in spaces] if spaces else [vmem] * len(operands),
        out_specs=tuple(pl.BlockSpec(memory_space=x) for x in out_spaces)
        if out_spaces
        else jax.tree.map(lambda _: vmem, out_shape),
        out_shape=tuple(
            x if space is pl.ANY else pltpu.VMEM(x.shape, F32)
            for x, space in zip(out_shape, out_spaces or [None] * len(out_shape))
        ),
        scratch_shapes=list(scratch),
        input_output_aliases=aliases or {},
        compiler_params=pltpu.CompilerParams(vmem_limit_bytes=mib * MIB),
        cost_estimate=cost,
        name=name,
    )(*operands)


def out(*shape):
    return jax.ShapeDtypeStruct(shape, F32)


SWEEP_COST = pl.CostEstimate(flops=20_000_000, bytes_accessed=6_000_000, transcendentals=0)


LAST = (5, 5, 3, 2)
FIRST = (4, 4, 2, 2)


def padded(rows):
    return -(-rows // 8) * 8


def place(counts, p, f):
    return p * sum(counts) + sum(counts[:f]), counts[f]


def edge_rows_kernel(d, t, cx, cy, lo, hi, first, last, sems):
    planes, rows, _ = d.shape
    copies = []
    for f, ref in enumerate((d, t, cx, cy)):
        copies.append(pltpu.make_async_copy(ref.at[:, 0:RIM, :], first.at[f], sems.at[f]))
        copies.append(
            pltpu.make_async_copy(ref.at[:, rows - RIM : rows, :], last.at[f], sems.at[4 + f])
        )
    for c in copies:
        c.start()
    for c in copies:
        c.wait()
    for p in range(planes):
        for f in range(4):
            at, n = place(FIRST, p, f)
            lo[at : at + n, :] = first[f, p, 0:n, :]
            at, n = place(LAST, p, f)
            hi[at : at + n, :] = last[f, p, RIM - n : RIM, :]


def edge_rows(fields):
    planes, _, cols = fields[0].shape
    tiles = pltpu.VMEM((4, planes, RIM, cols), F32)
    return call(
        edge_rows_kernel,
        (out(padded(planes * sum(FIRST)), cols), out(padded(planes * sum(LAST)), cols)),
        [pltpu.with_memory_space_constraint(x, pltpu.HBM) for x in fields],
        "edge_rows",
        spaces=[pl.ANY] * 4,
        scratch=[tiles, tiles, pltpu.SemaphoreType.DMA((8,))],
        mib=8,
    )


def inner_kernel(d, t, cx, cy, x_e, cy_e, s_t, s, win, xs, x_t, cy_t, a_scr, f_scr):
    planes, rows, _ = d.shape

    def body(p, _):
        for h in range(2):
            for f, ref in enumerate((d, t, cx)):
                win[f, 0:rows, :] = ref[p, :, half(h)]

            def store(f, r, n, value):
                xs[f, h, pl.ds(RIM + r, n), :] = value

            sweep_rows(
                lambda f, r, n: win[f, pl.ds(r, n), :],
                lambda r, n: win[2, pl.ds(r, n), :],
                store,
                a_scr,
                f_scr,
                1,
                rows,
                32,
            )
            for x in range(2):
                cy_t[x, half(h, RIM), :] = cy[p, half(x), half(h)].T
        for x in range(2):
            for f in range(2):
                for h in range(2):
                    x_t[f, x, half(h, RIM), :] = xs[f, h, half(x, RIM), :].T

            def store_t(f, r, n, value):
                s_t[p, f, x, pl.ds(r, n), :] = value

            sweep_rows(
                lambda f, r, n: x_t[f, x, pl.ds(r, n), :],
                lambda r, n: cy_t[x, pl.ds(r, n), :],
                store_t,
                a_scr,
                f_scr,
                RIM + 1,
                rows,
                32,
            )
            for f in range(2):
                for h in range(2):
                    s[(p * 2 + f) * 2 + h, half(x, RIM), :] = s_t[p, f, x, half(h, RIM), :].T
            for high, at in enumerate((slice(RIM, 16 + RIM), slice(rows + RIM - 16, rows + RIM))):
                cy_e[high, p, x] = cy_t[x, at, :]
                for f in range(2):
                    x_e[high, p, f, x] = x_t[f, x, at, :]
        return 0

    lax.fori_loop(0, planes, body, 0, unroll=False)


def inner(d, t, cx, cy):
    planes, rows, cols = d.shape
    ext = rows + 2 * RIM
    return call(
        inner_kernel,
        (
            out(2, planes, 2, 2, 16, LANES),
            out(2, planes, 2, 16, LANES),
            out(planes, 2, 2, ext, LANES),
            out(4 * planes, ext, LANES),
        ),
        (d, t, cx, cy),
        "inner",
        scratch=[pltpu.VMEM((3, ext, LANES), F32)]
        + [pltpu.VMEM((2, 2, ext, LANES), F32)] * 2
        + [pltpu.VMEM((2, ext, LANES), F32)]
        + [pltpu.VMEM((2, ext, LANES), F32)] * 2,
        cost=SWEEP_COST,
        mib=16,
    )


def edge_sweep(own, rim, high, win, a_scr, f_scr, res):
    lead, rim_at = (0, 16) if high else (8, 0)
    for f in range(3):
        win[f, lead : lead + 16, :] = own(f)
        beyond = rim(f)
        if beyond is not None:
            n = beyond.shape[0]
            at = rim_at if high else 8 - n
            win[f, at : at + n, :] = beyond

    def store(f, r, n, value):
        res[f, pl.ds(r, n), :] = value

    sweep_rows(
        lambda f, r, n: win[f, pl.ds(r, n), :],
        lambda r, n: win[2, pl.ds(r, n), :],
        store,
        a_scr,
        f_scr,
        6 if high else 4,
        16,
        16,
    )


EDGE_SCRATCH = [
    pltpu.VMEM((3, 32, LANES), F32),
    pltpu.VMEM((2, 32, LANES), F32),
    pltpu.VMEM((2, 32, LANES), F32),
    pltpu.VMEM((2, 32, LANES), F32),
]


STRIP = 16
EDGE = 5


def x_edge_kernel(
    d,
    t,
    cx,
    cy,
    left,
    right,
    x_e,
    cy_e,
    s_in,
    h_t,
    hc_t,
    to_l,
    to_r,
    s,
    q_rows,
    c_rows,
    win,
    a_scr,
    f_scr,
    res,
):
    del s_in, s
    planes, rows, _ = d.shape

    for p in range(planes):
        for h in range(2):
            for high in range(2):
                rim, counts = (right, FIRST) if high else (left, LAST)
                at = slice(rows - 16, rows) if high else slice(0, 16)

                def beyond(f):
                    r, n = place(counts, p, f)
                    return rim[r : r + n, half(h)]

                edge_sweep(
                    lambda f: (d, t, cx)[f][p, at, half(h)],
                    beyond,
                    high,
                    win,
                    a_scr,
                    f_scr,
                    res,
                )
                for f in range(2):
                    k = (f * 4 + p) * STRIP + EDGE * high
                    if high:
                        q_rows[h, k : k + EDGE, :] = res[f, 13:18, :]
                        c_rows[h, k : k + 3, :] = cy[p, rows - 3 : rows, half(h)]
                        c_rows[h, k + 3 : k + EDGE, :] = beyond(3)
                    else:
                        q_rows[h, k : k + EDGE, :] = res[f, 6:11, :]
                        c_rows[h, k : k + 2, :] = beyond(3)
                        c_rows[h, k + 2 : k + EDGE, :] = cy[p, 0:3, half(h)]
    for h in range(2):
        h_t[half(h, RIM), :] = q_rows[h].T
        hc_t[half(h, RIM), :] = c_rows[h].T
    for buf, counts in ((to_l, FIRST), (to_r, LAST)):

        last = counts is LAST

        def put(i, f, ref, start, stop):
            at, n = y_place(counts, i, f)
            top = stop - n if last else start
            buf[at : at + n, :] = ref[top : top + n, :]

        for p in range(planes):
            for x in range(2):
                for f in range(2):
                    put((p * 2 + f) * 2 + x, 0, x_e.at[int(last), p, f, x], 0, 16)
                put(p * 2 + x, 2, cy_e.at[int(last), p, x], 0, 16)
        put(16, 0, h_t, RIM, RIM + rows)
        put(8, 2, hc_t, RIM, RIM + rows)


def y_place(counts, i, f):
    return (17 * counts[0] if f == 2 else 0) + i * counts[f], counts[f]


def y_rim(counts):
    return out(padded(17 * counts[0] + 9 * counts[2]), LANES)


def x_edge(d, t, cx, cy, left, right, x_e, cy_e, s):
    ext = s.shape[1]
    return call(
        x_edge_kernel,
        (out(ext, LANES), out(ext, LANES), y_rim(FIRST), y_rim(LAST), out(*s.shape)),
        (d, t, cx, cy, left, right, x_e, cy_e, s),
        "x_edge",
        mib=12,
        scratch=[pltpu.VMEM((2, LANES, LANES), F32)] * 2 + EDGE_SCRATCH,
        spaces=[pltpu.VMEM] * 8 + [pl.ANY],
        out_spaces=[pltpu.VMEM] * 4 + [pl.ANY],
        aliases={8: 4},
    )


def slope(w1, w2):
    return (2.0 / 3.0) * w1 - (1.0 / 12.0) * w2


def rows_slope(ref, r, n):
    return slope(
        ref[pl.ds(r + 1, n), :] - ref[pl.ds(r - 1, n), :],
        ref[pl.ds(r + 2, n), :] - ref[pl.ds(r - 2, n), :],
    )


def inner_slopes_kernel(s_t, h_t, hc_t, sh_t, gy_out, gy, a_scr, f_scr, sems):
    planes, _, _, ext, _ = s_t.shape
    rows = ext - 2 * RIM

    def copy(p):
        at = pl.ds(p * 4, 4)
        return pltpu.make_async_copy(gy.at[at], gy_out.at[at], sems.at[p])

    def body(p, _):
        for f in range(2):
            for x in range(2):
                for h in range(2):
                    gy[(p * 2 + f) * 2 + h, half(x), :] = rows_slope(
                        s_t.at[p, f, x], RIM + h * LANES, LANES
                    ).T
        copy(p).start()
        return 0

    lax.fori_loop(0, planes, body, 0, unroll=False)

    def store(f, r, n, value):
        sh_t[pl.ds(r, n), :] = value

    sweep_rows(
        lambda f, r, n: h_t[pl.ds(r, n), :],
        lambda r, n: hc_t[pl.ds(r, n), :],
        store,
        a_scr,
        f_scr,
        RIM + 1,
        rows,
        32,
        fields=1,
    )
    for p in range(planes):
        copy(p).wait()


def inner_slopes(s_t, h_t, hc_t):
    planes, _, _, ext, _ = s_t.shape
    return call(
        inner_slopes_kernel,
        (out(ext, LANES), out(4 * planes, ext - 2 * RIM, LANES)),
        (s_t, h_t, hc_t),
        "inner_slopes",
        mib=8,
        scratch=[pltpu.VMEM((4 * planes, ext - 2 * RIM, LANES), F32)]
        + [pltpu.VMEM((2, ext, LANES), F32)] * 2
        + [pltpu.SemaphoreType.DMA((planes,))],
        out_spaces=[pltpu.VMEM, pl.ANY],
        cost=SWEEP_COST,
    )


VALUES_AT = 2
SLOPES_AT = 9


def y_edge_kernel(
    x_e,
    cy_e,
    h_t,
    hc_t,
    from_l,
    from_r,
    sh_in,
    gy_in,
    sh_t,
    edges,
    gy,
    strips,
    win,
    a_scr,
    f_scr,
    res,
):
    del gy_in, gy
    planes = x_e.shape[1]
    ext = h_t.shape[0]

    for high in range(2):
        rim, counts = (from_r, FIRST) if high else (from_l, LAST)
        at = slice(ext - 24, ext - 8) if high else slice(8, 24)

        def beyond(i, f):
            r, n = y_place(counts, i, f)
            return rim[r : r + n, :]

        for p in range(planes):
            for x in range(2):
                edge_sweep(
                    lambda f: cy_e[high, p, x] if f == 2 else x_e[high, p, f, x],
                    lambda f: beyond(p * 2 + x if f == 2 else (p * 2 + f) * 2 + x, f),
                    high,
                    win,
                    a_scr,
                    f_scr,
                    res,
                )
                for f in range(2):
                    k = (f * 4 + p) * STRIP
                    slopes = rows_slope(res.at[f], 8, 8)
                    if high:
                        strips[x, k : k + 2, :] = res[f, 14:16, :]
                        strips[x, k + 5 : k + 9, :] = slopes[4:8]
                    else:
                        strips[x, k + 2 : k + 5, :] = res[f, 8:11, :]
                        strips[x, k + 9 : k + 14, :] = slopes[0:5]
        edge_sweep(
            lambda f: hc_t[at, :] if f == 2 else h_t[at, :],
            lambda f: beyond(8, 2) if f == 2 else beyond(16, 0),
            high,
            win,
            a_scr,
            f_scr,
            res,
        )
        if high:
            sh_t[ext - 16 : ext, :] = res[0, 8:24, :]
        else:
            sh_t[0:16, :] = res[0, 0:16, :]
    for i in range(2):
        edges[i] = strips[i].T
        edges[2 + i] = sh_t[half(i, RIM), :].T
        edges[4 + i] = rows_slope(sh_t, RIM + i * LANES, LANES).T


def y_edge(x_e, cy_e, h_t, hc_t, from_l, from_r, sh_t, gy):
    return call(
        y_edge_kernel,
        (out(*sh_t.shape), out(6, LANES, LANES), out(*gy.shape)),
        (x_e, cy_e, h_t, hc_t, from_l, from_r, sh_t, gy),
        "y_edge",
        mib=8,
        scratch=[pltpu.VMEM((2, LANES, LANES), F32)] + EDGE_SCRATCH,
        spaces=[pltpu.VMEM] * 7 + [pl.ANY],
        out_spaces=[pltpu.VMEM] * 2 + [pl.ANY],
        aliases={6: 0, 7: 2},
    )[1:]


def finish_field(f, s_in, gy, edges, s, xy, adv=None, ready=None):
    planes, rows = xy.shape[2:4]
    n = 64
    lane = lane_iota(n)

    def body(p, _):
        if ready is not None:
            ready(p, f)
        strip = pl.multiple_of((f * 4 + p) * STRIP, STRIP)
        first = (p * 2 + f) * 2
        for r in range(0, rows, n):
            strips = edges[r // LANES, r % LANES : r % LANES + n, :]
            value = pltpu.roll(strips, LANES - VALUES_AT - strip, 1)
            y_slope = pltpu.roll(strips, LANES - SLOPES_AT - strip, 1)
            to = slice(RIM + r, RIM + r + n)
            for h in range(2):
                q = s_in[first + h, to, :]
                q = jnp.where(lane >= LANES - 2 if h else lane < 3, value, q)
                s[first + h, to, :] = q
                if adv is not None:
                    adv[f, p, r : r + n, half(h)] = q
                xy[1, f, p, r : r + n, half(h)] = jnp.where(
                    lane >= LANES - 4 if h else lane < 5, y_slope, gy[first + h, r : r + n, :]
                )
        for h in range(2):

            def outer(kind, at, count):
                return edges[kind * 2 + h, pl.ds(strip + at, count), :]

            s[first + h, RIM - 2 : RIM + 3, :] = outer(1, 0, EDGE)
            s[first + h, RIM + rows - 3 : RIM + rows + 2, :] = outer(1, EDGE, EDGE)
            for ref, kind in ((xy.at[1, f, p], 2), (None if adv is None else adv.at[f, p], 1)):
                if ref is not None:
                    ref[0:3, half(h)] = outer(kind, 2, 3)
                    ref[rows - 3 : rows, half(h)] = outer(kind, EDGE, 3)
            for r in range(0, rows, n):
                xy[0, f, p, r : r + n, half(h)] = rows_slope(s.at[first + h], RIM + r, n)
        return 0

    lax.fori_loop(0, planes, body, 0, unroll=False)


def piece_of(owner, core, slot):
    rank = jnp.int32(0)
    piece = jnp.int32(0)
    for j in range(NP):
        mine = owner[0, j] == core
        piece = jnp.where(jnp.logical_and(mine, rank == slot), j, piece)
        rank = rank + mine.astype(jnp.int32)
    return piece, slot < rank


def slope_copy(piece, used, src, zeros, to, sem):
    width = zeros.shape[1]

    @pl.when(used)
    def _():
        at = pl.ds(pl.multiple_of(piece * width, width), width)
        pltpu.make_async_copy(src.at[:, at, :], to, sem).start()

    @pl.when(jnp.logical_not(used))
    def _():
        pltpu.make_async_copy(zeros, to, sem).start()


def own_slopes_kernel(
    owner, core, s_in, gy_in, edges, adv, grad, s, xy, gy, buf, zeros, adv_sem, sems, in_sems
):
    planes = xy.shape[2]
    me = core[0]
    mine = pl.ds(pl.multiple_of(planes * me, planes), planes)

    def arrival(p, f):
        at = pl.ds((p * 2 + f) * 2, 2)
        return pltpu.make_async_copy(gy_in.at[at], gy.at[at], in_sems.at[f, p])

    for f in range(2):
        for p in range(planes):
            arrival(p, f).start()
    zeros[...] = jnp.zeros_like(zeros)
    pieces = [piece_of(owner, me, slot) for slot in range(CAP)]

    def adv_copy(f):
        return pltpu.make_async_copy(buf.at[f], adv.at[f], adv_sem.at[f])

    for f in range(2):
        finish_field(f, s_in, gy, edges, s, xy, buf, lambda p, f: arrival(p, f).wait())
        adv_copy(f).start()
        for slot in range(CAP):
            for k in range(2):
                slope_copy(
                    *pieces[slot], xy.at[k, f], zeros, grad.at[slot, f, k, mine], sems.at[slot, f, k]
                )
    for f in range(2):
        adv_copy(f).wait()
        for slot in range(CAP):
            for k in range(2):
                pltpu.make_async_copy(zeros, grad.at[slot, f, k, mine], sems.at[slot, f, k]).wait()


SMEM = pl.BlockSpec(memory_space=pltpu.SMEM)
VMEM = pl.BlockSpec(memory_space=pltpu.VMEM)
ANY = pl.BlockSpec(memory_space=pl.ANY)


def own_slopes(owner, core, s_in, gy, edges):
    planes = s_in.shape[0] // 4
    rows = gy.shape[1]
    cols = 2 * LANES
    width = rows // NP
    return pl.pallas_call(
        own_slopes_kernel,
        in_specs=[SMEM, SMEM, VMEM, ANY, VMEM],
        out_specs=(ANY, ANY, VMEM, VMEM),
        out_shape=(
            out(2, planes, rows, cols),
            out(CAP, 2, 3, 2 * planes, width, cols),
            pltpu.VMEM(s_in.shape, F32),
            pltpu.VMEM((2, 2, planes, rows, cols), F32),
        ),
        scratch_shapes=[
            pltpu.VMEM(gy.shape, F32),
            pltpu.VMEM((2, planes, rows, cols), F32),
            pltpu.VMEM((planes, width, cols), F32),
            pltpu.SemaphoreType.DMA((2,)),
            pltpu.SemaphoreType.DMA((CAP, 2, 2)),
            pltpu.SemaphoreType.DMA((2, planes)),
        ],
        compiler_params=pltpu.CompilerParams(vmem_limit_bytes=14 * MIB),
        cost_estimate=SWEEP_COST,
        name="own_slopes",
    )(owner, core, s_in, gy, edges)


def gradient_kernel(
    owner,
    core,
    own,
    own_xy,
    other_in,
    other_gy,
    other_edges,
    grad_in,
    grad,
    wedge,
    other,
    other_xy,
    other_y,
    part,
    wpart,
    zeros,
    xy_sems,
    sems,
    wsems,
    in_sems,
):
    planes = own_xy.shape[2]
    width = grad.shape[4]
    me = core[0]
    mine = pl.ds(pl.multiple_of(planes * me, planes), planes)
    theirs = pl.ds(pl.multiple_of(planes * (1 - me), planes), planes)

    def arrivals(p, f):
        at = pl.ds((p * 2 + f) * 2, 2)
        return (
            pltpu.make_async_copy(other_in.at[at], other.at[at], in_sems.at[0, f, p]),
            pltpu.make_async_copy(other_gy.at[at], other_y.at[at], in_sems.at[1, f, p]),
        )

    for f in range(2):
        for p in range(planes):
            for c in arrivals(p, f):
                c.start()

    def ready(p, f):
        for c in arrivals(p, f):
            c.wait()

    zeros[...] = jnp.zeros_like(zeros)
    pieces = [piece_of(owner, me, slot) for slot in range(CAP)]
    for f in range(2):
        finish_field(f, other, other_y, other_edges, other, other_xy, ready=ready)
        for slot in range(CAP):
            for k in range(2):
                slope_copy(
                    *pieces[slot],
                    other_xy.at[k, f],
                    zeros,
                    grad.at[slot, f, k, theirs],
                    xy_sems.at[slot, f, k],
                )

    def copies(slot, used=True):
        res = []
        for k, where in enumerate((mine, theirs)):
            for f in range(2):
                src = part.at[slot, f, k] if used else zeros
                res.append(
                    pltpu.make_async_copy(src, grad.at[slot, f, 2, where], sems.at[slot, f, k])
                )
            src = wpart.at[slot, k] if used else zeros
            res.append(pltpu.make_async_copy(src, wedge.at[slot, where], wsems.at[slot, k]))
        return res

    def fill(slot, piece):
        n = 8
        first = pl.multiple_of(piece * width, 8)

        def body(i, _):
            at = pl.multiple_of(first + i * n, n)
            r = pl.multiple_of(RIM + at, n)
            to = pl.ds(pl.multiple_of(i * n, n), n)
            for h in range(2):
                cols = half(h)

                def plane(z, f):
                    ref = own if z < planes else other
                    return ref[((z % planes) * 2 + f) * 2 + h, pl.ds(r, n), :]

                q = [[plane(z, f) for f in range(2)] for z in range(8)]
                for z in range(8):
                    g = []
                    p = z % planes
                    xy = own_xy if z < planes else other_xy
                    for f in range(2):
                        z_slope = slope(
                            q[(z + 1) % 8][f] - q[(z + 7) % 8][f],
                            q[(z + 2) % 8][f] - q[(z + 6) % 8][f],
                        )
                        part[slot, f, z // planes, p, to, cols] = z_slope
                        x_slope = xy[0, f, p, pl.ds(at, n), cols]
                        y_slope = xy[1, f, p, pl.ds(at, n), cols]
                        g.append((x_slope, y_slope, z_slope))
                    rx, ry, rz = g[0]
                    tx, ty, tz = g[1]
                    a = ry * tz - rz * ty
                    b = rz * tx - rx * tz
                    c = rx * ty - ry * tx
                    wpart[slot, z // planes, p, to, cols] = a * a + b * b + c * c
            return 0

        lax.fori_loop(0, width // n, body, 0, unroll=False)

    def slot_body(slot, _):
        piece, used = piece_of(owner, me, slot)

        @pl.when(used)
        def _():
            fill(slot, piece)
            for c in copies(slot):
                c.start()

        @pl.when(jnp.logical_not(used))
        def _():
            for c in copies(slot, False):
                c.start()

        return 0

    lax.fori_loop(0, CAP, slot_body, 0, unroll=False)

    def wait_body(slot, _):
        for f in range(2):
            for k in range(2):
                pltpu.make_async_copy(
                    zeros, grad.at[slot, f, k, theirs], xy_sems.at[slot, f, k]
                ).wait()
        for c in copies(slot):
            c.wait()
        return 0

    lax.fori_loop(0, CAP, wait_body, 0, unroll=False)


def gradients_of(owner, core, own, own_xy, other, other_gy, other_edges, grad):
    _, _, planes, rows, cols = own_xy.shape
    width = rows // NP
    return pl.pallas_call(
        gradient_kernel,
        in_specs=[SMEM, SMEM, VMEM, VMEM, ANY, ANY, VMEM, ANY],
        out_specs=(ANY, ANY),
        out_shape=(out(*grad.shape), out(CAP, 2 * planes, width, cols)),
        scratch_shapes=[
            pltpu.VMEM(own.shape, F32),
            pltpu.VMEM(own_xy.shape, F32),
            pltpu.VMEM(other_gy.shape, F32),
            pltpu.VMEM((CAP, 2, 2, planes, width, cols), F32),
            pltpu.VMEM((CAP, 2, planes, width, cols), F32),
            pltpu.VMEM((planes, width, cols), F32),
            pltpu.SemaphoreType.DMA((CAP, 2, 2)),
            pltpu.SemaphoreType.DMA((CAP, 2, 2)),
            pltpu.SemaphoreType.DMA((CAP, 2)),
            pltpu.SemaphoreType.DMA((2, 2, planes)),
        ],
        input_output_aliases={7: 0},
        compiler_params=pltpu.CompilerParams(vmem_limit_bytes=24 * MIB),
        name="gradient",
    )(owner, core, own, own_xy, other, other_gy, other_edges, grad)


def per_device(density, heat, cx, cy, owner):
    nx, ny = lax.axis_size("gx"), lax.axis_size("gy")
    lo, hi = edge_rows((density, heat, cx, cy))
    left = lax.ppermute(hi, "gx", ring(nx, 1))
    right = lax.ppermute(lo, "gx", ring(nx, -1))
    x_e, cy_e, s_t, swept = inner(density, heat, cx, cy)
    h_t, hc_t, to_l, to_r, swept = x_edge(density, heat, cx, cy, left, right, x_e, cy_e, swept)
    other = lax.ppermute(swept, "sa", ring(2, 1))
    from_l = lax.ppermute(to_r, "gy", ring(ny, 1))
    from_r = lax.ppermute(to_l, "gy", ring(ny, -1))
    sh_t, gy = inner_slopes(s_t, h_t, hc_t)
    edges, gy = y_edge(x_e, cy_e, h_t, hc_t, from_l, from_r, sh_t, gy)
    other_edges = lax.ppermute(edges, "sa", ring(2, 1))
    other_gy = lax.ppermute(gy, "sa", ring(2, 1))
    core = lax.axis_index("sa").astype(jnp.int32).reshape(1)
    advected, gradients, own, own_xy = own_slopes(owner, core, swept, gy, edges)
    gradients, wedge = gradients_of(
        owner, core, own, own_xy, other, other_gy, other_edges, gradients
    )
    return advected, gradients, wedge


def solution(mesh):
    block = P("sa", "gx", "gy")
    return jax.shard_map(
        per_device,
        mesh=mesh,
        in_specs=(block, block, block, block, P("gx", None)),
        out_specs=(
            P(None, "sa", "gx", "gy"),
            P(("gx", "sa"), None, None, None, None, "gy"),
            P(("gx", "sa"), None, None, "gy"),
        ),
        check_vma=False,
    )
```

time: 33.8 us -> 33.8 us (level)
    ppermute x1, starting transfers between devices: 2.72 us -> 1.03 us  [per_device(): other = lax.ppermute(swept, 'sa', ring(2, 1))]
    ppermute x0 -> x2, starting transfers between devices: none -> 1.5 us  [the longest x1 1.4 us: per_device(): other_gy = lax.ppermute(gy, 'sa', ring(2, 1))]
    pallas_call x5, Pallas kernels: 6.9 us -> 8.12 us  [call(): pl.pallas_call(kernel, in_specs=[pl.BlockSpec(memory_space=x) for x in sp...]
    pallas_call x2, Pallas kernels: 12.4 us -> 11.1 us  [the longest x1 6.23 us: gradients_of(): pl.pallas_call(gradient_kernel, in_specs=[SMEM, SMEM, VMEM, VMEM, ANY, AN...]
  transfers between devices with their start and end apart: 5 -> 7, of which waited for: 1 -> 2; matrix products, arithmetic and copies ran while one was open for 0% -> 0% of each run, Pallas kernels for 25% -> 34%
where the time goes in v2:
time: 33.8 us; the launch traced here: 33.7 us
  Pallas kernels  19.3 us (57%)
  starting transfers between devices  13.3 us (39%)
  between operations  0.74 us (2%)
    pallas_call x5, Pallas kernels, call(): pl.pallas_call(kernel, in_specs=[pl.BlockSpec(memory_space=x) for x in sp...  8.12 us
    pallas_call x1, Pallas kernels, gradients_of(): pl.pallas_call(gradient_kernel, in_specs=[SMEM, SMEM, VMEM, VMEM, ANY, AN...  6.23 us
    pallas_call x1, Pallas kernels, own_slopes(): pl.pallas_call(own_slopes_kernel, in_specs=[SMEM, SMEM, VMEM, ANY, VMEM],...  4.91 us
    ppermute x1, starting transfers between devices, per_device(): left = lax.ppermute(hi, 'gx', ring(nx, 1))  3.64 us
    ppermute x1, starting transfers between devices, per_device(): right = lax.ppermute(lo, 'gx', ring(nx, -1))  3.55 us
    ppermute x1, starting transfers between devices, per_device(): from_r = lax.ppermute(to_l, 'gy', ring(ny, -1))  3.26 us
    ppermute x1, starting transfers between devices, per_device(): other_gy = lax.ppermute(gy, 'sa', ring(2, 1))  1.4 us
    ppermute x1, starting transfers between devices, per_device(): other = lax.ppermute(swept, 'sa', ring(2, 1))  1.03 us
  transfers between devices with their start and end apart: 7, of which 2 were waited for; matrix products, arithmetic and copies ran while one was open for 0% of the time, Pallas kernels for 34%

profile of v2, /device:TPU:1, one launch (start us, length us, event | category | flops | bytes accessed | tf_op | source)
XLA Modules:
  0.0 33.7 jit_solution(4343939358434923416)
XLA Ops:
  0.6 0.0 copy-start.3
  0.6 0.0 copy-start.2
  0.7 0.0 copy-start.1
  0.7 0.0 copy-start
  0.7 1.1 %edge_rows.1 = (f32[48,256]{1,0:T(8,128)S(1)}, f32[64,256]{1,0:T(8,128)S(1)}) custom-call(f32[4,256,256]{2,1,0:T(8,128)} %d.5, f32[4,256,256]{2,1,0:T(8,128)} %t.5, f32[4,256,256]{2,1,0:T(8,128)} %cx.5, f32[4,256,256]{2,1,0:T(8,128)} %cy.5), custom_call_target="tpu_custom_call" | custom-call | tf_op jit(solution)/shard_map/edge_rows/pallas_call | solution.py:61
  1.8 3.6 %collective-permute-start = (f32[64,256]{1,0:T(8,128)S(1)}, f32[64,256]{1,0:T(8,128)S(1)}, u32[]{:S(2)}, u32[]{:S(2)}) collective-permute-start(f32[64,256]{1,0:T(8,128)S(1)} %get-tuple-element.24), channel_id=1, source_target_pairs={{0,16},{16,32},{32,48},{48,64},{64,80},{80,96},{96,112},{112,0},{1... | collective-permute-start | bytes 196616 | tf_op jit(solution)/shard_map/ppermute | solution.py:797
  5.4 3.6 %collective-permute-start.1 = (f32[48,256]{1,0:T(8,128)S(1)}, f32[48,256]{1,0:T(8,128)S(1)}, u32[]{:S(2)}, u32[]{:S(2)}) collective-permute-start(f32[48,256]{1,0:T(8,128)S(1)} %get-tuple-element.25), channel_id=1, source_target_pairs={{0,112},{16,0},{32,16},{48,32},{64,48},{80,64},{96,80},{112,96},{1... | collective-permute-start | bytes 147464 | tf_op jit(solution)/shard_map/ppermute | solution.py:798
  9.0 0.0 copy-done.3
  9.0 0.0 copy-done.2
  9.0 0.0 copy-done.1
  9.0 0.0 copy-done
  9.0 4.4 %inner.1 = (f32[2,4,2,2,16,128]{5,4,3,2,1,0:T(8,128)S(1)}, f32[2,4,2,16,128]{4,3,2,1,0:T(8,128)S(1)}, f32[4,2,2,272,128]{4,3,2,1,0:T(8,128)S(1)}, f32[16,272,128]{2,1,0:T(8,128)S(1)}) custom-call(f32[4,256,256]{2,1,0:T(8,128)S(1)} %copy-done, f32[4,256,256]{2,1,0:T(8,128)S(1)} %copy-done.1, f32[4,256,256]{2,1,0:T(8,128)S(1)} %copy-done.2, ...), custom_call_target="tpu_custom_call" | custom-call | flops 20000000 | bytes 6000000 | tf_op jit(solution)/shard_map/inner/pallas_call | solution.py:61
  13.4 0.0 collective-permute-done.1.right
  13.4 0.0 collective-permute-done.left
  13.5 0.4 %x_edge.1 = (f32[272,128]{1,0:T(8,128)S(1)}, f32[272,128]{1,0:T(8,128)S(1)}, f32[88,128]{1,0:T(8,128)S(1)}, f32[112,128]{1,0:T(8,128)S(1)}, f32[16,272,128]{2,1,0:T(8,128)S(1)}) custom-call(f32[4,256,256]{2,1,0:T(8,128)S(1)} %copy-done, f32[4,256,256]{2,1,0:T(8,128)S(1)} %copy-done.1, f32[4,256,256]{2,1,0:T(8,128)S(1)} %copy-done.2, ...), custom_call_target="tpu_custom_call", output_to_operand_aliasing={{4}: (8, {})} | custom-call | tf_op jit(solution)/shard_map/x_edge/pallas_call | solution.py:61
  13.9 1.0 %collective-permute-start.4 = (f32[16,272,128]{2,1,0:T(8,128)S(1)}, f32[16,272,128]{2,1,0:T(8,128)}, u32[]{:S(2)}, u32[]{:S(2)}) collective-permute-start(f32[16,272,128]{2,1,0:T(8,128)S(1)} %get-tuple-element.29.s_in), channel_id=1, source_target_pairs={{0,1},{1,0},{2,3},{3,2},{4,5},{5,4},{6,7},{7,6},{8,9},{9,8},{10,11... | collective-permute-start | bytes 6684680 | tf_op jit(solution)/shard_map/ppermute | solution.py:801
  14.9 0.3 collective-permute-start.2
  15.2 3.3 %collective-permute-start.3 = (f32[88,128]{1,0:T(8,128)S(1)}, f32[88,128]{1,0:T(8,128)S(1)}, u32[]{:S(2)}, u32[]{:S(2)}) collective-permute-start(f32[88,128]{1,0:T(8,128)S(1)} %get-tuple-element.33), channel_id=1, source_target_pairs={{0,14},{2,0},{4,2},{6,4},{8,6},{10,8},{12,10},{14,12},{1,15},{3,1}... | collective-permute-start | bytes 135176 | tf_op jit(solution)/shard_map/ppermute | solution.py:803
  18.5 0.0 copy-start.4
  18.5 1.7 %inner_slopes.1 = (f32[272,128]{1,0:T(8,128)S(1)}, f32[16,256,128]{2,1,0:T(8,128)}) custom-call(f32[4,2,2,272,128]{4,3,2,1,0:T(8,128)S(1)} %get-tuple-element.34.s_t, f32[272,128]{1,0:T(8,128)S(1)} %get-tuple-element.30.h_t, f32[272,128]{1,0:T(8,128)S(1)} %get-tuple-element.31.hc_t), custom_call_target="tpu_custom_call" | custom-call | flops 20000000 | bytes 6000000 | tf_op jit(solution)/shard_map/inner_slopes/pallas_call | solution.py:61
  20.2 0.2 collective-permute-done.3.from_r
  20.4 0.1 collective-permute-done.2.from_l
  20.5 0.5 %y_edge.1 = (f32[272,128]{1,0:T(8,128)S(1)}, f32[6,128,128]{2,1,0:T(8,128)S(1)}, f32[16,256,128]{2,1,0:T(8,128)}) custom-call(f32[2,4,2,2,16,128]{5,4,3,2,1,0:T(8,128)S(1)} %get-tuple-element.26.x_e, f32[2,4,2,16,128]{4,3,2,1,0:T(8,128)S(1)} %get-tuple-element.27.cy_e, ...), custom_call_target="tpu_custom_call", output_to_operand_aliasing={{0}: (6, {}), {2}: (7, {})} | custom-call | tf_op jit(solution)/shard_map/y_edge/pallas_call | solution.py:61
  21.0 1.4 %collective-permute-start.5 = (f32[16,256,128]{2,1,0:T(8,128)}, f32[16,256,128]{2,1,0:T(8,128)}, u32[]{:S(2)}, u32[]{:S(2)}) collective-permute-start(f32[16,256,128]{2,1,0:T(8,128)} %get-tuple-element.37.gy_in), channel_id=1, source_target_pairs={{0,1},{1,0},{2,3},{3,2},{4,5},{5,4},{6,7},{7,6},{8,9},{9,8},{10,11... | collective-permute-start | bytes 6291464 | tf_op jit(solution)/shard_map/ppermute | solution.py:807
  22.4 0.1 collective-permute-start.6
  22.5 0.0 copy-done.4
  22.5 4.9 %own_slopes.1 = (f32[2,4,256,256]{3,2,1,0:T(8,128)}, f32[6,2,3,8,32,256]{5,4,3,2,1,0:T(8,128)}, f32[16,272,128]{2,1,0:T(8,128)S(1)}, f32[2,2,4,256,256]{4,3,2,1,0:T(8,128)S(1)}) custom-call(s32[1,8]{1,0:T(1,128)S(1)} %copy-done.4, s32[1]{0:T(128)} %bitcast.core, f32[16,272,128]{2,1,0:T(8,128)S(1)} %get-tuple-element.29.s_in, ...), custom_call_target="tpu_custom_call" | custom-call | flops 20000000 | bytes 6000000 | tf_op jit(solution)/shard_map/own_slopes/pallas_call | solution.py:604
  27.4 0.0 collective-permute-done.6.other_edges
  27.4 0.0 collective-permute-done.5.other_gy
  27.4 0.0 collective-permute-done.4.other_in
  27.4 6.2 %gradient.1 = (f32[6,2,3,8,32,256]{5,4,3,2,1,0:T(8,128)}, f32[6,8,32,256]{3,2,1,0:T(8,128)}) custom-call(s32[1,8]{1,0:T(1,128)S(1)} %copy-done.4, s32[1]{0:T(128)} %bitcast.core, f32[16,272,128]{2,1,0:T(8,128)S(1)} %get-tuple-element.40.own, f32[2,2,4,256,256]{4,3,2,1,0:T(8,128)S(1)} %get-tuple-element.41.own_xy, ...), custom_call_target="tpu_custom_call", output_to_operand_aliasing={{0}: (7, {})} | custom-call | tf_op jit(solution)/shard_map/gradient/pallas_call | solution.py:771
Async XLA Ops:
  0.6 8.4 %copy-start.3 = (f32[4,256,256]{2,1,0:T(8,128)S(1)}, f32[4,256,256]{2,1,0:T(8,128)}, u32[]{:S(2)}) copy-start(f32[4,256,256]{2,1,0:T(8,128)} %cy.5) | copy-start | bytes 3145732
  0.6 8.4 %copy-start.2 = (f32[4,256,256]{2,1,0:T(8,128)S(1)}, f32[4,256,256]{2,1,0:T(8,128)}, u32[]{:S(2)}) copy-start(f32[4,256,256]{2,1,0:T(8,128)} %cx.5) | copy-start | bytes 3145732
  0.7 8.4 %copy-start.1 = (f32[4,256,256]{2,1,0:T(8,128)S(1)}, f32[4,256,256]{2,1,0:T(8,128)}, u32[]{:S(2)}) copy-start(f32[4,256,256]{2,1,0:T(8,128)} %t.5) | copy-start | bytes 3145732
  0.7 8.3 %copy-start = (f32[4,256,256]{2,1,0:T(8,128)S(1)}, f32[4,256,256]{2,1,0:T(8,128)}, u32[]{:S(2)}) copy-start(f32[4,256,256]{2,1,0:T(8,128)} %d.5) | copy-start | bytes 3145732
  1.8 11.6 %collective-permute-start = (f32[64,256]{1,0:T(8,128)S(1)}, f32[64,256]{1,0:T(8,128)S(1)}, u32[]{:S(2)}, u32[]{:S(2)}) collective-permute-start(f32[64,256]{1,0:T(8,128)S(1)} %get-tuple-element.24), channel_id=1, source_target_pairs={{0,16},{16,32},{32,48},{48,64},{64,80},{80,96},{96,112},{112,0},{1... | collective-permute-start | bytes 196616 | tf_op jit(solution)/shard_map/ppermute | solution.py:797
  5.4 8.0 %collective-permute-start.1 = (f32[48,256]{1,0:T(8,128)S(1)}, f32[48,256]{1,0:T(8,128)S(1)}, u32[]{:S(2)}, u32[]{:S(2)}) collective-permute-start(f32[48,256]{1,0:T(8,128)S(1)} %get-tuple-element.25), channel_id=1, source_target_pairs={{0,112},{16,0},{32,16},{48,32},{64,48},{80,64},{96,80},{112,96},{1... | collective-permute-start | bytes 147464 | tf_op jit(solution)/shard_map/ppermute | solution.py:798
  13.9 13.6 %collective-permute-start.4 = (f32[16,272,128]{2,1,0:T(8,128)S(1)}, f32[16,272,128]{2,1,0:T(8,128)}, u32[]{:S(2)}, u32[]{:S(2)}) collective-permute-start(f32[16,272,128]{2,1,0:T(8,128)S(1)} %get-tuple-element.29.s_in), channel_id=1, source_target_pairs={{0,1},{1,0},{2,3},{3,2},{4,5},{5,4},{6,7},{7,6},{8,9},{9,8},{10,11... | collective-permute-start | bytes 6684680 | tf_op jit(solution)/shard_map/ppermute | solution.py:801
  14.9 5.6 %collective-permute-start.2 = (f32[112,128]{1,0:T(8,128)S(1)}, f32[112,128]{1,0:T(8,128)S(1)}, u32[]{:S(2)}, u32[]{:S(2)}) collective-permute-start(f32[112,128]{1,0:T(8,128)S(1)} %get-tuple-element.32), channel_id=1, source_target_pairs={{0,2},{2,4},{4,6},{6,8},{8,10},{10,12},{12,14},{14,0},{1,3},{3,5},... | collective-permute-start | bytes 172040 | tf_op jit(solution)/shard_map/ppermute | solution.py:802
  15.2 5.1 %collective-permute-start.3 = (f32[88,128]{1,0:T(8,128)S(1)}, f32[88,128]{1,0:T(8,128)S(1)}, u32[]{:S(2)}, u32[]{:S(2)}) collective-permute-start(f32[88,128]{1,0:T(8,128)S(1)} %get-tuple-element.33), channel_id=1, source_target_pairs={{0,14},{2,0},{4,2},{6,4},{8,6},{10,8},{12,10},{14,12},{1,15},{3,1}... | collective-permute-start | bytes 135176 | tf_op jit(solution)/shard_map/ppermute | solution.py:803
  18.5 4.0 %copy-start.4 = (s32[1,8]{1,0:T(1,128)S(1)}, s32[1,8]{1,0:T(1,128)}, u32[]{:S(2)}) copy-start(s32[1,8]{1,0:T(1,128)} %owner.3) | copy-start | bytes 100
  21.0 6.4 %collective-permute-start.5 = (f32[16,256,128]{2,1,0:T(8,128)}, f32[16,256,128]{2,1,0:T(8,128)}, u32[]{:S(2)}, u32[]{:S(2)}) collective-permute-start(f32[16,256,128]{2,1,0:T(8,128)} %get-tuple-element.37.gy_in), channel_id=1, source_target_pairs={{0,1},{1,0},{2,3},{3,2},{4,5},{5,4},{6,7},{7,6},{8,9},{9,8},{10,11... | collective-permute-start | bytes 6291464 | tf_op jit(solution)/shard_map/ppermute | solution.py:807
  22.4 5.0 %collective-permute-start.6 = (f32[6,128,128]{2,1,0:T(8,128)S(1)}, f32[6,128,128]{2,1,0:T(8,128)S(1)}, u32[]{:S(2)}, u32[]{:S(2)}) collective-permute-start(f32[6,128,128]{2,1,0:T(8,128)S(1)} %get-tuple-element.38.edges), channel_id=1, source_target_pairs={{0,1},{1,0},{2,3},{3,2},{4,5},{5,4},{6,7},{7,6},{8,9},{9,8},{10,11... | collective-permute-start | bytes 1179656 | tf_op jit(solution)/shard_map/ppermute | solution.py:806

commit v3 on v2

--- a/solution.py
+++ b/solution.py
@@ -416,17 +416,14 @@
     from_l,
     from_r,
     sh_in,
-    gy_in,
     sh_t,
     edges,
-    gy,
     strips,
     win,
     a_scr,
     f_scr,
     res,
 ):
-    del gy_in, gy
     planes = x_e.shape[1]
     ext = h_t.shape[0]
 
@@ -477,24 +474,27 @@
         edges[4 + i] = rows_slope(sh_t, RIM + i * LANES, LANES).T
 
 
-def y_edge(x_e, cy_e, h_t, hc_t, from_l, from_r, sh_t, gy):
+def y_edge(x_e, cy_e, h_t, hc_t, from_l, from_r, sh_t):
     return call(
         y_edge_kernel,
-        (out(*sh_t.shape), out(6, LANES, LANES), out(*gy.shape)),
-        (x_e, cy_e, h_t, hc_t, from_l, from_r, sh_t, gy),
+        (out(*sh_t.shape), out(6, LANES, LANES)),
+        (x_e, cy_e, h_t, hc_t, from_l, from_r, sh_t),
         "y_edge",
         mib=8,
         scratch=[pltpu.VMEM((2, LANES, LANES), F32)] + EDGE_SCRATCH,
-        spaces=[pltpu.VMEM] * 7 + [pl.ANY],
-        out_spaces=[pltpu.VMEM] * 2 + [pl.ANY],
-        aliases={6: 0, 7: 2},
-    )[1:]
+        aliases={6: 0},
+    )[1]
 
 
 def finish_field(f, s_in, gy, edges, s, xy, adv=None, ready=None):
-    planes, rows = xy.shape[2:4]
-    n = 64
+    planes, width = xy.shape[3:5]
+    rows = NP * width
+    n = 2 * width
     lane = lane_iota(n)
+
+    def put(dim, p, r, h, value):
+        for i in range(n // width):
+            xy[f, r // width + i, dim, p, :, half(h)] = value[i * width : (i + 1) * width]
 
     def body(p, _):
         if ready is not None:
@@ -512,9 +512,8 @@
                 s[first + h, to, :] = q
                 if adv is not None:
                     adv[f, p, r : r + n, half(h)] = q
-                xy[1, f, p, r : r + n, half(h)] = jnp.where(
-                    lane >= LANES - 4 if h else lane < 5, y_slope, gy[first + h, r : r + n, :]
-                )
+                y = gy[first + h, r : r + n, :]
+                put(1, p, r, h, jnp.where(lane >= LANES - 4 if h else lane < 5, y_slope, y))
         for h in range(2):
 
             def outer(kind, at, count):
@@ -522,12 +521,13 @@
 
             s[first + h, RIM - 2 : RIM + 3, :] = outer(1, 0, EDGE)
             s[first + h, RIM + rows - 3 : RIM + rows + 2, :] = outer(1, EDGE, EDGE)
-            for ref, kind in ((xy.at[1, f, p], 2), (None if adv is None else adv.at[f, p], 1)):
-                if ref is not None:
-                    ref[0:3, half(h)] = outer(kind, 2, 3)
-                    ref[rows - 3 : rows, half(h)] = outer(kind, EDGE, 3)
+            if adv is not None:
+                adv[f, p, 0:3, half(h)] = outer(1, 2, 3)
+                adv[f, p, rows - 3 : rows, half(h)] = outer(1, EDGE, 3)
+            xy[f, 0, 1, p, 0:3, half(h)] = outer(2, 2, 3)
+            xy[f, NP - 1, 1, p, width - 3 : width, half(h)] = outer(2, EDGE, 3)
             for r in range(0, rows, n):
-                xy[0, f, p, r : r + n, half(h)] = rows_slope(s.at[first + h], RIM + r, n)
+                put(0, p, r, h, rows_slope(s.at[first + h], RIM + r, n))
         return 0
 
     lax.fori_loop(0, planes, body, 0, unroll=False)
@@ -543,13 +543,17 @@
     return piece, slot < rank
 
 
-def slope_copy(piece, used, src, zeros, to, sem):
-    width = zeros.shape[1]
-
+def clear(used, *refs):
+    @pl.when(jnp.logical_not(used))
+    def _():
+        for ref in refs:
+            ref[...] = jnp.zeros_like(ref)
+
+
+def start_copy(used, src, zeros, to, sem):
     @pl.when(used)
     def _():
-        at = pl.ds(pl.multiple_of(piece * width, width), width)
-        pltpu.make_async_copy(src.at[:, at, :], to, sem).start()
+        pltpu.make_async_copy(src, to, sem).start()
 
     @pl.when(jnp.logical_not(used))
     def _():
@@ -559,7 +563,7 @@
 def own_slopes_kernel(
     owner, core, s_in, gy_in, edges, adv, grad, s, xy, gy, buf, zeros, adv_sem, sems, in_sems
 ):
-    planes = xy.shape[2]
+    planes = xy.shape[3]
     me = core[0]
     mine = pl.ds(pl.multiple_of(planes * me, planes), planes)
 
@@ -570,8 +574,8 @@
     for f in range(2):
         for p in range(planes):
             arrival(p, f).start()
-    zeros[...] = jnp.zeros_like(zeros)
     pieces = [piece_of(owner, me, slot) for slot in range(CAP)]
+    clear(pieces[-1][1], zeros)
 
     def adv_copy(f):
         return pltpu.make_async_copy(buf.at[f], adv.at[f], adv_sem.at[f])
@@ -579,16 +583,13 @@
     for f in range(2):
         finish_field(f, s_in, gy, edges, s, xy, buf, lambda p, f: arrival(p, f).wait())
         adv_copy(f).start()
-        for slot in range(CAP):
-            for k in range(2):
-                slope_copy(
-                    *pieces[slot], xy.at[k, f], zeros, grad.at[slot, f, k, mine], sems.at[slot, f, k]
-                )
+        if f == 0:
+            for slot, (piece, used) in enumerate(pieces):
+                start_copy(used, xy.at[0, piece], zeros, grad.at[slot, 0, 0:2, mine], sems.at[slot])
     for f in range(2):
         adv_copy(f).wait()
-        for slot in range(CAP):
-            for k in range(2):
-                pltpu.make_async_copy(zeros, grad.at[slot, f, k, mine], sems.at[slot, f, k]).wait()
+    for slot in range(CAP):
+        pltpu.make_async_copy(zeros, grad.at[slot, 0, 0:2, mine], sems.at[slot]).wait()
 
 
 SMEM = pl.BlockSpec(memory_space=pltpu.SMEM)
@@ -609,14 +610,14 @@
             out(2, planes, rows, cols),
             out(CAP, 2, 3, 2 * planes, width, cols),
             pltpu.VMEM(s_in.shape, F32),
-            pltpu.VMEM((2, 2, planes, rows, cols), F32),
+            pltpu.VMEM((2, NP, 2, planes, width, cols), F32),
         ),
         scratch_shapes=[
             pltpu.VMEM(gy.shape, F32),
             pltpu.VMEM((2, planes, rows, cols), F32),
-            pltpu.VMEM((planes, width, cols), F32),
+            pltpu.VMEM((2, planes, width, cols), F32),
             pltpu.SemaphoreType.DMA((2,)),
-            pltpu.SemaphoreType.DMA((CAP, 2, 2)),
+            pltpu.SemaphoreType.DMA((CAP,)),
             pltpu.SemaphoreType.DMA((2, planes)),
         ],
         compiler_params=pltpu.CompilerParams(vmem_limit_bytes=14 * MIB),
@@ -642,13 +643,13 @@
     part,
     wpart,
     zeros,
+    xy_zeros,
+    in_sems,
+    own_sems,
     xy_sems,
     sems,
-    wsems,
-    in_sems,
 ):
-    planes = own_xy.shape[2]
-    width = grad.shape[4]
+    planes, width = own_xy.shape[3:5]
     me = core[0]
     mine = pl.ds(pl.multiple_of(planes * me, planes), planes)
     theirs = pl.ds(pl.multiple_of(planes * (1 - me), planes), planes)
@@ -660,76 +661,67 @@
             pltpu.make_async_copy(other_gy.at[at], other_y.at[at], in_sems.at[1, f, p]),
         )
 
+    def ready(p, f):
+        for c in arrivals(p, f):
+            c.wait()
+
     for f in range(2):
         for p in range(planes):
             for c in arrivals(p, f):
                 c.start()
-
-    def ready(p, f):
-        for c in arrivals(p, f):
-            c.wait()
-
-    zeros[...] = jnp.zeros_like(zeros)
     pieces = [piece_of(owner, me, slot) for slot in range(CAP)]
+    clear(pieces[-1][1], zeros, xy_zeros)
+    for slot, (piece, used) in enumerate(pieces):
+        start_copy(
+            used, own_xy.at[1, piece], xy_zeros, grad.at[slot, 1, 0:2, mine], own_sems.at[slot]
+        )
     for f in range(2):
         finish_field(f, other, other_y, other_edges, other, other_xy, ready=ready)
-        for slot in range(CAP):
-            for k in range(2):
-                slope_copy(
-                    *pieces[slot],
-                    other_xy.at[k, f],
-                    zeros,
-                    grad.at[slot, f, k, theirs],
-                    xy_sems.at[slot, f, k],
-                )
-
-    def copies(slot, used=True):
-        res = []
-        for k, where in enumerate((mine, theirs)):
-            for f in range(2):
-                src = part.at[slot, f, k] if used else zeros
-                res.append(
-                    pltpu.make_async_copy(src, grad.at[slot, f, 2, where], sems.at[slot, f, k])
-                )
-            src = wpart.at[slot, k] if used else zeros
-            res.append(pltpu.make_async_copy(src, wedge.at[slot, where], wsems.at[slot, k]))
-        return res
+        for slot, (piece, used) in enumerate(pieces):
+            start_copy(
+                used,
+                other_xy.at[f, piece],
+                xy_zeros,
+                grad.at[slot, f, 0:2, theirs],
+                xy_sems.at[slot, f],
+            )
+
+    def targets(slot):
+        return grad.at[slot, 0, 2], grad.at[slot, 1, 2], wedge.at[slot]
 
     def fill(slot, piece):
         n = 8
         first = pl.multiple_of(piece * width, 8)
 
         def body(i, _):
-            at = pl.multiple_of(first + i * n, n)
-            r = pl.multiple_of(RIM + at, n)
+            r = pl.ds(pl.multiple_of(RIM + first + i * n, n), n)
             to = pl.ds(pl.multiple_of(i * n, n), n)
             for h in range(2):
                 cols = half(h)
 
                 def plane(z, f):
                     ref = own if z < planes else other
-                    return ref[((z % planes) * 2 + f) * 2 + h, pl.ds(r, n), :]
+                    return ref[((z % planes) * 2 + f) * 2 + h, r, :]
 
                 q = [[plane(z, f) for f in range(2)] for z in range(8)]
                 for z in range(8):
                     g = []
                     p = z % planes
+                    zo = lax.rem(z + planes * me, 2 * planes)
                     xy = own_xy if z < planes else other_xy
                     for f in range(2):
                         z_slope = slope(
                             q[(z + 1) % 8][f] - q[(z + 7) % 8][f],
                             q[(z + 2) % 8][f] - q[(z + 6) % 8][f],
                         )
-                        part[slot, f, z // planes, p, to, cols] = z_slope
-                        x_slope = xy[0, f, p, pl.ds(at, n), cols]
-                        y_slope = xy[1, f, p, pl.ds(at, n), cols]
-                        g.append((x_slope, y_slope, z_slope))
+                        part[slot, f, zo, to, cols] = z_slope
+                        g.append((xy[f, piece, 0, p, to, cols], xy[f, piece, 1, p, to, cols], z_slope))
                     rx, ry, rz = g[0]
                     tx, ty, tz = g[1]
                     a = ry * tz - rz * ty
                     b = rz * tx - rx * tz
                     c = rx * ty - ry * tx
-                    wpart[slot, z // planes, p, to, cols] = a * a + b * b + c * c
+                    wpart[slot, zo, to, cols] = a * a + b * b + c * c
             return 0
 
         lax.fori_loop(0, width // n, body, 0, unroll=False)
@@ -740,34 +732,29 @@
         @pl.when(used)
         def _():
             fill(slot, piece)
-            for c in copies(slot):
-                c.start()
-
-        @pl.when(jnp.logical_not(used))
-        def _():
-            for c in copies(slot, False):
-                c.start()
-
+
+        sources = part.at[slot, 0], part.at[slot, 1], wpart.at[slot]
+        for k, (src, to) in enumerate(zip(sources, targets(slot))):
+            start_copy(used, src, zeros, to, sems.at[slot, k])
         return 0
 
     lax.fori_loop(0, CAP, slot_body, 0, unroll=False)
 
     def wait_body(slot, _):
+        pltpu.make_async_copy(xy_zeros, grad.at[slot, 1, 0:2, mine], own_sems.at[slot]).wait()
         for f in range(2):
-            for k in range(2):
-                pltpu.make_async_copy(
-                    zeros, grad.at[slot, f, k, theirs], xy_sems.at[slot, f, k]
-                ).wait()
-        for c in copies(slot):
-            c.wait()
+            pltpu.make_async_copy(
+                xy_zeros, grad.at[slot, f, 0:2, theirs], xy_sems.at[slot, f]
+            ).wait()
+        for k, to in enumerate(targets(slot)):
+            pltpu.make_async_copy(zeros, to, sems.at[slot, k]).wait()
         return 0
 
     lax.fori_loop(0, CAP, wait_body, 0, unroll=False)
 
 
 def gradients_of(owner, core, own, own_xy, other, other_gy, other_edges, grad):
-    _, _, planes, rows, cols = own_xy.shape
-    width = rows // NP
+    planes, width, cols = own_xy.shape[3:]
     return pl.pallas_call(
         gradient_kernel,
         in_specs=[SMEM, SMEM, VMEM, VMEM, ANY, ANY, VMEM, ANY],
@@ -777,13 +764,14 @@
             pltpu.VMEM(own.shape, F32),
             pltpu.VMEM(own_xy.shape, F32),
             pltpu.VMEM(other_gy.shape, F32),
-            pltpu.VMEM((CAP, 2, 2, planes, width, cols), F32),
-            pltpu.VMEM((CAP, 2, planes, width, cols), F32),
-            pltpu.VMEM((planes, width, cols), F32),
-            pltpu.SemaphoreType.DMA((CAP, 2, 2)),
-            pltpu.SemaphoreType.DMA((CAP, 2, 2)),
+            pltpu.VMEM((CAP, 2, 2 * planes, width, cols), F32),
+            pltpu.VMEM((CAP, 2 * planes, width, cols), F32),
+            pltpu.VMEM((2 * planes, width, cols), F32),
+            pltpu.VMEM((2, planes, width, cols), F32),
+            pltpu.SemaphoreType.DMA((2, 2, planes)),
+            pltpu.SemaphoreType.DMA((CAP,)),
             pltpu.SemaphoreType.DMA((CAP, 2)),
-            pltpu.SemaphoreType.DMA((2, 2, planes)),
+            pltpu.SemaphoreType.DMA((CAP, 3)),
         ],
         input_output_aliases={7: 0},
         compiler_params=pltpu.CompilerParams(vmem_limit_bytes=24 * MIB),
@@ -802,9 +790,10 @@
     from_l = lax.ppermute(to_r, "gy", ring(ny, 1))
     from_r = lax.ppermute(to_l, "gy", ring(ny, -1))
     sh_t, gy = inner_slopes(s_t, h_t, hc_t)
-    edges, gy = y_edge(x_e, cy_e, h_t, hc_t, from_l, from_r, sh_t, gy)
+    gy, from_l, from_r = lax.optimization_barrier((gy, from_l, from_r))
+    other_gy = lax.ppermute(gy, "sa", ring(2, 1))
+    edges = y_edge(x_e, cy_e, h_t, hc_t, from_l, from_r, sh_t)
     other_edges = lax.ppermute(edges, "sa", ring(2, 1))
-    other_gy = lax.ppermute(gy, "sa", ring(2, 1))
     core = lax.axis_index("sa").astype(jnp.int32).reshape(1)
     advected, gradients, own, own_xy = own_slopes(owner, core, swept, gy, edges)
     gradients, wedge = gradients_of(

time: 33.8 us -> 33.3 us (0.985)
  Pallas kernels: 19.3 us -> 18.9 us
    pallas_call x1, Pallas kernels: 4.91 us -> 4.24 us  [own_slopes(): pl.pallas_call(own_slopes_kernel, in_specs=[SMEM, SMEM, VMEM, ANY, VMEM],...]
  transfers between devices with their start and end apart: 7 -> 7, of which waited for: 2 -> 2; matrix products, arithmetic and copies ran while one was open for 0% -> 0% of each run, Pallas kernels for 34% -> 33%
where the time goes in v3:
time: 33.3 us; the launch traced here: 33.2 us
  Pallas kernels  18.9 us (57%)
  starting transfers between devices  13.2 us (40%)
  between operations  0.77 us (2%)
    pallas_call x5, Pallas kernels, call(): pl.pallas_call(kernel, in_specs=[pl.BlockSpec(memory_space=x) for x in sp...  8.12 us
    pallas_call x1, Pallas kernels, gradients_of(): pl.pallas_call(gradient_kernel, in_specs=[SMEM, SMEM, VMEM, VMEM, ANY, AN...  6.5 us
    pallas_call x1, Pallas kernels, own_slopes(): pl.pallas_call(own_slopes_kernel, in_specs=[SMEM, SMEM, VMEM, ANY, VMEM],...  4.24 us
    ppermute x1, starting transfers between devices, per_device(): left = lax.ppermute(hi, 'gx', ring(nx, 1))  3.64 us
    ppermute x1, starting transfers between devices, per_device(): right = lax.ppermute(lo, 'gx', ring(nx, -1))  3.55 us
    ppermute x1, starting transfers between devices, per_device(): from_r = lax.ppermute(to_l, 'gy', ring(ny, -1))  3.26 us
    ppermute x1, starting transfers between devices, per_device(): other_gy = lax.ppermute(gy, 'sa', ring(2, 1))  1.32 us
    ppermute x1, starting transfers between devices, per_device(): other = lax.ppermute(swept, 'sa', ring(2, 1))  1.03 us
  transfers between devices with their start and end apart: 7, of which 2 were waited for; matrix products, arithmetic and copies ran while one was open for 0% of the time, Pallas kernels for 33%

profile of v3, /device:TPU:1, one launch (start us, length us, event | category | flops | bytes accessed | tf_op | source)
XLA Modules:
  0.0 33.2 jit_solution(16385828475674141304)
XLA Ops:
  0.6 0.0 copy-start.3
  0.6 0.0 copy-start.2
  0.7 0.0 copy-start.1
  0.7 0.0 copy-start
  0.7 1.1 %edge_rows.1 = (f32[48,256]{1,0:T(8,128)S(1)}, f32[64,256]{1,0:T(8,128)S(1)}) custom-call(f32[4,256,256]{2,1,0:T(8,128)} %d.5, f32[4,256,256]{2,1,0:T(8,128)} %t.5, f32[4,256,256]{2,1,0:T(8,128)} %cx.5, f32[4,256,256]{2,1,0:T(8,128)} %cy.5), custom_call_target="tpu_custom_call" | custom-call | tf_op jit(solution)/shard_map/edge_rows/pallas_call | solution.py:61
  1.8 3.6 %collective-permute-start = (f32[64,256]{1,0:T(8,128)S(1)}, f32[64,256]{1,0:T(8,128)S(1)}, u32[]{:S(2)}, u32[]{:S(2)}) collective-permute-start(f32[64,256]{1,0:T(8,128)S(1)} %get-tuple-element.26), channel_id=1, source_target_pairs={{0,16},{16,32},{32,48},{48,64},{64,80},{80,96},{96,112},{112,0},{1... | collective-permute-start | bytes 196616 | tf_op jit(solution)/shard_map/ppermute | solution.py:785
  5.4 3.6 %collective-permute-start.1 = (f32[48,256]{1,0:T(8,128)S(1)}, f32[48,256]{1,0:T(8,128)S(1)}, u32[]{:S(2)}, u32[]{:S(2)}) collective-permute-start(f32[48,256]{1,0:T(8,128)S(1)} %get-tuple-element.27), channel_id=1, source_target_pairs={{0,112},{16,0},{32,16},{48,32},{64,48},{80,64},{96,80},{112,96},{1... | collective-permute-start | bytes 147464 | tf_op jit(solution)/shard_map/ppermute | solution.py:786
  9.0 0.0 copy-done.3
  9.0 0.0 copy-done.2
  9.0 0.0 copy-done.1
  9.0 0.0 copy-done
  9.0 4.4 %inner.1 = (f32[2,4,2,2,16,128]{5,4,3,2,1,0:T(8,128)S(1)}, f32[2,4,2,16,128]{4,3,2,1,0:T(8,128)S(1)}, f32[4,2,2,272,128]{4,3,2,1,0:T(8,128)S(1)}, f32[16,272,128]{2,1,0:T(8,128)S(1)}) custom-call(f32[4,256,256]{2,1,0:T(8,128)S(1)} %copy-done, f32[4,256,256]{2,1,0:T(8,128)S(1)} %copy-done.1, f32[4,256,256]{2,1,0:T(8,128)S(1)} %copy-done.2, ...), custom_call_target="tpu_custom_call" | custom-call | flops 20000000 | bytes 6000000 | tf_op jit(solution)/shard_map/inner/pallas_call | solution.py:61
  13.4 0.0 collective-permute-done.1.right
  13.4 0.0 collective-permute-done.left
  13.5 0.4 %x_edge.1 = (f32[272,128]{1,0:T(8,128)S(1)}, f32[272,128]{1,0:T(8,128)S(1)}, f32[88,128]{1,0:T(8,128)S(1)}, f32[112,128]{1,0:T(8,128)S(1)}, f32[16,272,128]{2,1,0:T(8,128)S(1)}) custom-call(f32[4,256,256]{2,1,0:T(8,128)S(1)} %copy-done, f32[4,256,256]{2,1,0:T(8,128)S(1)} %copy-done.1, f32[4,256,256]{2,1,0:T(8,128)S(1)} %copy-done.2, ...), custom_call_target="tpu_custom_call", output_to_operand_aliasing={{4}: (8, {})} | custom-call | tf_op jit(solution)/shard_map/x_edge/pallas_call | solution.py:61
  13.9 0.0 copy-start.4
  13.9 1.0 %collective-permute-start.4 = (f32[16,272,128]{2,1,0:T(8,128)S(1)}, f32[16,272,128]{2,1,0:T(8,128)}, u32[]{:S(2)}, u32[]{:S(2)}) collective-permute-start(f32[16,272,128]{2,1,0:T(8,128)S(1)} %get-tuple-element.31.s_in), channel_id=1, source_target_pairs={{0,1},{1,0},{2,3},{3,2},{4,5},{5,4},{6,7},{7,6},{8,9},{9,8},{10,11... | collective-permute-start | bytes 6684680 | tf_op jit(solution)/shard_map/ppermute | solution.py:789
  14.9 0.3 collective-permute-start.2
  15.2 3.3 %collective-permute-start.3 = (f32[88,128]{1,0:T(8,128)S(1)}, f32[88,128]{1,0:T(8,128)S(1)}, u32[]{:S(2)}, u32[]{:S(2)}) collective-permute-start(f32[88,128]{1,0:T(8,128)S(1)} %get-tuple-element.37), channel_id=1, source_target_pairs={{0,14},{2,0},{4,2},{6,4},{8,6},{10,8},{12,10},{14,12},{1,15},{3,1}... | collective-permute-start | bytes 135176 | tf_op jit(solution)/shard_map/ppermute | solution.py:791
  18.5 1.7 %inner_slopes.1 = (f32[272,128]{1,0:T(8,128)S(1)}, f32[16,256,128]{2,1,0:T(8,128)}) custom-call(f32[4,2,2,272,128]{4,3,2,1,0:T(8,128)S(1)} %get-tuple-element.32.s_t, f32[272,128]{1,0:T(8,128)S(1)} %get-tuple-element.33.h_t, f32[272,128]{1,0:T(8,128)S(1)} %get-tuple-element.34.hc_t), custom_call_target="tpu_custom_call" | custom-call | flops 20000000 | bytes 6000000 | tf_op jit(solution)/shard_map/inner_slopes/pallas_call | solution.py:61
  20.2 0.2 collective-permute-done.3.from_r
  20.4 0.1 collective-permute-done.2.from_l
  20.5 1.3 %collective-permute-start.5 = (f32[16,256,128]{2,1,0:T(8,128)}, f32[16,256,128]{2,1,0:T(8,128)}, u32[]{:S(2)}, u32[]{:S(2)}) collective-permute-start(f32[16,256,128]{2,1,0:T(8,128)} %get-tuple-element.38.gy_in), channel_id=1, source_target_pairs={{0,1},{1,0},{2,3},{3,2},{4,5},{5,4},{6,7},{7,6},{8,9},{9,8},{10,11... | collective-permute-start | bytes 6291464 | tf_op jit(solution)/shard_map/ppermute | solution.py:794
  21.8 0.5 %y_edge.1 = (f32[272,128]{1,0:T(8,128)S(1)}, f32[6,128,128]{2,1,0:T(8,128)S(1)}) custom-call(f32[2,4,2,2,16,128]{5,4,3,2,1,0:T(8,128)S(1)} %get-tuple-element.28.x_e, f32[2,4,2,16,128]{4,3,2,1,0:T(8,128)S(1)} %get-tuple-element.29.cy_e, f32[272,128]{1,0:T(8,128)S(1)} %get-tuple-element.33.h_t, ...), custom_call_target="tpu_custom_call", output_to_operand_aliasing={{0}: (6, {})} | custom-call | tf_op jit(solution)/shard_map/y_edge/pallas_call | solution.py:61
  22.3 0.1 collective-permute-start.6
  22.4 0.0 copy-done.4
  22.4 4.2 %own_slopes.1 = (f32[2,4,256,256]{3,2,1,0:T(8,128)}, f32[6,2,3,8,32,256]{5,4,3,2,1,0:T(8,128)}, f32[16,272,128]{2,1,0:T(8,128)S(1)}, f32[2,8,2,4,32,256]{5,4,3,2,1,0:T(8,128)S(1)}) custom-call(s32[1,8]{1,0:T(1,128)S(1)} %copy-done.4, s32[1]{0:T(128)} %bitcast.core, f32[16,272,128]{2,1,0:T(8,128)S(1)} %get-tuple-element.31.s_in, ...), custom_call_target="tpu_custom_call" | custom-call | flops 20000000 | bytes 6000000 | tf_op jit(solution)/shard_map/own_slopes/pallas_call | solution.py:605
  26.7 0.0 collective-permute-done.6.other_edges
  26.7 0.0 collective-permute-done.5.other_gy
  26.7 0.0 collective-permute-done.4.other_in
  26.7 6.5 %gradient.1 = (f32[6,2,3,8,32,256]{5,4,3,2,1,0:T(8,128)}, f32[6,8,32,256]{3,2,1,0:T(8,128)}) custom-call(s32[1,8]{1,0:T(1,128)S(1)} %copy-done.4, s32[1]{0:T(128)} %bitcast.core, f32[16,272,128]{2,1,0:T(8,128)S(1)} %get-tuple-element.44.own, f32[2,8,2,4,32,256]{5,4,3,2,1,0:T(8,128)S(1)} %get-tuple-element.45.own_xy, ...), custom_call_target="tpu_custom_call", output_to_operand_aliasing={{0}: (7, {})} | custom-call | tf_op jit(solution)/shard_map/gradient/pallas_call | solution.py:758
Async XLA Ops:
  0.6 8.4 %copy-start.3 = (f32[4,256,256]{2,1,0:T(8,128)S(1)}, f32[4,256,256]{2,1,0:T(8,128)}, u32[]{:S(2)}) copy-start(f32[4,256,256]{2,1,0:T(8,128)} %cy.5) | copy-start | bytes 3145732
  0.6 8.4 %copy-start.2 = (f32[4,256,256]{2,1,0:T(8,128)S(1)}, f32[4,256,256]{2,1,0:T(8,128)}, u32[]{:S(2)}) copy-start(f32[4,256,256]{2,1,0:T(8,128)} %cx.5) | copy-start | bytes 3145732
  0.7 8.4 %copy-start.1 = (f32[4,256,256]{2,1,0:T(8,128)S(1)}, f32[4,256,256]{2,1,0:T(8,128)}, u32[]{:S(2)}) copy-start(f32[4,256,256]{2,1,0:T(8,128)} %t.5) | copy-start | bytes 3145732
  0.7 8.3 %copy-start = (f32[4,256,256]{2,1,0:T(8,128)S(1)}, f32[4,256,256]{2,1,0:T(8,128)}, u32[]{:S(2)}) copy-start(f32[4,256,256]{2,1,0:T(8,128)} %d.5) | copy-start | bytes 3145732
  1.8 11.6 %collective-permute-start = (f32[64,256]{1,0:T(8,128)S(1)}, f32[64,256]{1,0:T(8,128)S(1)}, u32[]{:S(2)}, u32[]{:S(2)}) collective-permute-start(f32[64,256]{1,0:T(8,128)S(1)} %get-tuple-element.26), channel_id=1, source_target_pairs={{0,16},{16,32},{32,48},{48,64},{64,80},{80,96},{96,112},{112,0},{1... | collective-permute-start | bytes 196616 | tf_op jit(solution)/shard_map/ppermute | solution.py:785
  5.4 8.0 %collective-permute-start.1 = (f32[48,256]{1,0:T(8,128)S(1)}, f32[48,256]{1,0:T(8,128)S(1)}, u32[]{:S(2)}, u32[]{:S(2)}) collective-permute-start(f32[48,256]{1,0:T(8,128)S(1)} %get-tuple-element.27), channel_id=1, source_target_pairs={{0,112},{16,0},{32,16},{48,32},{64,48},{80,64},{96,80},{112,96},{1... | collective-permute-start | bytes 147464 | tf_op jit(solution)/shard_map/ppermute | solution.py:786
  13.9 8.6 %copy-start.4 = (s32[1,8]{1,0:T(1,128)S(1)}, s32[1,8]{1,0:T(1,128)}, u32[]{:S(2)}) copy-start(s32[1,8]{1,0:T(1,128)} %owner.3) | copy-start | bytes 100
  13.9 12.8 %collective-permute-start.4 = (f32[16,272,128]{2,1,0:T(8,128)S(1)}, f32[16,272,128]{2,1,0:T(8,128)}, u32[]{:S(2)}, u32[]{:S(2)}) collective-permute-start(f32[16,272,128]{2,1,0:T(8,128)S(1)} %get-tuple-element.31.s_in), channel_id=1, source_target_pairs={{0,1},{1,0},{2,3},{3,2},{4,5},{5,4},{6,7},{7,6},{8,9},{9,8},{10,11... | collective-permute-start | bytes 6684680 | tf_op jit(solution)/shard_map/ppermute | solution.py:789
  14.9 5.6 %collective-permute-start.2 = (f32[112,128]{1,0:T(8,128)S(1)}, f32[112,128]{1,0:T(8,128)S(1)}, u32[]{:S(2)}, u32[]{:S(2)}) collective-permute-start(f32[112,128]{1,0:T(8,128)S(1)} %get-tuple-element.36), channel_id=1, source_target_pairs={{0,2},{2,4},{4,6},{6,8},{8,10},{10,12},{12,14},{14,0},{1,3},{3,5},... | collective-permute-start | bytes 172040 | tf_op jit(solution)/shard_map/ppermute | solution.py:790
  15.2 5.1 %collective-permute-start.3 = (f32[88,128]{1,0:T(8,128)S(1)}, f32[88,128]{1,0:T(8,128)S(1)}, u32[]{:S(2)}, u32[]{:S(2)}) collective-permute-start(f32[88,128]{1,0:T(8,128)S(1)} %get-tuple-element.37), channel_id=1, source_target_pairs={{0,14},{2,0},{4,2},{6,4},{8,6},{10,8},{12,10},{14,12},{1,15},{3,1}... | collective-permute-start | bytes 135176 | tf_op jit(solution)/shard_map/ppermute | solution.py:791
  20.5 6.2 %collective-permute-start.5 = (f32[16,256,128]{2,1,0:T(8,128)}, f32[16,256,128]{2,1,0:T(8,128)}, u32[]{:S(2)}, u32[]{:S(2)}) collective-permute-start(f32[16,256,128]{2,1,0:T(8,128)} %get-tuple-element.38.gy_in), channel_id=1, source_target_pairs={{0,1},{1,0},{2,3},{3,2},{4,5},{5,4},{6,7},{7,6},{8,9},{9,8},{10,11... | collective-permute-start | bytes 6291464 | tf_op jit(solution)/shard_map/ppermute | solution.py:794
  22.3 4.4 %collective-permute-start.6 = (f32[6,128,128]{2,1,0:T(8,128)S(1)}, f32[6,128,128]{2,1,0:T(8,128)S(1)}, u32[]{:S(2)}, u32[]{:S(2)}) collective-permute-start(f32[6,128,128]{2,1,0:T(8,128)S(1)} %get-tuple-element.42.edges), channel_id=1, source_target_pairs={{0,1},{1,0},{2,3},{3,2},{4,5},{5,4},{6,7},{7,6},{8,9},{9,8},{10,11... | collective-permute-start | bytes 1179656 | tf_op jit(solution)/shard_map/ppermute | solution.py:796

commit v4 on v3

--- a/solution.py
+++ b/solution.py
@@ -561,7 +561,24 @@
 
 
 def own_slopes_kernel(
-    owner, core, s_in, gy_in, edges, adv, grad, s, xy, gy, buf, zeros, adv_sem, sems, in_sems
+    owner,
+    core,
+    s_in,
+    gy_in,
+    edges,
+    other_in,
+    adv,
+    grad,
+    s,
+    xy,
+    other,
+    gy,
+    buf,
+    zeros,
+    adv_sem,
+    sems,
+    in_sems,
+    other_sem,
 ):
     planes = xy.shape[3]
     me = core[0]
@@ -574,6 +591,8 @@
     for f in range(2):
         for p in range(planes):
             arrival(p, f).start()
+    bring = pltpu.make_async_copy(other_in, other, other_sem)
+    bring.start()
     pieces = [piece_of(owner, me, slot) for slot in range(CAP)]
     clear(pieces[-1][1], zeros)
 
@@ -583,13 +602,13 @@
     for f in range(2):
         finish_field(f, s_in, gy, edges, s, xy, buf, lambda p, f: arrival(p, f).wait())
         adv_copy(f).start()
-        if f == 0:
-            for slot, (piece, used) in enumerate(pieces):
-                start_copy(used, xy.at[0, piece], zeros, grad.at[slot, 0, 0:2, mine], sems.at[slot])
+        for slot, (piece, used) in enumerate(pieces):
+            start_copy(used, xy.at[f, piece], zeros, grad.at[slot, f, 0:2, mine], sems.at[slot, f])
+    bring.wait()
     for f in range(2):
         adv_copy(f).wait()
-    for slot in range(CAP):
-        pltpu.make_async_copy(zeros, grad.at[slot, 0, 0:2, mine], sems.at[slot]).wait()
+        for slot in range(CAP):
+            pltpu.make_async_copy(zeros, grad.at[slot, f, 0:2, mine], sems.at[slot, f]).wait()
 
 
 SMEM = pl.BlockSpec(memory_space=pltpu.SMEM)
@@ -597,33 +616,36 @@
 ANY = pl.BlockSpec(memory_space=pl.ANY)
 
 
-def own_slopes(owner, core, s_in, gy, edges):
+def own_slopes(owner, core, s_in, gy, edges, other):
     planes = s_in.shape[0] // 4
     rows = gy.shape[1]
     cols = 2 * LANES
     width = rows // NP
     return pl.pallas_call(
         own_slopes_kernel,
-        in_specs=[SMEM, SMEM, VMEM, ANY, VMEM],
-        out_specs=(ANY, ANY, VMEM, VMEM),
+        in_specs=[SMEM, SMEM, VMEM, ANY, VMEM, ANY],
+        out_specs=(ANY, ANY, VMEM, VMEM, VMEM),
+        input_output_aliases={2: 2},
         out_shape=(
             out(2, planes, rows, cols),
             out(CAP, 2, 3, 2 * planes, width, cols),
             pltpu.VMEM(s_in.shape, F32),
             pltpu.VMEM((2, NP, 2, planes, width, cols), F32),
+            pltpu.VMEM(other.shape, F32),
         ),
         scratch_shapes=[
             pltpu.VMEM(gy.shape, F32),
             pltpu.VMEM((2, planes, rows, cols), F32),
             pltpu.VMEM((2, planes, width, cols), F32),
             pltpu.SemaphoreType.DMA((2,)),
-            pltpu.SemaphoreType.DMA((CAP,)),
+            pltpu.SemaphoreType.DMA((CAP, 2)),
             pltpu.SemaphoreType.DMA((2, planes)),
+            pltpu.SemaphoreType.DMA,
         ],
         compiler_params=pltpu.CompilerParams(vmem_limit_bytes=14 * MIB),
         cost_estimate=SWEEP_COST,
         name="own_slopes",
-    )(owner, core, s_in, gy, edges)
+    )(owner, core, s_in, gy, edges, other)
 
 
 def gradient_kernel(
@@ -645,7 +667,6 @@
     zeros,
     xy_zeros,
     in_sems,
-    own_sems,
     xy_sems,
     sems,
 ):
@@ -654,29 +675,20 @@
     mine = pl.ds(pl.multiple_of(planes * me, planes), planes)
     theirs = pl.ds(pl.multiple_of(planes * (1 - me), planes), planes)
 
-    def arrivals(p, f):
+    def arrival(p, f):
         at = pl.ds((p * 2 + f) * 2, 2)
-        return (
-            pltpu.make_async_copy(other_in.at[at], other.at[at], in_sems.at[0, f, p]),
-            pltpu.make_async_copy(other_gy.at[at], other_y.at[at], in_sems.at[1, f, p]),
-        )
+        return pltpu.make_async_copy(other_gy.at[at], other_y.at[at], in_sems.at[f, p])
 
     def ready(p, f):
-        for c in arrivals(p, f):
-            c.wait()
+        arrival(p, f).wait()
 
     for f in range(2):
         for p in range(planes):
-            for c in arrivals(p, f):
-                c.start()
+            arrival(p, f).start()
     pieces = [piece_of(owner, me, slot) for slot in range(CAP)]
     clear(pieces[-1][1], zeros, xy_zeros)
-    for slot, (piece, used) in enumerate(pieces):
-        start_copy(
-            used, own_xy.at[1, piece], xy_zeros, grad.at[slot, 1, 0:2, mine], own_sems.at[slot]
-        )
     for f in range(2):
-        finish_field(f, other, other_y, other_edges, other, other_xy, ready=ready)
+        finish_field(f, other_in, other_y, other_edges, other, other_xy, ready=ready)
         for slot, (piece, used) in enumerate(pieces):
             start_copy(
                 used,
@@ -741,7 +753,6 @@
     lax.fori_loop(0, CAP, slot_body, 0, unroll=False)
 
     def wait_body(slot, _):
-        pltpu.make_async_copy(xy_zeros, grad.at[slot, 1, 0:2, mine], own_sems.at[slot]).wait()
         for f in range(2):
             pltpu.make_async_copy(
                 xy_zeros, grad.at[slot, f, 0:2, theirs], xy_sems.at[slot, f]
@@ -757,7 +768,7 @@
     planes, width, cols = own_xy.shape[3:]
     return pl.pallas_call(
         gradient_kernel,
-        in_specs=[SMEM, SMEM, VMEM, VMEM, ANY, ANY, VMEM, ANY],
+        in_specs=[SMEM, SMEM, VMEM, VMEM, VMEM, ANY, VMEM, ANY],
         out_specs=(ANY, ANY),
         out_shape=(out(*grad.shape), out(CAP, 2 * planes, width, cols)),
         scratch_shapes=[
@@ -768,8 +779,7 @@
             pltpu.VMEM((CAP, 2 * planes, width, cols), F32),
             pltpu.VMEM((2 * planes, width, cols), F32),
             pltpu.VMEM((2, planes, width, cols), F32),
-            pltpu.SemaphoreType.DMA((2, 2, planes)),
-            pltpu.SemaphoreType.DMA((CAP,)),
+            pltpu.SemaphoreType.DMA((2, planes)),
             pltpu.SemaphoreType.DMA((CAP, 2)),
             pltpu.SemaphoreType.DMA((CAP, 3)),
         ],
@@ -795,7 +805,7 @@
     edges = y_edge(x_e, cy_e, h_t, hc_t, from_l, from_r, sh_t)
     other_edges = lax.ppermute(edges, "sa", ring(2, 1))
     core = lax.axis_index("sa").astype(jnp.int32).reshape(1)
-    advected, gradients, own, own_xy = own_slopes(owner, core, swept, gy, edges)
+    advected, gradients, own, own_xy, other = own_slopes(owner, core, swept, gy, edges, other)
     gradients, wedge = gradients_of(
         owner, core, own, own_xy, other, other_gy, other_edges, gradients
     )

time: 33.3 us -> 33.1 us (level)
  transfers between devices with their start and end apart: 7 -> 7, of which waited for: 2 -> 2; matrix products, arithmetic and copies ran while one was open for 0% -> 0% of each run, Pallas kernels for 33% -> 34%
where the time goes in v4:
time: 33.1 us; the launch traced here: 33 us
  Pallas kernels  18.6 us (56%)
  starting transfers between devices  13.2 us (40%)
  between operations  0.77 us (2%)
  waiting for transfers between devices  0.36 us (1%)
    pallas_call x5, Pallas kernels, call(): pl.pallas_call(kernel, in_specs=[pl.BlockSpec(memory_space=x) for x in sp...  8.09 us
    pallas_call x1, Pallas kernels, gradients_of(): pl.pallas_call(gradient_kernel, in_specs=[SMEM, SMEM, VMEM, VMEM, VMEM, A...  5.73 us
    pallas_call x1, Pallas kernels, own_slopes(): pl.pallas_call(own_slopes_kernel, in_specs=[SMEM, SMEM, VMEM, ANY, VMEM,...  4.78 us
    ppermute x1, starting transfers between devices, per_device(): left = lax.ppermute(hi, 'gx', ring(nx, 1))  3.64 us
    ppermute x1, starting transfers between devices, per_device(): right = lax.ppermute(lo, 'gx', ring(nx, -1))  3.55 us
    ppermute x1, starting transfers between devices, per_device(): from_r = lax.ppermute(to_l, 'gy', ring(ny, -1))  3.26 us
    ppermute x1, starting transfers between devices, per_device(): other_gy = lax.ppermute(gy, 'sa', ring(2, 1))  1.32 us
    ppermute x1, starting transfers between devices, per_device(): other = lax.ppermute(swept, 'sa', ring(2, 1))  1.03 us
  transfers between devices with their start and end apart: 7, of which 2 were waited for; matrix products, arithmetic and copies ran while one was open for 0% of the time, Pallas kernels for 34%

profile of v4, /device:TPU:1, one launch (start us, length us, event | category | flops | bytes accessed | tf_op | source)
XLA Modules:
  0.0 33.0 jit_solution(503796765316993477)
XLA Ops:
  0.6 0.0 copy-start.3
  0.6 0.0 copy-start.2
  0.7 0.0 copy-start.1
  0.7 0.0 copy-start
  0.7 1.1 %edge_rows.1 = (f32[48,256]{1,0:T(8,128)S(1)}, f32[64,256]{1,0:T(8,128)S(1)}) custom-call(f32[4,256,256]{2,1,0:T(8,128)} %d.5, f32[4,256,256]{2,1,0:T(8,128)} %t.5, f32[4,256,256]{2,1,0:T(8,128)} %cx.5, f32[4,256,256]{2,1,0:T(8,128)} %cy.5), custom_call_target="tpu_custom_call" | custom-call | tf_op jit(solution)/shard_map/edge_rows/pallas_call | solution.py:61
  1.8 3.6 %collective-permute-start = (f32[64,256]{1,0:T(8,128)S(1)}, f32[64,256]{1,0:T(8,128)S(1)}, u32[]{:S(2)}, u32[]{:S(2)}) collective-permute-start(f32[64,256]{1,0:T(8,128)S(1)} %get-tuple-element.27), channel_id=1, source_target_pairs={{0,16},{16,32},{32,48},{48,64},{64,80},{80,96},{96,112},{112,0},{1... | collective-permute-start | bytes 196616 | tf_op jit(solution)/shard_map/ppermute | solution.py:795
  5.4 3.6 %collective-permute-start.1 = (f32[48,256]{1,0:T(8,128)S(1)}, f32[48,256]{1,0:T(8,128)S(1)}, u32[]{:S(2)}, u32[]{:S(2)}) collective-permute-start(f32[48,256]{1,0:T(8,128)S(1)} %get-tuple-element.28), channel_id=1, source_target_pairs={{0,112},{16,0},{32,16},{48,32},{64,48},{80,64},{96,80},{112,96},{1... | collective-permute-start | bytes 147464 | tf_op jit(solution)/shard_map/ppermute | solution.py:796
  9.0 0.0 copy-done.3
  9.0 0.0 copy-done.2
  9.0 0.0 copy-done.1
  9.0 0.0 copy-done
  9.0 4.4 %inner.1 = (f32[2,4,2,2,16,128]{5,4,3,2,1,0:T(8,128)S(1)}, f32[2,4,2,16,128]{4,3,2,1,0:T(8,128)S(1)}, f32[4,2,2,272,128]{4,3,2,1,0:T(8,128)S(1)}, f32[16,272,128]{2,1,0:T(8,128)S(1)}) custom-call(f32[4,256,256]{2,1,0:T(8,128)S(1)} %copy-done, f32[4,256,256]{2,1,0:T(8,128)S(1)} %copy-done.1, f32[4,256,256]{2,1,0:T(8,128)S(1)} %copy-done.2, ...), custom_call_target="tpu_custom_call" | custom-call | flops 20000000 | bytes 6000000 | tf_op jit(solution)/shard_map/inner/pallas_call | solution.py:61
  13.4 0.0 collective-permute-done.1.right
  13.4 0.0 collective-permute-done.left
  13.5 0.4 %x_edge.1 = (f32[272,128]{1,0:T(8,128)S(1)}, f32[272,128]{1,0:T(8,128)S(1)}, f32[88,128]{1,0:T(8,128)S(1)}, f32[112,128]{1,0:T(8,128)S(1)}, f32[16,272,128]{2,1,0:T(8,128)S(1)}) custom-call(f32[4,256,256]{2,1,0:T(8,128)S(1)} %copy-done, f32[4,256,256]{2,1,0:T(8,128)S(1)} %copy-done.1, f32[4,256,256]{2,1,0:T(8,128)S(1)} %copy-done.2, ...), custom_call_target="tpu_custom_call", output_to_operand_aliasing={{4}: (8, {})} | custom-call | tf_op jit(solution)/shard_map/x_edge/pallas_call | solution.py:61
  13.9 0.0 copy-start.4
  13.9 1.0 %collective-permute-start.4 = (f32[16,272,128]{2,1,0:T(8,128)S(1)}, f32[16,272,128]{2,1,0:T(8,128)}, u32[]{:S(2)}, u32[]{:S(2)}) collective-permute-start(f32[16,272,128]{2,1,0:T(8,128)S(1)} %get-tuple-element.32.s_in), channel_id=1, source_target_pairs={{0,1},{1,0},{2,3},{3,2},{4,5},{5,4},{6,7},{7,6},{8,9},{9,8},{10,11... | collective-permute-start | bytes 6684680 | tf_op jit(solution)/shard_map/ppermute | solution.py:799
  14.9 0.3 collective-permute-start.2
  15.2 3.3 %collective-permute-start.3 = (f32[88,128]{1,0:T(8,128)S(1)}, f32[88,128]{1,0:T(8,128)S(1)}, u32[]{:S(2)}, u32[]{:S(2)}) collective-permute-start(f32[88,128]{1,0:T(8,128)S(1)} %get-tuple-element.38), channel_id=1, source_target_pairs={{0,14},{2,0},{4,2},{6,4},{8,6},{10,8},{12,10},{14,12},{1,15},{3,1}... | collective-permute-start | bytes 135176 | tf_op jit(solution)/shard_map/ppermute | solution.py:801
  18.5 1.7 %inner_slopes.1 = (f32[272,128]{1,0:T(8,128)S(1)}, f32[16,256,128]{2,1,0:T(8,128)}) custom-call(f32[4,2,2,272,128]{4,3,2,1,0:T(8,128)S(1)} %get-tuple-element.33.s_t, f32[272,128]{1,0:T(8,128)S(1)} %get-tuple-element.34.h_t, f32[272,128]{1,0:T(8,128)S(1)} %get-tuple-element.35.hc_t), custom_call_target="tpu_custom_call" | custom-call | flops 20000000 | bytes 6000000 | tf_op jit(solution)/shard_map/inner_slopes/pallas_call | solution.py:61
  20.2 0.2 collective-permute-done.3.from_r
  20.4 0.1 collective-permute-done.2.from_l
  20.5 1.3 %collective-permute-start.5 = (f32[16,256,128]{2,1,0:T(8,128)}, f32[16,256,128]{2,1,0:T(8,128)}, u32[]{:S(2)}, u32[]{:S(2)}) collective-permute-start(f32[16,256,128]{2,1,0:T(8,128)} %get-tuple-element.39.gy_in), channel_id=1, source_target_pairs={{0,1},{1,0},{2,3},{3,2},{4,5},{5,4},{6,7},{7,6},{8,9},{9,8},{10,11... | collective-permute-start | bytes 6291464 | tf_op jit(solution)/shard_map/ppermute | solution.py:804
  21.8 0.5 %y_edge.1 = (f32[272,128]{1,0:T(8,128)S(1)}, f32[6,128,128]{2,1,0:T(8,128)S(1)}) custom-call(f32[2,4,2,2,16,128]{5,4,3,2,1,0:T(8,128)S(1)} %get-tuple-element.29.x_e, f32[2,4,2,16,128]{4,3,2,1,0:T(8,128)S(1)} %get-tuple-element.30.cy_e, f32[272,128]{1,0:T(8,128)S(1)} %get-tuple-element.34.h_t, ...), custom_call_target="tpu_custom_call", output_to_operand_aliasing={{0}: (6, {})} | custom-call | tf_op jit(solution)/shard_map/y_edge/pallas_call | solution.py:61
  22.3 0.1 collective-permute-start.6
  22.4 0.0 collective-permute-done.4.other_in
  22.4 0.0 copy-done.4
  22.4 4.8 %own_slopes.1 = (f32[2,4,256,256]{3,2,1,0:T(8,128)}, f32[6,2,3,8,32,256]{5,4,3,2,1,0:T(8,128)}, f32[16,272,128]{2,1,0:T(8,128)S(1)}, f32[2,8,2,4,32,256]{5,4,3,2,1,0:T(8,128)S(1)}, f32[16,272,128]{2,1,0:T(8,128)S(1)}) custom-call(s32[1,8]{1,0:T(1,128)S(1)} %copy-done.4, s32[1]{0:T(128)} %bitcast.core, ...), custom_call_target="tpu_custom_call", output_to_operand_aliasing={{2}: (2, {})} | custom-call | flops 20000000 | bytes 6000000 | tf_op jit(solution)/shard_map/own_slopes/pallas_call | solution.py:624
  27.2 0.0 collective-permute-done.6.other_edges
  27.2 0.0 collective-permute-done.5.other_gy
  27.2 5.7 %gradient.1 = (f32[6,2,3,8,32,256]{5,4,3,2,1,0:T(8,128)}, f32[6,8,32,256]{3,2,1,0:T(8,128)}) custom-call(s32[1,8]{1,0:T(1,128)S(1)} %copy-done.4, s32[1]{0:T(128)} %bitcast.core, f32[16,272,128]{2,1,0:T(8,128)S(1)} %get-tuple-element.45.own, f32[2,8,2,4,32,256]{5,4,3,2,1,0:T(8,128)S(1)} %get-tuple-element.46.own_xy, ...), custom_call_target="tpu_custom_call", output_to_operand_aliasing={{0}: (7, {})} | custom-call | tf_op jit(solution)/shard_map/gradient/pallas_call | solution.py:769
Async XLA Ops:
  0.6 8.4 %copy-start.3 = (f32[4,256,256]{2,1,0:T(8,128)S(1)}, f32[4,256,256]{2,1,0:T(8,128)}, u32[]{:S(2)}) copy-start(f32[4,256,256]{2,1,0:T(8,128)} %cy.5) | copy-start | bytes 3145732
  0.6 8.4 %copy-start.2 = (f32[4,256,256]{2,1,0:T(8,128)S(1)}, f32[4,256,256]{2,1,0:T(8,128)}, u32[]{:S(2)}) copy-start(f32[4,256,256]{2,1,0:T(8,128)} %cx.5) | copy-start | bytes 3145732
  0.7 8.4 %copy-start.1 = (f32[4,256,256]{2,1,0:T(8,128)S(1)}, f32[4,256,256]{2,1,0:T(8,128)}, u32[]{:S(2)}) copy-start(f32[4,256,256]{2,1,0:T(8,128)} %t.5) | copy-start | bytes 3145732
  0.7 8.3 %copy-start = (f32[4,256,256]{2,1,0:T(8,128)S(1)}, f32[4,256,256]{2,1,0:T(8,128)}, u32[]{:S(2)}) copy-start(f32[4,256,256]{2,1,0:T(8,128)} %d.5) | copy-start | bytes 3145732
  1.8 11.6 %collective-permute-start = (f32[64,256]{1,0:T(8,128)S(1)}, f32[64,256]{1,0:T(8,128)S(1)}, u32[]{:S(2)}, u32[]{:S(2)}) collective-permute-start(f32[64,256]{1,0:T(8,128)S(1)} %get-tuple-element.27), channel_id=1, source_target_pairs={{0,16},{16,32},{32,48},{48,64},{64,80},{80,96},{96,112},{112,0},{1... | collective-permute-start | bytes 196616 | tf_op jit(solution)/shard_map/ppermute | solution.py:795
  5.4 8.0 %collective-permute-start.1 = (f32[48,256]{1,0:T(8,128)S(1)}, f32[48,256]{1,0:T(8,128)S(1)}, u32[]{:S(2)}, u32[]{:S(2)}) collective-permute-start(f32[48,256]{1,0:T(8,128)S(1)} %get-tuple-element.28), channel_id=1, source_target_pairs={{0,112},{16,0},{32,16},{48,32},{64,48},{80,64},{96,80},{112,96},{1... | collective-permute-start | bytes 147464 | tf_op jit(solution)/shard_map/ppermute | solution.py:796
  13.9 8.6 %copy-start.4 = (s32[1,8]{1,0:T(1,128)S(1)}, s32[1,8]{1,0:T(1,128)}, u32[]{:S(2)}) copy-start(s32[1,8]{1,0:T(1,128)} %owner.3) | copy-start | bytes 100
  13.9 8.6 %collective-permute-start.4 = (f32[16,272,128]{2,1,0:T(8,128)S(1)}, f32[16,272,128]{2,1,0:T(8,128)}, u32[]{:S(2)}, u32[]{:S(2)}) collective-permute-start(f32[16,272,128]{2,1,0:T(8,128)S(1)} %get-tuple-element.32.s_in), channel_id=1, source_target_pairs={{0,1},{1,0},{2,3},{3,2},{4,5},{5,4},{6,7},{7,6},{8,9},{9,8},{10,11... | collective-permute-start | bytes 6684680 | tf_op jit(solution)/shard_map/ppermute | solution.py:799
  14.9 5.6 %collective-permute-start.2 = (f32[112,128]{1,0:T(8,128)S(1)}, f32[112,128]{1,0:T(8,128)S(1)}, u32[]{:S(2)}, u32[]{:S(2)}) collective-permute-start(f32[112,128]{1,0:T(8,128)S(1)} %get-tuple-element.37), channel_id=1, source_target_pairs={{0,2},{2,4},{4,6},{6,8},{8,10},{10,12},{12,14},{14,0},{1,3},{3,5},... | collective-permute-start | bytes 172040 | tf_op jit(solution)/shard_map/ppermute | solution.py:800
  15.2 5.1 %collective-permute-start.3 = (f32[88,128]{1,0:T(8,128)S(1)}, f32[88,128]{1,0:T(8,128)S(1)}, u32[]{:S(2)}, u32[]{:S(2)}) collective-permute-start(f32[88,128]{1,0:T(8,128)S(1)} %get-tuple-element.38), channel_id=1, source_target_pairs={{0,14},{2,0},{4,2},{6,4},{8,6},{10,8},{12,10},{14,12},{1,15},{3,1}... | collective-permute-start | bytes 135176 | tf_op jit(solution)/shard_map/ppermute | solution.py:801
  20.5 6.7 %collective-permute-start.5 = (f32[16,256,128]{2,1,0:T(8,128)}, f32[16,256,128]{2,1,0:T(8,128)}, u32[]{:S(2)}, u32[]{:S(2)}) collective-permute-start(f32[16,256,128]{2,1,0:T(8,128)} %get-tuple-element.39.gy_in), channel_id=1, source_target_pairs={{0,1},{1,0},{2,3},{3,2},{4,5},{5,4},{6,7},{7,6},{8,9},{9,8},{10,11... | collective-permute-start | bytes 6291464 | tf_op jit(solution)/shard_map/ppermute | solution.py:804
  22.3 4.9 %collective-permute-start.6 = (f32[6,128,128]{2,1,0:T(8,128)S(1)}, f32[6,128,128]{2,1,0:T(8,128)S(1)}, u32[]{:S(2)}, u32[]{:S(2)}) collective-permute-start(f32[6,128,128]{2,1,0:T(8,128)S(1)} %get-tuple-element.43.edges), channel_id=1, source_target_pairs={{0,1},{1,0},{2,3},{3,2},{4,5},{5,4},{6,7},{7,6},{8,9},{9,8},{10,11... | collective-permute-start | bytes 1179656 | tf_op jit(solution)/shard_map/ppermute | solution.py:806

commit v5 on v3

--- a/solution.py
+++ b/solution.py
@@ -250,12 +250,10 @@
     right,
     x_e,
     cy_e,
-    s_in,
     h_t,
     hc_t,
     to_l,
     to_r,
-    s,
     q_rows,
     c_rows,
     win,
@@ -263,7 +261,6 @@
     f_scr,
     res,
 ):
-    del s_in, s
     planes, rows, _ = d.shape
 
     for p in range(planes):
@@ -324,18 +321,15 @@
     return out(padded(17 * counts[0] + 9 * counts[2]), LANES)
 
 
-def x_edge(d, t, cx, cy, left, right, x_e, cy_e, s):
-    ext = s.shape[1]
+def x_edge(d, t, cx, cy, left, right, x_e, cy_e):
+    ext = d.shape[1] + 2 * RIM
     return call(
         x_edge_kernel,
-        (out(ext, LANES), out(ext, LANES), y_rim(FIRST), y_rim(LAST), out(*s.shape)),
-        (d, t, cx, cy, left, right, x_e, cy_e, s),
+        (out(ext, LANES), out(ext, LANES), y_rim(FIRST), y_rim(LAST)),
+        (d, t, cx, cy, left, right, x_e, cy_e),
         "x_edge",
         mib=12,
         scratch=[pltpu.VMEM((2, LANES, LANES), F32)] * 2 + EDGE_SCRATCH,
-        spaces=[pltpu.VMEM] * 8 + [pl.ANY],
-        out_spaces=[pltpu.VMEM] * 4 + [pl.ANY],
-        aliases={8: 4},
     )
 
 
@@ -350,13 +344,9 @@
     )
 
 
-def inner_slopes_kernel(s_t, h_t, hc_t, sh_t, gy_out, gy, a_scr, f_scr, sems):
+def inner_slopes_kernel(s_t, h_t, hc_t, gy, sh_t, a_scr, f_scr):
     planes, _, _, ext, _ = s_t.shape
     rows = ext - 2 * RIM
-
-    def copy(p):
-        at = pl.ds(p * 4, 4)
-        return pltpu.make_async_copy(gy.at[at], gy_out.at[at], sems.at[p])
 
     def body(p, _):
         for f in range(2):
@@ -365,7 +355,6 @@
                     gy[(p * 2 + f) * 2 + h, half(x), :] = rows_slope(
                         s_t.at[p, f, x], RIM + h * LANES, LANES
                     ).T
-        copy(p).start()
         return 0
 
     lax.fori_loop(0, planes, body, 0, unroll=False)
@@ -384,22 +373,17 @@
         32,
         fields=1,
     )
-    for p in range(planes):
-        copy(p).wait()
 
 
 def inner_slopes(s_t, h_t, hc_t):
     planes, _, _, ext, _ = s_t.shape
     return call(
         inner_slopes_kernel,
-        (out(ext, LANES), out(4 * planes, ext - 2 * RIM, LANES)),
+        (out(4 * planes, ext - 2 * RIM, LANES), out(ext, LANES)),
         (s_t, h_t, hc_t),
         "inner_slopes",
         mib=8,
-        scratch=[pltpu.VMEM((4 * planes, ext - 2 * RIM, LANES), F32)]
-        + [pltpu.VMEM((2, ext, LANES), F32)] * 2
-        + [pltpu.SemaphoreType.DMA((planes,))],
-        out_spaces=[pltpu.VMEM, pl.ANY],
+        scratch=[pltpu.VMEM((2, ext, LANES), F32)] * 2,
         cost=SWEEP_COST,
     )
 
@@ -486,7 +470,7 @@
     )[1]
 
 
-def finish_field(f, s_in, gy, edges, s, xy, adv=None, ready=None):
+def finish_field(f, s_in, gy, edges, s, xy, adv=None):
     planes, width = xy.shape[3:5]
     rows = NP * width
     n = 2 * width
@@ -497,8 +481,6 @@
             xy[f, r // width + i, dim, p, :, half(h)] = value[i * width : (i + 1) * width]
 
     def body(p, _):
-        if ready is not None:
-            ready(p, f)
         strip = pl.multiple_of((f * 4 + p) * STRIP, STRIP)
         first = (p * 2 + f) * 2
         for r in range(0, rows, n):
@@ -560,20 +542,10 @@
         pltpu.make_async_copy(zeros, to, sem).start()
 
 
-def own_slopes_kernel(
-    owner, core, s_in, gy_in, edges, adv, grad, s, xy, gy, buf, zeros, adv_sem, sems, in_sems
-):
+def own_slopes_kernel(owner, s_in, gy, edges, adv, grad, s, xy, buf, zeros, adv_sem, sems):
     planes = xy.shape[3]
-    me = core[0]
+    me = lax.axis_index("sa")
     mine = pl.ds(pl.multiple_of(planes * me, planes), planes)
-
-    def arrival(p, f):
-        at = pl.ds((p * 2 + f) * 2, 2)
-        return pltpu.make_async_copy(gy_in.at[at], gy.at[at], in_sems.at[f, p])
-
-    for f in range(2):
-        for p in range(planes):
-            arrival(p, f).start()
     pieces = [piece_of(owner, me, slot) for slot in range(CAP)]
     clear(pieces[-1][1], zeros)
 
@@ -581,15 +553,14 @@
         return pltpu.make_async_copy(buf.at[f], adv.at[f], adv_sem.at[f])
 
     for f in range(2):
-        finish_field(f, s_in, gy, edges, s, xy, buf, lambda p, f: arrival(p, f).wait())
+        finish_field(f, s_in, gy, edges, s, xy, buf)
         adv_copy(f).start()
-        if f == 0:
-            for slot, (piece, used) in enumerate(pieces):
-                start_copy(used, xy.at[0, piece], zeros, grad.at[slot, 0, 0:2, mine], sems.at[slot])
+        for slot, (piece, used) in enumerate(pieces):
+            start_copy(used, xy.at[f, piece], zeros, grad.at[slot, f, 0:2, mine], sems.at[slot, f])
     for f in range(2):
         adv_copy(f).wait()
-    for slot in range(CAP):
-        pltpu.make_async_copy(zeros, grad.at[slot, 0, 0:2, mine], sems.at[slot]).wait()
+        for slot in range(CAP):
+            pltpu.make_async_copy(zeros, grad.at[slot, f, 0:2, mine], sems.at[slot, f]).wait()
 
 
 SMEM = pl.BlockSpec(memory_space=pltpu.SMEM)
@@ -597,14 +568,14 @@
 ANY = pl.BlockSpec(memory_space=pl.ANY)
 
 
-def own_slopes(owner, core, s_in, gy, edges):
+def own_slopes(owner, s_in, gy, edges):
     planes = s_in.shape[0] // 4
     rows = gy.shape[1]
     cols = 2 * LANES
     width = rows // NP
     return pl.pallas_call(
         own_slopes_kernel,
-        in_specs=[SMEM, SMEM, VMEM, ANY, VMEM],
+        in_specs=[SMEM, VMEM, VMEM, VMEM],
         out_specs=(ANY, ANY, VMEM, VMEM),
         out_shape=(
             out(2, planes, rows, cols),
@@ -613,22 +584,19 @@
             pltpu.VMEM((2, NP, 2, planes, width, cols), F32),
         ),
         scratch_shapes=[
-            pltpu.VMEM(gy.shape, F32),
             pltpu.VMEM((2, planes, rows, cols), F32),
             pltpu.VMEM((2, planes, width, cols), F32),
             pltpu.SemaphoreType.DMA((2,)),
-            pltpu.SemaphoreType.DMA((CAP,)),
-            pltpu.SemaphoreType.DMA((2, planes)),
+            pltpu.SemaphoreType.DMA((CAP, 2)),
         ],
         compiler_params=pltpu.CompilerParams(vmem_limit_bytes=14 * MIB),
         cost_estimate=SWEEP_COST,
         name="own_slopes",
-    )(owner, core, s_in, gy, edges)
+    )(owner, s_in, gy, edges)
 
 
 def gradient_kernel(
     owner,
-    core,
     own,
     own_xy,
     other_in,
@@ -639,44 +607,22 @@
     wedge,
     other,
     other_xy,
-    other_y,
     part,
     wpart,
     zeros,
     xy_zeros,
-    in_sems,
-    own_sems,
     xy_sems,
     sems,
 ):
     planes, width = own_xy.shape[3:5]
-    me = core[0]
+    me = lax.axis_index("sa")
     mine = pl.ds(pl.multiple_of(planes * me, planes), planes)
     theirs = pl.ds(pl.multiple_of(planes * (1 - me), planes), planes)
 
-    def arrivals(p, f):
-        at = pl.ds((p * 2 + f) * 2, 2)
-        return (
-            pltpu.make_async_copy(other_in.at[at], other.at[at], in_sems.at[0, f, p]),
-            pltpu.make_async_copy(other_gy.at[at], other_y.at[at], in_sems.at[1, f, p]),
-        )
-
-    def ready(p, f):
-        for c in arrivals(p, f):
-            c.wait()
-
-    for f in range(2):
-        for p in range(planes):
-            for c in arrivals(p, f):
-                c.start()
     pieces = [piece_of(owner, me, slot) for slot in range(CAP)]
     clear(pieces[-1][1], zeros, xy_zeros)
-    for slot, (piece, used) in enumerate(pieces):
-        start_copy(
-            used, own_xy.at[1, piece], xy_zeros, grad.at[slot, 1, 0:2, mine], own_sems.at[slot]
-        )
     for f in range(2):
-        finish_field(f, other, other_y, other_edges, other, other_xy, ready=ready)
+        finish_field(f, other_in, other_gy, other_edges, other, other_xy)
         for slot, (piece, used) in enumerate(pieces):
             start_copy(
                 used,
@@ -741,7 +687,6 @@
     lax.fori_loop(0, CAP, slot_body, 0, unroll=False)
 
     def wait_body(slot, _):
-        pltpu.make_async_copy(xy_zeros, grad.at[slot, 1, 0:2, mine], own_sems.at[slot]).wait()
         for f in range(2):
             pltpu.make_async_copy(
                 xy_zeros, grad.at[slot, f, 0:2, theirs], xy_sems.at[slot, f]
@@ -753,30 +698,27 @@
     lax.fori_loop(0, CAP, wait_body, 0, unroll=False)
 
 
-def gradients_of(owner, core, own, own_xy, other, other_gy, other_edges, grad):
+def gradients_of(owner, own, own_xy, other, other_gy, other_edges, grad):
     planes, width, cols = own_xy.shape[3:]
     return pl.pallas_call(
         gradient_kernel,
-        in_specs=[SMEM, SMEM, VMEM, VMEM, ANY, ANY, VMEM, ANY],
+        in_specs=[SMEM, VMEM, VMEM, VMEM, VMEM, VMEM, ANY],
         out_specs=(ANY, ANY),
         out_shape=(out(*grad.shape), out(CAP, 2 * planes, width, cols)),
         scratch_shapes=[
             pltpu.VMEM(own.shape, F32),
             pltpu.VMEM(own_xy.shape, F32),
-            pltpu.VMEM(other_gy.shape, F32),
             pltpu.VMEM((CAP, 2, 2 * planes, width, cols), F32),
             pltpu.VMEM((CAP, 2 * planes, width, cols), F32),
             pltpu.VMEM((2 * planes, width, cols), F32),
             pltpu.VMEM((2, planes, width, cols), F32),
-            pltpu.SemaphoreType.DMA((2, 2, planes)),
-            pltpu.SemaphoreType.DMA((CAP,)),
             pltpu.SemaphoreType.DMA((CAP, 2)),
             pltpu.SemaphoreType.DMA((CAP, 3)),
         ],
-        input_output_aliases={7: 0},
+        input_output_aliases={6: 0},
         compiler_params=pltpu.CompilerParams(vmem_limit_bytes=24 * MIB),
         name="gradient",
-    )(owner, core, own, own_xy, other, other_gy, other_edges, grad)
+    )(owner, own, own_xy, other, other_gy, other_edges, grad)
 
 
 def per_device(density, heat, cx, cy, owner):
@@ -785,20 +727,18 @@
     left = lax.ppermute(hi, "gx", ring(nx, 1))
     right = lax.ppermute(lo, "gx", ring(nx, -1))
     x_e, cy_e, s_t, swept = inner(density, heat, cx, cy)
-    h_t, hc_t, to_l, to_r, swept = x_edge(density, heat, cx, cy, left, right, x_e, cy_e, swept)
-    other = lax.ppermute(swept, "sa", ring(2, 1))
+    h_t, hc_t, to_l, to_r = x_edge(density, heat, cx, cy, left, right, x_e, cy_e)
+    sent, to_l, to_r = lax.optimization_barrier((swept, to_l, to_r))
+    other = lax.ppermute(sent, "sa", ring(2, 1))
     from_l = lax.ppermute(to_r, "gy", ring(ny, 1))
     from_r = lax.ppermute(to_l, "gy", ring(ny, -1))
-    sh_t, gy = inner_slopes(s_t, h_t, hc_t)
-    gy, from_l, from_r = lax.optimization_barrier((gy, from_l, from_r))
-    other_gy = lax.ppermute(gy, "sa", ring(2, 1))
+    gy, sh_t = inner_slopes(s_t, h_t, hc_t)
+    sent, from_l, from_r = lax.optimization_barrier((gy, from_l, from_r))
+    other_gy = lax.ppermute(sent, "sa", ring(2, 1))
     edges = y_edge(x_e, cy_e, h_t, hc_t, from_l, from_r, sh_t)
     other_edges = lax.ppermute(edges, "sa", ring(2, 1))
-    core = lax.axis_index("sa").astype(jnp.int32).reshape(1)
-    advected, gradients, own, own_xy = own_slopes(owner, core, swept, gy, edges)
-    gradients, wedge = gradients_of(
-        owner, core, own, own_xy, other, other_gy, other_edges, gradients
-    )
+    advected, gradients, own, own_xy = own_slopes(owner, swept, gy, edges)
+    gradients, wedge = gradients_of(owner, own, own_xy, other, other_gy, other_edges, gradients)
     return advected, gradients, wedge
 
 

time: 33.3 us -> 31.4 us (0.943)
  Pallas kernels: 18.9 us -> 16.2 us
  waiting for transfers between devices: 0.33 us -> 1.08 us
    pallas_call x2, Pallas kernels: 10.7 us -> 8.7 us  [the longest x1 4.94 us: gradients_of(): pl.pallas_call(gradient_kernel, in_specs=[SMEM, VMEM, VMEM, VMEM, VMEM, V...]
    ppermute x1, waiting for transfers between devices: 0.19 us -> 0.94 us  [per_device(): from_r = lax.ppermute(to_l, 'gy', ring(ny, -1))]
    pallas_call x5, Pallas kernels: 8.12 us -> 7.48 us  [call(): pl.pallas_call(kernel, in_specs=[pl.BlockSpec(memory_space=x) for x in sp...]
  transfers between devices with their start and end apart: 7 -> 7, of which waited for: 2 -> 2; matrix products, arithmetic and copies ran while one was open for 0% -> 0% of each run, Pallas kernels for 33% -> 31%
where the time goes in v5:
time: 31.4 us; the launch traced here: 31.3 us
  Pallas kernels  16.2 us (52%)
  starting transfers between devices  13.2 us (42%)
  waiting for transfers between devices  1.08 us (3%)
  between operations  0.76 us (2%)
    pallas_call x5, Pallas kernels, call(): pl.pallas_call(kernel, in_specs=[pl.BlockSpec(memory_space=x) for x in sp...  7.48 us
    pallas_call x1, Pallas kernels, gradients_of(): pl.pallas_call(gradient_kernel, in_specs=[SMEM, VMEM, VMEM, VMEM, VMEM, V...  4.94 us
    pallas_call x1, Pallas kernels, own_slopes(): pl.pallas_call(own_slopes_kernel, in_specs=[SMEM, VMEM, VMEM, VMEM], out_...  3.76 us
    ppermute x1, starting transfers between devices, per_device(): left = lax.ppermute(hi, 'gx', ring(nx, 1))  3.64 us
    ppermute x1, starting transfers between devices, per_device(): right = lax.ppermute(lo, 'gx', ring(nx, -1))  3.55 us
    ppermute x1, starting transfers between devices, per_device(): from_r = lax.ppermute(to_l, 'gy', ring(ny, -1))  3.26 us
    ppermute x1, starting transfers between devices, per_device(): other_gy = lax.ppermute(sent, 'sa', ring(2, 1))  1.32 us
    ppermute x1, starting transfers between devices, per_device(): other = lax.ppermute(sent, 'sa', ring(2, 1))  1.03 us
  transfers between devices with their start and end apart: 7, of which 2 were waited for; matrix products, arithmetic and copies ran while one was open for 0% of the time, Pallas kernels for 31%

profile of v5, /device:TPU:1, one launch (start us, length us, event | category | flops | bytes accessed | tf_op | source)
XLA Modules:
  0.0 31.3 jit_solution(10155890119183433853)
XLA Ops:
  0.6 0.0 copy-start.3
  0.6 0.0 copy-start.2
  0.7 0.0 copy-start.1
  0.7 0.0 copy-start
  0.7 1.1 %edge_rows.1 = (f32[48,256]{1,0:T(8,128)S(1)}, f32[64,256]{1,0:T(8,128)S(1)}) custom-call(f32[4,256,256]{2,1,0:T(8,128)} %d.5, f32[4,256,256]{2,1,0:T(8,128)} %t.5, f32[4,256,256]{2,1,0:T(8,128)} %cx.5, f32[4,256,256]{2,1,0:T(8,128)} %cy.5), custom_call_target="tpu_custom_call" | custom-call | tf_op jit(solution)/shard_map/edge_rows/pallas_call | solution.py:61
  1.8 3.6 %collective-permute-start = (f32[64,256]{1,0:T(8,128)S(1)}, f32[64,256]{1,0:T(8,128)S(1)}, u32[]{:S(2)}, u32[]{:S(2)}) collective-permute-start(f32[64,256]{1,0:T(8,128)S(1)} %get-tuple-element.30), channel_id=1, source_target_pairs={{0,16},{16,32},{32,48},{48,64},{64,80},{80,96},{96,112},{112,0},{1... | collective-permute-start | bytes 196616 | tf_op jit(solution)/shard_map/ppermute | solution.py:727
  5.4 3.6 %collective-permute-start.1 = (f32[48,256]{1,0:T(8,128)S(1)}, f32[48,256]{1,0:T(8,128)S(1)}, u32[]{:S(2)}, u32[]{:S(2)}) collective-permute-start(f32[48,256]{1,0:T(8,128)S(1)} %get-tuple-element.31), channel_id=1, source_target_pairs={{0,112},{16,0},{32,16},{48,32},{64,48},{80,64},{96,80},{112,96},{1... | collective-permute-start | bytes 147464 | tf_op jit(solution)/shard_map/ppermute | solution.py:728
  9.0 0.0 copy-done.3
  9.0 0.0 copy-done.2
  9.0 0.0 copy-done.1
  9.0 0.0 copy-done
  9.0 4.5 %inner.1 = (f32[2,4,2,2,16,128]{5,4,3,2,1,0:T(8,128)S(1)}, f32[2,4,2,16,128]{4,3,2,1,0:T(8,128)S(1)}, f32[4,2,2,272,128]{4,3,2,1,0:T(8,128)S(1)}, f32[16,272,128]{2,1,0:T(8,128)S(1)}) custom-call(f32[4,256,256]{2,1,0:T(8,128)S(1)} %copy-done, f32[4,256,256]{2,1,0:T(8,128)S(1)} %copy-done.1, f32[4,256,256]{2,1,0:T(8,128)S(1)} %copy-done.2, ...), custom_call_target="tpu_custom_call" | custom-call | flops 20000000 | bytes 6000000 | tf_op jit(solution)/shard_map/inner/pallas_call | solution.py:61
  13.5 0.0 collective-permute-done.1.right
  13.5 0.0 collective-permute-done.left
  13.5 0.4 %x_edge.1 = (f32[272,128]{1,0:T(8,128)S(1)}, f32[272,128]{1,0:T(8,128)S(1)}, f32[88,128]{1,0:T(8,128)S(1)}, f32[112,128]{1,0:T(8,128)S(1)}) custom-call(f32[4,256,256]{2,1,0:T(8,128)S(1)} %copy-done, f32[4,256,256]{2,1,0:T(8,128)S(1)} %copy-done.1, f32[4,256,256]{2,1,0:T(8,128)S(1)} %copy-done.2, f32[4,256,256]{2,1,0:T(8,128)S(1)} %copy-done.3, ...), custom_call_target="tpu_custom_call" | custom-call | tf_op jit(solution)/shard_map/x_edge/pallas_call | solution.py:61
  14.0 0.0 copy-start.4
  14.0 1.0 %collective-permute-start.4 = (f32[16,272,128]{2,1,0:T(8,128)S(1)}, f32[16,272,128]{2,1,0:T(8,128)S(1)}, u32[]{:S(2)}, u32[]{:S(2)}) collective-permute-start(f32[16,272,128]{2,1,0:T(8,128)S(1)} %get-tuple-element.48.s_in), channel_id=1, source_target_pairs={{0,1},{1,0},{2,3},{3,2},{4,5},{5,4},{6,7},{7,6},{8,9},{9,8},{10,11... | collective-permute-start | bytes 6684680 | tf_op jit(solution)/shard_map/ppermute | solution.py:732
  15.0 0.3 %collective-permute-start.2 = (f32[112,128]{1,0:T(8,128)S(1)}, f32[112,128]{1,0:T(8,128)S(1)}, u32[]{:S(2)}, u32[]{:S(2)}) collective-permute-start(f32[112,128]{1,0:T(8,128)S(1)} %get-tuple-element.39), channel_id=1, source_target_pairs={{0,2},{2,4},{4,6},{6,8},{8,10},{10,12},{12,14},{14,0},{1,3},{3,5},... | collective-permute-start | bytes 172040 | tf_op jit(solution)/shard_map/ppermute | solution.py:733
  15.3 3.3 %collective-permute-start.3 = (f32[88,128]{1,0:T(8,128)S(1)}, f32[88,128]{1,0:T(8,128)S(1)}, u32[]{:S(2)}, u32[]{:S(2)}) collective-permute-start(f32[88,128]{1,0:T(8,128)S(1)} %get-tuple-element.40), channel_id=1, source_target_pairs={{0,14},{2,0},{4,2},{6,4},{8,6},{10,8},{12,10},{14,12},{1,15},{3,1}... | collective-permute-start | bytes 135176 | tf_op jit(solution)/shard_map/ppermute | solution.py:734
  18.6 0.9 %inner_slopes.1 = (f32[16,256,128]{2,1,0:T(8,128)S(1)}, f32[272,128]{1,0:T(8,128)S(1)}) custom-call(f32[4,2,2,272,128]{4,3,2,1,0:T(8,128)S(1)} %get-tuple-element.29.s_t, f32[272,128]{1,0:T(8,128)S(1)} %get-tuple-element.34.h_t, f32[272,128]{1,0:T(8,128)S(1)} %get-tuple-element.35.hc_t), custom_call_target="tpu_custom_call" | custom-call | flops 20000000 | bytes 6000000 | tf_op jit(solution)/shard_map/inner_slopes/pallas_call | solution.py:61
  19.5 0.9 %collective-permute-done.3.from_r = f32[88,128]{1,0:T(8,128)S(1)} collective-permute-done((f32[88,128]{1,0:T(8,128)S(1)}, f32[88,128]{1,0:T(8,128)S(1)}, u32[]{:S(2)}, u32[]{:S(2)}) %collective-permute-start.3) | collective-permute-done | bytes 45088 | tf_op jit(solution)/shard_map/ppermute | solution.py:734
  20.5 0.1 collective-permute-done.2.from_l
  20.6 1.3 %collective-permute-start.5 = (f32[16,256,128]{2,1,0:T(8,128)S(1)}, f32[16,256,128]{2,1,0:T(8,128)S(1)}, u32[]{:S(2)}, u32[]{:S(2)}) collective-permute-start(f32[16,256,128]{2,1,0:T(8,128)S(1)} %get-tuple-element.49.gy), channel_id=1, source_target_pairs={{0,1},{1,0},{2,3},{3,2},{4,5},{5,4},{6,7},{7,6},{8,9},{9,8},{10,11... | collective-permute-start | bytes 6291464 | tf_op jit(solution)/shard_map/ppermute | solution.py:737
  21.9 0.5 %y_edge.1 = (f32[272,128]{1,0:T(8,128)S(1)}, f32[6,128,128]{2,1,0:T(8,128)S(1)}) custom-call(f32[2,4,2,2,16,128]{5,4,3,2,1,0:T(8,128)S(1)} %get-tuple-element.32.x_e, f32[2,4,2,16,128]{4,3,2,1,0:T(8,128)S(1)} %get-tuple-element.33.cy_e, f32[272,128]{1,0:T(8,128)S(1)} %get-tuple-element.34.h_t, ...), custom_call_target="tpu_custom_call", output_to_operand_aliasing={{0}: (6, {})} | custom-call | tf_op jit(solution)/shard_map/y_edge/pallas_call | solution.py:61
  22.4 0.1 collective-permute-start.6
  22.5 0.0 copy-done.4
  22.5 3.8 %own_slopes.1 = (f32[2,4,256,256]{3,2,1,0:T(8,128)}, f32[6,2,3,8,32,256]{5,4,3,2,1,0:T(8,128)}, f32[16,272,128]{2,1,0:T(8,128)S(1)}, f32[2,8,2,4,32,256]{5,4,3,2,1,0:T(8,128)S(1)}) custom-call(s32[1,8]{1,0:T(1,128)S(1)} %copy-done.4, f32[16,272,128]{2,1,0:T(8,128)S(1)} %get-tuple-element.48.s_in, f32[16,256,128]{2,1,0:T(8,128)S(1)} %get-tuple-element.49.gy, ...), custom_call_target="tpu_custom_call" | custom-call | flops 20000000 | bytes 6000000 | tf_op jit(solution)/shard_map/own_slopes/pallas_call | solution.py:576
  26.3 0.0 collective-permute-done.6.other_edges
  26.3 0.0 collective-permute-done.5.other_gy
  26.3 0.0 collective-permute-done.4.other_in
  26.3 4.9 %gradient.1 = (f32[6,2,3,8,32,256]{5,4,3,2,1,0:T(8,128)}, f32[6,8,32,256]{3,2,1,0:T(8,128)}) custom-call(s32[1,8]{1,0:T(1,128)S(1)} %copy-done.4, f32[16,272,128]{2,1,0:T(8,128)S(1)} %get-tuple-element.46.own, f32[2,8,2,4,32,256]{5,4,3,2,1,0:T(8,128)S(1)} %get-tuple-element.47.own_xy, ...), custom_call_target="tpu_custom_call", output_to_operand_aliasing={{0}: (6, {})} | custom-call | tf_op jit(solution)/shard_map/gradient/pallas_call | solution.py:703
Async XLA Ops:
  0.6 8.4 %copy-start.3 = (f32[4,256,256]{2,1,0:T(8,128)S(1)}, f32[4,256,256]{2,1,0:T(8,128)}, u32[]{:S(2)}) copy-start(f32[4,256,256]{2,1,0:T(8,128)} %cy.5) | copy-start | bytes 3145732
  0.6 8.4 %copy-start.2 = (f32[4,256,256]{2,1,0:T(8,128)S(1)}, f32[4,256,256]{2,1,0:T(8,128)}, u32[]{:S(2)}) copy-start(f32[4,256,256]{2,1,0:T(8,128)} %cx.5) | copy-start | bytes 3145732
  0.7 8.4 %copy-start.1 = (f32[4,256,256]{2,1,0:T(8,128)S(1)}, f32[4,256,256]{2,1,0:T(8,128)}, u32[]{:S(2)}) copy-start(f32[4,256,256]{2,1,0:T(8,128)} %t.5) | copy-start | bytes 3145732
  0.7 8.3 %copy-start = (f32[4,256,256]{2,1,0:T(8,128)S(1)}, f32[4,256,256]{2,1,0:T(8,128)}, u32[]{:S(2)}) copy-start(f32[4,256,256]{2,1,0:T(8,128)} %d.5) | copy-start | bytes 3145732
  1.8 11.7 %collective-permute-start = (f32[64,256]{1,0:T(8,128)S(1)}, f32[64,256]{1,0:T(8,128)S(1)}, u32[]{:S(2)}, u32[]{:S(2)}) collective-permute-start(f32[64,256]{1,0:T(8,128)S(1)} %get-tuple-element.30), channel_id=1, source_target_pairs={{0,16},{16,32},{32,48},{48,64},{64,80},{80,96},{96,112},{112,0},{1... | collective-permute-start | bytes 196616 | tf_op jit(solution)/shard_map/ppermute | solution.py:727
  5.4 8.1 %collective-permute-start.1 = (f32[48,256]{1,0:T(8,128)S(1)}, f32[48,256]{1,0:T(8,128)S(1)}, u32[]{:S(2)}, u32[]{:S(2)}) collective-permute-start(f32[48,256]{1,0:T(8,128)S(1)} %get-tuple-element.31), channel_id=1, source_target_pairs={{0,112},{16,0},{32,16},{48,32},{64,48},{80,64},{96,80},{112,96},{1... | collective-permute-start | bytes 147464 | tf_op jit(solution)/shard_map/ppermute | solution.py:728
  14.0 8.6 %copy-start.4 = (s32[1,8]{1,0:T(1,128)S(1)}, s32[1,8]{1,0:T(1,128)}, u32[]{:S(2)}) copy-start(s32[1,8]{1,0:T(1,128)} %owner.3) | copy-start | bytes 100
  14.0 12.4 %collective-permute-start.4 = (f32[16,272,128]{2,1,0:T(8,128)S(1)}, f32[16,272,128]{2,1,0:T(8,128)S(1)}, u32[]{:S(2)}, u32[]{:S(2)}) collective-permute-start(f32[16,272,128]{2,1,0:T(8,128)S(1)} %get-tuple-element.48.s_in), channel_id=1, source_target_pairs={{0,1},{1,0},{2,3},{3,2},{4,5},{5,4},{6,7},{7,6},{8,9},{9,8},{10,11... | collective-permute-start | bytes 6684680 | tf_op jit(solution)/shard_map/ppermute | solution.py:732
  15.0 5.6 %collective-permute-start.2 = (f32[112,128]{1,0:T(8,128)S(1)}, f32[112,128]{1,0:T(8,128)S(1)}, u32[]{:S(2)}, u32[]{:S(2)}) collective-permute-start(f32[112,128]{1,0:T(8,128)S(1)} %get-tuple-element.39), channel_id=1, source_target_pairs={{0,2},{2,4},{4,6},{6,8},{8,10},{10,12},{12,14},{14,0},{1,3},{3,5},... | collective-permute-start | bytes 172040 | tf_op jit(solution)/shard_map/ppermute | solution.py:733
  15.3 5.1 %collective-permute-start.3 = (f32[88,128]{1,0:T(8,128)S(1)}, f32[88,128]{1,0:T(8,128)S(1)}, u32[]{:S(2)}, u32[]{:S(2)}) collective-permute-start(f32[88,128]{1,0:T(8,128)S(1)} %get-tuple-element.40), channel_id=1, source_target_pairs={{0,14},{2,0},{4,2},{6,4},{8,6},{10,8},{12,10},{14,12},{1,15},{3,1}... | collective-permute-start | bytes 135176 | tf_op jit(solution)/shard_map/ppermute | solution.py:734
  20.6 5.7 %collective-permute-start.5 = (f32[16,256,128]{2,1,0:T(8,128)S(1)}, f32[16,256,128]{2,1,0:T(8,128)S(1)}, u32[]{:S(2)}, u32[]{:S(2)}) collective-permute-start(f32[16,256,128]{2,1,0:T(8,128)S(1)} %get-tuple-element.49.gy), channel_id=1, source_target_pairs={{0,1},{1,0},{2,3},{3,2},{4,5},{5,4},{6,7},{7,6},{8,9},{9,8},{10,11... | collective-permute-start | bytes 6291464 | tf_op jit(solution)/shard_map/ppermute | solution.py:737
  22.4 3.9 %collective-permute-start.6 = (f32[6,128,128]{2,1,0:T(8,128)S(1)}, f32[6,128,128]{2,1,0:T(8,128)S(1)}, u32[]{:S(2)}, u32[]{:S(2)}) collective-permute-start(f32[6,128,128]{2,1,0:T(8,128)S(1)} %get-tuple-element.44.edges), channel_id=1, source_target_pairs={{0,1},{1,0},{2,3},{3,2},{4,5},{5,4},{6,7},{7,6},{8,9},{9,8},{10,11... | collective-permute-start | bytes 1179656 | tf_op jit(solution)/shard_map/ppermute | solution.py:739

commit v6 on v5

--- a/solution.py
+++ b/solution.py
@@ -555,12 +555,13 @@
     for f in range(2):
         finish_field(f, s_in, gy, edges, s, xy, buf)
         adv_copy(f).start()
-        for slot, (piece, used) in enumerate(pieces):
-            start_copy(used, xy.at[f, piece], zeros, grad.at[slot, f, 0:2, mine], sems.at[slot, f])
+        if f == 0:
+            for slot, (piece, used) in enumerate(pieces):
+                start_copy(used, xy.at[0, piece], zeros, grad.at[slot, 0, 0:2, mine], sems.at[slot])
     for f in range(2):
         adv_copy(f).wait()
-        for slot in range(CAP):
-            pltpu.make_async_copy(zeros, grad.at[slot, f, 0:2, mine], sems.at[slot, f]).wait()
+    for slot in range(CAP):
+        pltpu.make_async_copy(zeros, grad.at[slot, 0, 0:2, mine], sems.at[slot]).wait()
 
 
 SMEM = pl.BlockSpec(memory_space=pltpu.SMEM)
@@ -587,7 +588,7 @@
             pltpu.VMEM((2, planes, rows, cols), F32),
             pltpu.VMEM((2, planes, width, cols), F32),
             pltpu.SemaphoreType.DMA((2,)),
-            pltpu.SemaphoreType.DMA((CAP, 2)),
+            pltpu.SemaphoreType.DMA((CAP,)),
         ],
         compiler_params=pltpu.CompilerParams(vmem_limit_bytes=14 * MIB),
         cost_estimate=SWEEP_COST,
@@ -611,6 +612,7 @@
     wpart,
     zeros,
     xy_zeros,
+    own_sems,
     xy_sems,
     sems,
 ):
@@ -621,6 +623,10 @@
 
     pieces = [piece_of(owner, me, slot) for slot in range(CAP)]
     clear(pieces[-1][1], zeros, xy_zeros)
+    for slot, (piece, used) in enumerate(pieces):
+        start_copy(
+            used, own_xy.at[1, piece], xy_zeros, grad.at[slot, 1, 0:2, mine], own_sems.at[slot]
+        )
     for f in range(2):
         finish_field(f, other_in, other_gy, other_edges, other, other_xy)
         for slot, (piece, used) in enumerate(pieces):
@@ -687,6 +693,7 @@
     lax.fori_loop(0, CAP, slot_body, 0, unroll=False)
 
     def wait_body(slot, _):
+        pltpu.make_async_copy(xy_zeros, grad.at[slot, 1, 0:2, mine], own_sems.at[slot]).wait()
         for f in range(2):
             pltpu.make_async_copy(
                 xy_zeros, grad.at[slot, f, 0:2, theirs], xy_sems.at[slot, f]
@@ -712,6 +719,7 @@
             pltpu.VMEM((CAP, 2 * planes, width, cols), F32),
             pltpu.VMEM((2 * planes, width, cols), F32),
             pltpu.VMEM((2, planes, width, cols), F32),
+            pltpu.SemaphoreType.DMA((CAP,)),
             pltpu.SemaphoreType.DMA((CAP, 2)),
             pltpu.SemaphoreType.DMA((CAP, 3)),
         ],

time: 31.4 us -> 31.4 us (level)
  Pallas kernels: 16.2 us -> 15.7 us
  waiting for transfers between devices: 1.08 us -> 1.58 us
    pallas_call x1, Pallas kernels: 3.76 us -> 3.23 us  [own_slopes(): pl.pallas_call(own_slopes_kernel, in_specs=[SMEM, VMEM, VMEM, VMEM], out_...]
    ppermute x1, waiting for transfers between devices: 0.01 us -> 0.5 us  [per_device(): other_edges = lax.ppermute(edges, 'sa', ring(2, 1))]
  transfers between devices with their start and end apart: 7 -> 7, of which waited for: 2 -> 3; matrix products, arithmetic and copies ran while one was open for 0% -> 0% of each run, Pallas kernels for 31% -> 29%
where the time goes in v6:
time: 31.4 us; the launch traced here: 31.3 us
  Pallas kernels  15.7 us (50%)
  starting transfers between devices  13.2 us (42%)
  waiting for transfers between devices  1.58 us (5%)
  between operations  0.74 us (2%)
    pallas_call x5, Pallas kernels, call(): pl.pallas_call(kernel, in_specs=[pl.BlockSpec(memory_space=x) for x in sp...  7.48 us
    pallas_call x1, Pallas kernels, gradients_of(): pl.pallas_call(gradient_kernel, in_specs=[SMEM, VMEM, VMEM, VMEM, VMEM, V...  4.98 us
    ppermute x1, starting transfers between devices, per_device(): left = lax.ppermute(hi, 'gx', ring(nx, 1))  3.64 us
    ppermute x1, starting transfers between devices, per_device(): right = lax.ppermute(lo, 'gx', ring(nx, -1))  3.55 us
    ppermute x1, starting transfers between devices, per_device(): from_r = lax.ppermute(to_l, 'gy', ring(ny, -1))  3.26 us
    pallas_call x1, Pallas kernels, own_slopes(): pl.pallas_call(own_slopes_kernel, in_specs=[SMEM, VMEM, VMEM, VMEM], out_...  3.23 us
    ppermute x1, starting transfers between devices, per_device(): other_gy = lax.ppermute(sent, 'sa', ring(2, 1))  1.32 us
    ppermute x1, starting transfers between devices, per_device(): other = lax.ppermute(sent, 'sa', ring(2, 1))  1.03 us
  transfers between devices with their start and end apart: 7, of which 3 were waited for; matrix products, arithmetic and copies ran while one was open for 0% of the time, Pallas kernels for 29%

profile of v6, /device:TPU:1, one launch (start us, length us, event | category | flops | bytes accessed | tf_op | source)
XLA Modules:
  0.0 31.3 jit_solution(14209440818992270933)
XLA Ops:
  0.6 0.0 copy-start.3
  0.6 0.0 copy-start.2
  0.7 0.0 copy-start.1
  0.7 0.0 copy-start
  0.7 1.1 %edge_rows.1 = (f32[48,256]{1,0:T(8,128)S(1)}, f32[64,256]{1,0:T(8,128)S(1)}) custom-call(f32[4,256,256]{2,1,0:T(8,128)} %d.5, f32[4,256,256]{2,1,0:T(8,128)} %t.5, f32[4,256,256]{2,1,0:T(8,128)} %cx.5, f32[4,256,256]{2,1,0:T(8,128)} %cy.5), custom_call_target="tpu_custom_call" | custom-call | tf_op jit(solution)/shard_map/edge_rows/pallas_call | solution.py:61
  1.8 3.6 %collective-permute-start = (f32[64,256]{1,0:T(8,128)S(1)}, f32[64,256]{1,0:T(8,128)S(1)}, u32[]{:S(2)}, u32[]{:S(2)}) collective-permute-start(f32[64,256]{1,0:T(8,128)S(1)} %get-tuple-element.30), channel_id=1, source_target_pairs={{0,16},{16,32},{32,48},{48,64},{64,80},{80,96},{96,112},{112,0},{1... | collective-permute-start | bytes 196616 | tf_op jit(solution)/shard_map/ppermute | solution.py:735
  5.4 3.6 %collective-permute-start.1 = (f32[48,256]{1,0:T(8,128)S(1)}, f32[48,256]{1,0:T(8,128)S(1)}, u32[]{:S(2)}, u32[]{:S(2)}) collective-permute-start(f32[48,256]{1,0:T(8,128)S(1)} %get-tuple-element.31), channel_id=1, source_target_pairs={{0,112},{16,0},{32,16},{48,32},{64,48},{80,64},{96,80},{112,96},{1... | collective-permute-start | bytes 147464 | tf_op jit(solution)/shard_map/ppermute | solution.py:736
  9.0 0.0 copy-done.3
  9.0 0.0 copy-done.2
  9.0 0.0 copy-done.1
  9.0 0.0 copy-done
  9.0 4.5 %inner.1 = (f32[2,4,2,2,16,128]{5,4,3,2,1,0:T(8,128)S(1)}, f32[2,4,2,16,128]{4,3,2,1,0:T(8,128)S(1)}, f32[4,2,2,272,128]{4,3,2,1,0:T(8,128)S(1)}, f32[16,272,128]{2,1,0:T(8,128)S(1)}) custom-call(f32[4,256,256]{2,1,0:T(8,128)S(1)} %copy-done, f32[4,256,256]{2,1,0:T(8,128)S(1)} %copy-done.1, f32[4,256,256]{2,1,0:T(8,128)S(1)} %copy-done.2, ...), custom_call_target="tpu_custom_call" | custom-call | flops 20000000 | bytes 6000000 | tf_op jit(solution)/shard_map/inner/pallas_call | solution.py:61
  13.5 0.0 collective-permute-done.1.right
  13.5 0.0 collective-permute-done.left
  13.5 0.4 %x_edge.1 = (f32[272,128]{1,0:T(8,128)S(1)}, f32[272,128]{1,0:T(8,128)S(1)}, f32[88,128]{1,0:T(8,128)S(1)}, f32[112,128]{1,0:T(8,128)S(1)}) custom-call(f32[4,256,256]{2,1,0:T(8,128)S(1)} %copy-done, f32[4,256,256]{2,1,0:T(8,128)S(1)} %copy-done.1, f32[4,256,256]{2,1,0:T(8,128)S(1)} %copy-done.2, f32[4,256,256]{2,1,0:T(8,128)S(1)} %copy-done.3, ...), custom_call_target="tpu_custom_call" | custom-call | tf_op jit(solution)/shard_map/x_edge/pallas_call | solution.py:61
  14.0 0.0 copy-start.4
  14.0 1.0 %collective-permute-start.4 = (f32[16,272,128]{2,1,0:T(8,128)S(1)}, f32[16,272,128]{2,1,0:T(8,128)S(1)}, u32[]{:S(2)}, u32[]{:S(2)}) collective-permute-start(f32[16,272,128]{2,1,0:T(8,128)S(1)} %get-tuple-element.48.s_in), channel_id=1, source_target_pairs={{0,1},{1,0},{2,3},{3,2},{4,5},{5,4},{6,7},{7,6},{8,9},{9,8},{10,11... | collective-permute-start | bytes 6684680 | tf_op jit(solution)/shard_map/ppermute | solution.py:740
  15.0 0.3 %collective-permute-start.2 = (f32[112,128]{1,0:T(8,128)S(1)}, f32[112,128]{1,0:T(8,128)S(1)}, u32[]{:S(2)}, u32[]{:S(2)}) collective-permute-start(f32[112,128]{1,0:T(8,128)S(1)} %get-tuple-element.39), channel_id=1, source_target_pairs={{0,2},{2,4},{4,6},{6,8},{8,10},{10,12},{12,14},{14,0},{1,3},{3,5},... | collective-permute-start | bytes 172040 | tf_op jit(solution)/shard_map/ppermute | solution.py:741
  15.3 3.3 %collective-permute-start.3 = (f32[88,128]{1,0:T(8,128)S(1)}, f32[88,128]{1,0:T(8,128)S(1)}, u32[]{:S(2)}, u32[]{:S(2)}) collective-permute-start(f32[88,128]{1,0:T(8,128)S(1)} %get-tuple-element.40), channel_id=1, source_target_pairs={{0,14},{2,0},{4,2},{6,4},{8,6},{10,8},{12,10},{14,12},{1,15},{3,1}... | collective-permute-start | bytes 135176 | tf_op jit(solution)/shard_map/ppermute | solution.py:742
  18.6 0.9 %inner_slopes.1 = (f32[16,256,128]{2,1,0:T(8,128)S(1)}, f32[272,128]{1,0:T(8,128)S(1)}) custom-call(f32[4,2,2,272,128]{4,3,2,1,0:T(8,128)S(1)} %get-tuple-element.29.s_t, f32[272,128]{1,0:T(8,128)S(1)} %get-tuple-element.34.h_t, f32[272,128]{1,0:T(8,128)S(1)} %get-tuple-element.35.hc_t), custom_call_target="tpu_custom_call" | custom-call | flops 20000000 | bytes 6000000 | tf_op jit(solution)/shard_map/inner_slopes/pallas_call | solution.py:61
  19.5 0.9 %collective-permute-done.3.from_r = f32[88,128]{1,0:T(8,128)S(1)} collective-permute-done((f32[88,128]{1,0:T(8,128)S(1)}, f32[88,128]{1,0:T(8,128)S(1)}, u32[]{:S(2)}, u32[]{:S(2)}) %collective-permute-start.3) | collective-permute-done | bytes 45088 | tf_op jit(solution)/shard_map/ppermute | solution.py:742
  20.5 0.1 collective-permute-done.2.from_l
  20.6 1.3 %collective-permute-start.5 = (f32[16,256,128]{2,1,0:T(8,128)S(1)}, f32[16,256,128]{2,1,0:T(8,128)S(1)}, u32[]{:S(2)}, u32[]{:S(2)}) collective-permute-start(f32[16,256,128]{2,1,0:T(8,128)S(1)} %get-tuple-element.49.gy), channel_id=1, source_target_pairs={{0,1},{1,0},{2,3},{3,2},{4,5},{5,4},{6,7},{7,6},{8,9},{9,8},{10,11... | collective-permute-start | bytes 6291464 | tf_op jit(solution)/shard_map/ppermute | solution.py:745
  21.9 0.5 %y_edge.1 = (f32[272,128]{1,0:T(8,128)S(1)}, f32[6,128,128]{2,1,0:T(8,128)S(1)}) custom-call(f32[2,4,2,2,16,128]{5,4,3,2,1,0:T(8,128)S(1)} %get-tuple-element.32.x_e, f32[2,4,2,16,128]{4,3,2,1,0:T(8,128)S(1)} %get-tuple-element.33.cy_e, f32[272,128]{1,0:T(8,128)S(1)} %get-tuple-element.34.h_t, ...), custom_call_target="tpu_custom_call", output_to_operand_aliasing={{0}: (6, {})} | custom-call | tf_op jit(solution)/shard_map/y_edge/pallas_call | solution.py:61
  22.4 0.1 collective-permute-start.6
  22.5 0.0 copy-done.4
  22.5 3.2 %own_slopes.1 = (f32[2,4,256,256]{3,2,1,0:T(8,128)}, f32[6,2,3,8,32,256]{5,4,3,2,1,0:T(8,128)}, f32[16,272,128]{2,1,0:T(8,128)S(1)}, f32[2,8,2,4,32,256]{5,4,3,2,1,0:T(8,128)S(1)}) custom-call(s32[1,8]{1,0:T(1,128)S(1)} %copy-done.4, f32[16,272,128]{2,1,0:T(8,128)S(1)} %get-tuple-element.48.s_in, f32[16,256,128]{2,1,0:T(8,128)S(1)} %get-tuple-element.49.gy, ...), custom_call_target="tpu_custom_call" | custom-call | flops 20000000 | bytes 6000000 | tf_op jit(solution)/shard_map/own_slopes/pallas_call | solution.py:577
  25.8 0.5 %collective-permute-done.6.other_edges = f32[6,128,128]{2,1,0:T(8,128)S(1)} collective-permute-done((f32[6,128,128]{2,1,0:T(8,128)S(1)}, f32[6,128,128]{2,1,0:T(8,128)S(1)}, u32[]{:S(2)}, u32[]{:S(2)}) %collective-permute-start.6) | collective-permute-done | bytes 393248 | tf_op jit(solution)/shard_map/ppermute | solution.py:747
  26.3 0.0 collective-permute-done.5.other_gy
  26.3 0.0 collective-permute-done.4.other_in
  26.3 5.0 %gradient.1 = (f32[6,2,3,8,32,256]{5,4,3,2,1,0:T(8,128)}, f32[6,8,32,256]{3,2,1,0:T(8,128)}) custom-call(s32[1,8]{1,0:T(1,128)S(1)} %copy-done.4, f32[16,272,128]{2,1,0:T(8,128)S(1)} %get-tuple-element.46.own, f32[2,8,2,4,32,256]{5,4,3,2,1,0:T(8,128)S(1)} %get-tuple-element.47.own_xy, ...), custom_call_target="tpu_custom_call", output_to_operand_aliasing={{0}: (6, {})} | custom-call | tf_op jit(solution)/shard_map/gradient/pallas_call | solution.py:710
Async XLA Ops:
  0.6 8.4 %copy-start.3 = (f32[4,256,256]{2,1,0:T(8,128)S(1)}, f32[4,256,256]{2,1,0:T(8,128)}, u32[]{:S(2)}) copy-start(f32[4,256,256]{2,1,0:T(8,128)} %cy.5) | copy-start | bytes 3145732
  0.6 8.4 %copy-start.2 = (f32[4,256,256]{2,1,0:T(8,128)S(1)}, f32[4,256,256]{2,1,0:T(8,128)}, u32[]{:S(2)}) copy-start(f32[4,256,256]{2,1,0:T(8,128)} %cx.5) | copy-start | bytes 3145732
  0.7 8.4 %copy-start.1 = (f32[4,256,256]{2,1,0:T(8,128)S(1)}, f32[4,256,256]{2,1,0:T(8,128)}, u32[]{:S(2)}) copy-start(f32[4,256,256]{2,1,0:T(8,128)} %t.5) | copy-start | bytes 3145732
  0.7 8.3 %copy-start = (f32[4,256,256]{2,1,0:T(8,128)S(1)}, f32[4,256,256]{2,1,0:T(8,128)}, u32[]{:S(2)}) copy-start(f32[4,256,256]{2,1,0:T(8,128)} %d.5) | copy-start | bytes 3145732
  1.8 11.7 %collective-permute-start = (f32[64,256]{1,0:T(8,128)S(1)}, f32[64,256]{1,0:T(8,128)S(1)}, u32[]{:S(2)}, u32[]{:S(2)}) collective-permute-start(f32[64,256]{1,0:T(8,128)S(1)} %get-tuple-element.30), channel_id=1, source_target_pairs={{0,16},{16,32},{32,48},{48,64},{64,80},{80,96},{96,112},{112,0},{1... | collective-permute-start | bytes 196616 | tf_op jit(solution)/shard_map/ppermute | solution.py:735
  5.4 8.1 %collective-permute-start.1 = (f32[48,256]{1,0:T(8,128)S(1)}, f32[48,256]{1,0:T(8,128)S(1)}, u32[]{:S(2)}, u32[]{:S(2)}) collective-permute-start(f32[48,256]{1,0:T(8,128)S(1)} %get-tuple-element.31), channel_id=1, source_target_pairs={{0,112},{16,0},{32,16},{48,32},{64,48},{80,64},{96,80},{112,96},{1... | collective-permute-start | bytes 147464 | tf_op jit(solution)/shard_map/ppermute | solution.py:736
  14.0 8.6 %copy-start.4 = (s32[1,8]{1,0:T(1,128)S(1)}, s32[1,8]{1,0:T(1,128)}, u32[]{:S(2)}) copy-start(s32[1,8]{1,0:T(1,128)} %owner.3) | copy-start | bytes 100
  14.0 12.3 %collective-permute-start.4 = (f32[16,272,128]{2,1,0:T(8,128)S(1)}, f32[16,272,128]{2,1,0:T(8,128)S(1)}, u32[]{:S(2)}, u32[]{:S(2)}) collective-permute-start(f32[16,272,128]{2,1,0:T(8,128)S(1)} %get-tuple-element.48.s_in), channel_id=1, source_target_pairs={{0,1},{1,0},{2,3},{3,2},{4,5},{5,4},{6,7},{7,6},{8,9},{9,8},{10,11... | collective-permute-start | bytes 6684680 | tf_op jit(solution)/shard_map/ppermute | solution.py:740
  15.0 5.6 %collective-permute-start.2 = (f32[112,128]{1,0:T(8,128)S(1)}, f32[112,128]{1,0:T(8,128)S(1)}, u32[]{:S(2)}, u32[]{:S(2)}) collective-permute-start(f32[112,128]{1,0:T(8,128)S(1)} %get-tuple-element.39), channel_id=1, source_target_pairs={{0,2},{2,4},{4,6},{6,8},{8,10},{10,12},{12,14},{14,0},{1,3},{3,5},... | collective-permute-start | bytes 172040 | tf_op jit(solution)/shard_map/ppermute | solution.py:741
  15.3 5.1 %collective-permute-start.3 = (f32[88,128]{1,0:T(8,128)S(1)}, f32[88,128]{1,0:T(8,128)S(1)}, u32[]{:S(2)}, u32[]{:S(2)}) collective-permute-start(f32[88,128]{1,0:T(8,128)S(1)} %get-tuple-element.40), channel_id=1, source_target_pairs={{0,14},{2,0},{4,2},{6,4},{8,6},{10,8},{12,10},{14,12},{1,15},{3,1}... | collective-permute-start | bytes 135176 | tf_op jit(solution)/shard_map/ppermute | solution.py:742
  20.6 5.7 %collective-permute-start.5 = (f32[16,256,128]{2,1,0:T(8,128)S(1)}, f32[16,256,128]{2,1,0:T(8,128)S(1)}, u32[]{:S(2)}, u32[]{:S(2)}) collective-permute-start(f32[16,256,128]{2,1,0:T(8,128)S(1)} %get-tuple-element.49.gy), channel_id=1, source_target_pairs={{0,1},{1,0},{2,3},{3,2},{4,5},{5,4},{6,7},{7,6},{8,9},{9,8},{10,11... | collective-permute-start | bytes 6291464 | tf_op jit(solution)/shard_map/ppermute | solution.py:745
  22.4 3.8 %collective-permute-start.6 = (f32[6,128,128]{2,1,0:T(8,128)S(1)}, f32[6,128,128]{2,1,0:T(8,128)S(1)}, u32[]{:S(2)}, u32[]{:S(2)}) collective-permute-start(f32[6,128,128]{2,1,0:T(8,128)S(1)} %get-tuple-element.44.edges), channel_id=1, source_target_pairs={{0,1},{1,0},{2,3},{3,2},{4,5},{5,4},{6,7},{7,6},{8,9},{9,8},{10,11... | collective-permute-start | bytes 1179656 | tf_op jit(solution)/shard_map/ppermute | solution.py:747
